TPU v7x, 1024 devices: a whole 8x8x8 slice. The times are simulated.
1024 devices in a mesh: dp: 32 (over z, x_hi), mp: 32 (over y, x_lo, core).
Axes of the slice: x: 8 (x_hi: 4, x_lo: 2; x = x_hi * 2 + x_lo), y: 8, z: 8, core: 2. Of those that a mesh axis runs over, the one named last changes fastest.
Arguments:
- tokens: bfloat16 [8192, 3072], P('dp', 'mp'), may hold values from -6 to 6
- w_in: bfloat16 [3072, 12288], P(None, 'mp'), may hold values from -0.21875 to 0.21875
- hidden_grad: bfloat16 [8192, 12288], P('dp', 'mp'), may hold values from -6 to 6
Outputs:
- input_grad: bfloat16 [8192, 3072], P('dp', 'mp')
- weight_grad: bfloat16 [3072, 12288], P('dp', 'mp')
All inputs are finite; a program needn't handle non-finite values.
Results may differ from a plain program's by a relative error of at most 0.0049.
Values may be sent and summed in bfloat16 or wider, within the bound.
No kernel may reach another device: no remote copies, remote signals or barrier semaphores. Data moves between devices by JAX's collectives and lax.ppermute only.
A program may use at most 64 MiB of HBM per device.

v0:
```python
import jax
import jax.numpy as jnp
from jax import lax
from jax.sharding import PartitionSpec as P


def gelu_slope(pre):
    coef = 0.7978845608028654
    inner = coef * (pre + 0.044715 * pre * pre * pre)
    tval = jnp.tanh(inner)
    return 0.5 * (1.0 + tval) + 0.5 * pre * (1.0 - tval * tval) * coef * (
        1.0 + 3.0 * 0.044715 * pre * pre
    )


def local(tokens, w_in, hidden_grad):
    whole = lax.all_gather(tokens, "mp", axis=1, tiled=True)
    pre = jnp.dot(whole, w_in, preferred_element_type=jnp.float32)
    pre_grad = (hidden_grad.astype(jnp.float32) * gelu_slope(pre)).astype(jnp.bfloat16)
    input_sum = lax.psum_scatter(
        lax.dot_general(
            w_in, pre_grad, (((1,), (1,)), ((), ())), preferred_element_type=jnp.float32
        ),
        "mp",
        scatter_dimension=0,
        tiled=True,
    )
    weight_sum = lax.psum_scatter(
        lax.dot_general(
            whole, pre_grad, (((0,), (0,)), ((), ())), preferred_element_type=jnp.float32
        ),
        "dp",
        scatter_dimension=0,
        tiled=True,
    )
    input_grad = input_sum.astype(jnp.bfloat16).T
    return (input_grad, weight_sum.astype(jnp.bfloat16))


def solution(mesh):
    return jax.shard_map(
        local,
        mesh=mesh,
        in_specs=(P("dp", "mp"), P(None, "mp"), P("dp", "mp")),
        out_specs=(P("dp", "mp"), P("dp", "mp")),
        check_vma=False,
    )
```

profile of v0, /device:TPU:1, one launch (start us, length us, event | category | flops | bytes accessed | tf_op | source)
XLA Modules:
  0.0 478.1 jit_solution(1281700463585240050)
XLA Ops:
  7.2 0.0 copy-start
  7.2 0.0 all-gather.2.cloned.1.call-start
  7.2 0.7 all-gather.2.cloned.1.call-update
  7.9 0.0 copy-start.1
  7.9 0.0 reduce-scatter.7.cloned.1.call-start
  8.0 84.8 %all-gather.2.cloned.1.call-done = bf16[256,3072]{0,1:T(8,128)(2,1)} async-done(((bf16[256,96]{0,1:T(8,128)(2,1)}), bf16[256,3072]{0,1:T(8,128)(2,1)}) %all-gather.2.cloned.1.call-update) | async-done | bytes 1572880 | tf_op jit(solution)/shard_map/all_gather | solution.py:17
  92.8 0.0 copy-done
  92.8 2.4 fusion.31
  95.2 0.0 copy-done.1
  95.3 2.8 convolution_bitcast_fusion.1
  98.0 3.5 copy.9
  101.6 0.0 reduce-scatter.7.cloned.1.call-update
  101.6 0.0 reduce-scatter.9.cloned.1.call-start
  101.6 4.6 convolution_bitcast_fusion
  106.2 6.1 %copy.11 = f32[3072,384]{1,0:T(8,128)} copy(f32[3072,384]{0,1:T(8,128)} %convolution_bitcast_fusion) | data formatting | bytes 9437184
  112.3 0.0 reduce-scatter.9.cloned.1.call-update
  112.3 113.4 %reduce-scatter.7.cloned.1.call-done = f32[96,256]{1,0:T(8,128)} async-done(((f32[3072,256]{1,0:T(8,128)}), f32[96,256]{1,0:T(8,128)}) %reduce-scatter.7.cloned.1.call-update) | async-done | bytes 98320
  225.7 1.0 copy.10
  226.7 0.7 copy.7
  227.5 242.4 %reduce-scatter.9.cloned.1.call-done = f32[96,384]{1,0:T(8,128)} async-done(((f32[3072,384]{1,0:T(8,128)}), f32[96,384]{1,0:T(8,128)}) %reduce-scatter.9.cloned.1.call-update) | async-done | bytes 147472
  469.8 1.0 copy.12
  470.8 0.7 copy.8
Async XLA Ops:
  7.2 85.7 %copy-start = (bf16[3072,384]{1,0:T(8,128)(2,1)S(1)}, bf16[3072,384]{1,0:T(8,128)(2,1)}, u32[]{:S(2)}) copy-start(bf16[3072,384]{1,0:T(8,128)(2,1)} %param.4) | copy-start | bytes 7077892
  7.2 85.6 %all-gather.2.cloned.1.call-start = ((), (), s32[]{:S(2)}) async-start(), calls=%async_computation.2 | async-start | bytes 1622016 | tf_op jit(solution)/shard_map/all_gather | solution.py:17
  7.9 87.3 %copy-start.1 = (bf16[256,384]{1,0:T(8,128)(2,1)S(1)}, bf16[256,384]{1,0:T(8,128)(2,1)}, u32[]{:S(2)}) copy-start(bf16[256,384]{1,0:T(8,128)(2,1)} %param.5) | copy-start | bytes 589828
  7.9 217.8 %reduce-scatter.7.cloned.1.call-start = ((), (), s32[]{:S(2)}) async-start(), calls=%async_computation.3 | async-start | bytes 3244032
  101.6 368.2 %reduce-scatter.9.cloned.1.call-start = ((), (), s32[]{:S(2)}) async-start(), calls=%async_computation.4 | async-start | bytes 4866048
Sparse Core Ops, SparseCore 0:
  10.7 82.0 all-gather.1
  101.7 123.9 reduce-scatter.6
  232.4 237.4 reduce-scatter.8
where the time goes:
time: 482 us; the launch traced here: 478 us
  waiting for transfers between devices  441 us (91%)
  between operations  13.8 us (3%)
  local copies, waits for them, and re-layouts  13.1 us (3%)
  matrix products  9.81 us (2%)
    unnamed x5, waiting for transfers between devices  356 us
    all_gather x1, waiting for transfers between devices, local(): whole = lax.all_gather(tokens, 'mp', axis=1, tiled=True)  84.8 us
    unnamed x10, local copies, waits for them, and re-layouts  13.1 us
  transfers between devices with their start and end apart: 3, of which 3 were waited for; matrix products, arithmetic and copies ran while one was open for 3% of the time, Pallas kernels for 0%

commit v1 on v0

v1 whole, which is shorter than its diff:
```python
import jax
import jax.numpy as jnp
from jax import lax
from jax.experimental import pallas as pl
from jax.experimental.pallas import tpu as pltpu
from jax.sharding import Mesh, PartitionSpec as P

DP = ("z", "xh")
MP = ("y", "xl", "c")
F32 = jnp.float32
BF16 = jnp.bfloat16
VMEM = pl.BlockSpec(memory_space=pltpu.VMEM)
SMEM = pl.BlockSpec(memory_space=pltpu.SMEM)


def gelu_slope(pre):
    coef = 0.7978845608028654
    inner = coef * (pre + 0.044715 * pre * pre * pre)
    tval = jnp.tanh(inner)
    return 0.5 * (1.0 + tval) + 0.5 * pre * (1.0 - tval * tval) * coef * (
        1.0 + 3.0 * 0.044715 * pre * pre
    )


def hidden_kernel(core_ref, own_ref, other_ref, w_ref, g_ref, wpart_ref, pg_ref, whole):
    core = core_ref[0]
    feats = own_ref.shape[1]
    for i in range(own_ref.shape[0]):
        for ref, c in ((own_ref, core), (other_ref, 1 - core)):
            start = pl.multiple_of((2 * i + c) * feats, feats)
            whole[pl.ds(start, feats), :] = ref[i]
    pre = lax.dot_general(
        whole[...], w_ref[...], (((0,), (0,)), ((), ())), preferred_element_type=F32
    )
    pg = (g_ref[...].astype(F32) * gelu_slope(pre)).astype(BF16)
    pg_ref[...] = pg
    step = 256
    for i in range(whole.shape[0] // step):
        rows = pl.ds(i * step, step)
        wpart_ref[rows, :] = jnp.dot(
            whole[rows, :], pg, preferred_element_type=F32
        ).astype(BF16)


def input_kernel(core_ref, w_ref, pg_ref, keep_ref, send_ref):
    core = core_ref[0]
    pg = pg_ref[...]
    feats = keep_ref.shape[1]
    for i in range(keep_ref.shape[0]):
        for ref, c in ((send_ref, 1 - core), (keep_ref, core)):
            start = pl.multiple_of((2 * i + c) * feats, feats)
            ref[i] = lax.dot_general(
                w_ref[pl.ds(start, feats), :],
                pg,
                (((1,), (1,)), ((), ())),
                preferred_element_type=F32,
            ).astype(ref.dtype)


def local(tokens, w_in, hidden_grad):
    rows, feats = tokens.shape
    d, hidden = w_in.shape
    core = jnp.full((1,), lax.axis_index("c"), jnp.int32)
    swap = [(0, 1), (1, 0)]
    pair = lax.all_gather(tokens.T, "xl", axis=0)
    own = lax.all_gather(pair, "y", axis=0).reshape(16, feats, rows)
    other = lax.ppermute(own, "c", swap)
    wpart, pre_grad = pl.pallas_call(
        hidden_kernel,
        out_shape=(
            jax.ShapeDtypeStruct((d, hidden), BF16),
            jax.ShapeDtypeStruct((rows, hidden), BF16),
        ),
        in_specs=[SMEM, VMEM, VMEM, VMEM, VMEM],
        out_specs=(VMEM, VMEM),
        scratch_shapes=[pltpu.VMEM((d, rows), BF16)],
        compiler_params=pltpu.CompilerParams(vmem_limit_bytes=40 << 20),
        cost_estimate=pl.CostEstimate(
            flops=4 * d * rows * hidden, bytes_accessed=8 << 20, transcendentals=rows * hidden
        ),
    )(core, own, other, w_in, hidden_grad)
    pieces = lax.all_to_all(wpart.reshape(32, feats, hidden), DP, 0, 0, tiled=True)
    keep, send = pl.pallas_call(
        input_kernel,
        out_shape=(
            jax.ShapeDtypeStruct((16, feats, rows), F32),
            jax.ShapeDtypeStruct((16, feats, rows), BF16),
        ),
        in_specs=[SMEM, VMEM, VMEM],
        out_specs=(VMEM, VMEM),
        compiler_params=pltpu.CompilerParams(vmem_limit_bytes=40 << 20),
        cost_estimate=pl.CostEstimate(
            flops=2 * d * rows * hidden, bytes_accessed=5 << 20, transcendentals=0
        ),
    )(core, w_in, pre_grad)
    arrived = lax.ppermute(send, "c", swap)
    both = (keep + arrived.astype(F32)).reshape(16 * feats, rows)
    input_sum = lax.psum_scatter(both, ("y", "xl"), scatter_dimension=0, tiled=True)
    weight_sum = jnp.sum(pieces.astype(F32), axis=0)
    return (input_sum.astype(BF16).T, weight_sum.astype(BF16))


def solution(mesh):
    split = Mesh(mesh.devices.reshape(8, 4, 8, 2, 2), DP + MP)
    return jax.shard_map(
        local,
        mesh=split,
        in_specs=(P(DP, MP), P(None, MP), P(DP, MP)),
        out_specs=(P(DP, MP), P(DP, MP)),
        check_vma=False,
    )
```

time: 482 us -> 190 us (0.39)
  the two profiles are of different devices: /device:TPU:1 before, /device:TPU:50 now
where the time goes in v1:
time: 190 us; the launch traced here: 189 us
  waiting for transfers between devices  104 us (55%)
  blocking collectives  36.8 us (19%)
  starting transfers between devices  20.2 us (11%)
  between operations  14.1 us (7%)
  other arithmetic  5.54 us (3%)
  Pallas kernels  4.38 us (2%)
  local copies, waits for them, and re-layouts  3.99 us (2%)
    reduce_scatter x1, waiting for transfers between devices, local(): lax.psum_scatter(both, ('y', 'xl'), scatter_dimension=0, tiled=True)  99.6 us
    all_gather x1, blocking collectives, local(): own = lax.all_gather(pair, 'y', axis=0).reshape(16, feats, rows)  31.8 us
    all_to_all x1, starting transfers between devices, local(): lax.all_to_all(wpart.reshape(32, feats, hidden), DP, 0, 0, tiled=True)  16.3 us
    all_gather x1, blocking collectives, local(): pair = lax.all_gather(tokens.T, 'xl', axis=0)  4.98 us
    unnamed x8, local copies, waits for them, and re-layouts  3.99 us
  transfers between devices with their start and end apart: 4, of which 3 were waited for; matrix products, arithmetic and copies ran while one was open for 2% of the time, Pallas kernels for 1%

profile of v1, /device:TPU:50, one launch (start us, length us, event | category | flops | bytes accessed | tf_op | source)
XLA Modules:
  0.0 189.1 jit_solution(14540863862335640256)
XLA Ops:
  7.2 5.0 %all-gather = bf16[192,256]{1,0:T(8,128)(2,1)S(1)} all-gather(bf16[96,256]{1,0:T(8,128)(2,1)} %bitcast.10), channel_id=2, replica_groups=mesh['z'=8,'xh'=4,'y'=8,'xl'=2,'c'=2] {'xl'}, dimensions={0}, use_global_device_ids=true | all-gather | bytes 147456 | tf_op jit(solution)/shard_map/all_gather | solution.py:65
  12.1 31.8 %all-gather.1.own_ref = bf16[16,96,256]{2,1,0:T(8,128)(2,1)S(1)} all-gather(bf16[2,96,256]{2,1,0:T(8,128)(2,1)S(1)} %bitcast.9), channel_id=3, replica_groups=mesh['z'=8,'xh'=4,'y'=8,'xl'=2,'c'=2] {'y'}, dimensions={0}, use_global_device_ids=true | all-gather | bytes 884736 | tf_op jit(solution)/shard_map/all_gather | solution.py:66
  44.0 1.9 %collective-permute-start = (bf16[16,96,256]{2,1,0:T(8,128)(2,1)S(1)}, bf16[16,96,256]{2,1,0:T(8,128)(2,1)S(1)}, u32[]{:S(2)}, u32[]{:S(2)}) collective-permute-start(bf16[16,96,256]{2,1,0:T(8,128)(2,1)S(1)} %all-gather.1.own_ref), channel_id=1, source_target_pairs={{0,1},{1,0},{2,3},{3,2},{4,5},{5,4},{6,7},{7,6},{8,9},{9,8},{10,11... | collective-permute-start | bytes 2359304 | tf_op jit(solution)/shard_map/ppermute | solution.py:67
  45.9 2.2 %collective-permute-done.other_ref = bf16[16,96,256]{2,1,0:T(8,128)(2,1)S(1)} collective-permute-done((bf16[16,96,256]{2,1,0:T(8,128)(2,1)S(1)}, bf16[16,96,256]{2,1,0:T(8,128)(2,1)S(1)}, u32[]{:S(2)}, u32[]{:S(2)}) %collective-permute-start) | collective-permute-done | bytes 786464 | tf_op jit(solution)/shard_map/ppermute | solution.py:67
  48.2 0.0 copy-start
  48.2 1.7 copy-done
  49.8 0.0 copy-start.3
  49.8 0.9 copy-done.3
  50.8 2.3 %shard_map.50 = (bf16[3072,384]{1,0:T(8,128)(2,1)S(1)}, bf16[256,384]{1,0:T(8,128)(2,1)S(1)}) custom-call(s32[1]{0:T(128)} %bitcast.core_ref, bf16[16,96,256]{2,1,0:T(8,128)(2,1)S(1)} %all-gather.1.own_ref, bf16[16,96,256]{2,1,0:T(8,128)(2,1)S(1)} %collective-permute-done.other_ref, bf16[3072,384]{1,0:T(8,128)(2,1)S(1)} %copy-done, ...), custom_call_target="tpu_custom_call" | custom-call | flops 1207959552 | bytes 8388608 | tf_op jit(solution)/shard_map/pallas_call | solution.py:68
  53.1 0.0 copy-start.2
  53.1 1.4 copy-done.2
  54.5 0.0 copy-start.1
  54.5 16.3 %all-to-all-start = ((bf16[32,96,384]{2,1,0:T(8,128)(2,1)}), bf16[32,96,384]{2,1,0:T(8,128)(2,1)}, u32[]{:S(2)}, u32[]{:S(2)}) async-start(bf16[32,96,384]{2,1,0:T(8,128)(2,1)} %bitcast.7), calls=%async_computation.1 | async-start | bytes 4718592 | tf_op jit(solution)/shard_map/all_to_all | solution.py:82
  70.8 0.0 reduce-scatter.2.cloned.1.call-start
  70.8 0.0 copy-done.1
  70.8 2.1 %shard_map.51 = (f32[16,96,256]{2,1,0:T(8,128)S(1)}, bf16[16,96,256]{2,1,0:T(8,128)(2,1)S(1)}) custom-call(s32[1]{0:T(128)} %bitcast.core_ref, bf16[3072,384]{1,0:T(8,128)(2,1)S(1)} %copy-done.1, bf16[256,384]{1,0:T(8,128)(2,1)S(1)} %get-tuple-element.6.pg_ref), custom_call_target="tpu_custom_call" | custom-call | flops 603979776 | bytes 5242880 | tf_op jit(solution)/shard_map/pallas_call | solution.py:83
  72.9 1.9 %collective-permute-start.1 = (bf16[16,96,256]{2,1,0:T(8,128)(2,1)S(1)}, bf16[16,96,256]{2,1,0:T(8,128)(2,1)S(1)}, u32[]{:S(2)}, u32[]{:S(2)}) collective-permute-start(bf16[16,96,256]{2,1,0:T(8,128)(2,1)S(1)} %get-tuple-element.8), channel_id=1, source_target_pairs={{0,1},{1,0},{2,3},{3,2},{4,5},{5,4},{6,7},{7,6},{8,9},{9,8},{10,11... | collective-permute-start | bytes 2359304 | tf_op jit(solution)/shard_map/ppermute | solution.py:96
  74.8 2.3 %collective-permute-done.1 = bf16[16,96,256]{2,1,0:T(8,128)(2,1)S(1)} collective-permute-done((bf16[16,96,256]{2,1,0:T(8,128)(2,1)S(1)}, bf16[16,96,256]{2,1,0:T(8,128)(2,1)S(1)}, u32[]{:S(2)}, u32[]{:S(2)}) %collective-permute-start.1) | collective-permute-done | bytes 786464 | tf_op jit(solution)/shard_map/ppermute | solution.py:96
  77.1 1.4 convert_add_fusion
  78.5 0.0 reduce-scatter.2.cloned.1.call-update
  78.5 99.6 %reduce-scatter.2.cloned.1.call-done = f32[96,256]{1,0:T(8,128)} async-done(((f32[1536,256]{1,0:T(8,128)}), f32[96,256]{1,0:T(8,128)}) %reduce-scatter.2.cloned.1.call-update) | async-done | bytes 98320 | tf_op jit(solution)/shard_map/reduce_scatter | solution.py:98
  178.1 1.5 convert_bitcast_fusion
  179.6 0.0 all-to-all-done
  179.6 2.6 %reduce_sum.12 = bf16[96,384]{1,0:T(8,128)(2,1)} reduce(bf16[32,96,384]{2,1,0:T(8,128)(2,1)} %all-to-all-done, bf16[]{:T(256)} %constant.6.clone.1), dimensions={0}, to_apply=%region_1.0 | reduce | flops 1142784 | bytes 2433026 | tf_op jit(solution)/shard_map/reduce_sum | solution.py:99
Async XLA Ops:
  44.0 4.2 %collective-permute-start = (bf16[16,96,256]{2,1,0:T(8,128)(2,1)S(1)}, bf16[16,96,256]{2,1,0:T(8,128)(2,1)S(1)}, u32[]{:S(2)}, u32[]{:S(2)}) collective-permute-start(bf16[16,96,256]{2,1,0:T(8,128)(2,1)S(1)} %all-gather.1.own_ref), channel_id=1, source_target_pairs={{0,1},{1,0},{2,3},{3,2},{4,5},{5,4},{6,7},{7,6},{8,9},{9,8},{10,11... | collective-permute-start | bytes 2359304 | tf_op jit(solution)/shard_map/ppermute | solution.py:67
  48.2 1.7 copy-start
  49.8 0.9 copy-start.3
  53.1 1.4 copy-start.2
  54.5 16.4 %copy-start.1 = (bf16[3072,384]{1,0:T(8,128)(2,1)S(1)}, bf16[3072,384]{1,0:T(8,128)(2,1)}, u32[]{:S(2)}) copy-start(bf16[3072,384]{1,0:T(8,128)(2,1)} %w_ref.3) | copy-start | bytes 7077892
  54.5 125.2 %all-to-all-start = ((bf16[32,96,384]{2,1,0:T(8,128)(2,1)}), bf16[32,96,384]{2,1,0:T(8,128)(2,1)}, u32[]{:S(2)}, u32[]{:S(2)}) async-start(bf16[32,96,384]{2,1,0:T(8,128)(2,1)} %bitcast.7), calls=%async_computation.1 | async-start | bytes 4718592 | tf_op jit(solution)/shard_map/all_to_all | solution.py:82
  70.8 107.3 %reduce-scatter.2.cloned.1.call-start = ((), (), s32[]{:S(2)}) async-start(), calls=%async_computation.2 | async-start | bytes 1671168 | tf_op jit(solution)/shard_map/reduce_scatter | solution.py:98
  72.9 4.2 %collective-permute-start.1 = (bf16[16,96,256]{2,1,0:T(8,128)(2,1)S(1)}, bf16[16,96,256]{2,1,0:T(8,128)(2,1)S(1)}, u32[]{:S(2)}, u32[]{:S(2)}) collective-permute-start(bf16[16,96,256]{2,1,0:T(8,128)(2,1)S(1)} %get-tuple-element.8), channel_id=1, source_target_pairs={{0,1},{1,0},{2,3},{3,2},{4,5},{5,4},{6,7},{7,6},{8,9},{9,8},{10,11... | collective-permute-start | bytes 2359304 | tf_op jit(solution)/shard_map/ppermute | solution.py:96
Sparse Core Ops, SparseCore 0:
  78.6 99.4 reduce-scatter.1

commit v2 on v0

v2 whole, which is shorter than its diff:
```python
import jax
import jax.numpy as jnp
from jax import lax
from jax.experimental import pallas as pl
from jax.experimental.pallas import tpu as pltpu
from jax.sharding import Mesh, PartitionSpec as P

DP = ("z", "xh")
MP = ("y", "xl", "c")
F32 = jnp.float32
BF16 = jnp.bfloat16
VMEM = pl.BlockSpec(memory_space=pltpu.VMEM)
SMEM = pl.BlockSpec(memory_space=pltpu.SMEM)
PAIR = [(0, 1), (1, 0)]


def gelu_slope(pre):
    coef = 0.7978845608028654
    inner = coef * (pre + 0.044715 * pre * pre * pre)
    tval = jnp.tanh(inner)
    return 0.5 * (1.0 + tval) + 0.5 * pre * (1.0 - tval * tval) * coef * (
        1.0 + 3.0 * 0.044715 * pre * pre
    )


def hidden_kernel(at_ref, own_ref, mine_ref, other_ref, w_ref, g_ref, wpart_ref, pg_ref, whole):
    xl, core = at_ref[1], at_ref[2]
    feats = own_ref.shape[2]

    def put(y, x, c, block):
        start = pl.multiple_of((4 * y + 2 * x + c) * feats, feats)
        whole[pl.ds(start, feats), :] = block

    for y in range(own_ref.shape[0]):
        put(y, xl, 0, own_ref[y, 0])
        put(y, xl, 1, own_ref[y, 1])
        put(y, 1 - xl, core, mine_ref[y])
        put(y, 1 - xl, 1 - core, other_ref[y])
    pre = lax.dot_general(
        whole[...], w_ref[...], (((0,), (0,)), ((), ())), preferred_element_type=F32
    )
    pg = (g_ref[...].astype(F32) * gelu_slope(pre)).astype(BF16)
    pg_ref[...] = pg
    step = whole.shape[0] // 12
    for i in range(12):
        rows = pl.ds(i * step, step)
        wpart_ref[rows, :] = jnp.dot(
            whole[rows, :], pg, preferred_element_type=F32
        ).astype(BF16)


def input_kernel(at_ref, w_ref, pg_ref, keep_ref, send_ref):
    y_own, xl, core = at_ref[0], at_ref[1], at_ref[2]
    pg = pg_ref[...]
    feats = keep_ref.shape[1]
    blocks = keep_ref.shape[0]
    ny = blocks // 2
    bits = ny.bit_length() - 1
    for ref, c in ((send_ref, 1 - core), (keep_ref, core)):
        for i in range(blocks):
            x = xl if i < ny else 1 - xl
            r = sum(((i % ny) >> (bits - 1 - k) & 1) << k for k in range(bits))
            start = (4 * lax.bitwise_xor(y_own, jnp.int32(r)) + 2 * x + c) * feats
            ref[i] = lax.dot_general(
                w_ref[pl.ds(pl.multiple_of(start, feats), feats), :],
                pg,
                (((1,), (1,)), ((), ())),
                preferred_element_type=F32,
            ).astype(ref.dtype)


def make_local(nz, nx, ny):
    def local(tokens, w_in, hidden_grad):
        rows, feats = tokens.shape
        d, hidden = w_in.shape
        core = lax.axis_index("c")
        at = jnp.stack([lax.axis_index("y"), lax.axis_index("xl"), core]).astype(jnp.int32)
        own = lax.all_gather(tokens.T, ("y", "c"), axis=0).reshape(ny, 2, feats, rows)
        mine = lax.ppermute(lax.dynamic_index_in_dim(own, core, 1, False), "xl", PAIR)
        other = lax.ppermute(mine, "c", PAIR)
        wpart, pre_grad = pl.pallas_call(
            hidden_kernel,
            out_shape=(
                jax.ShapeDtypeStruct((d, hidden), BF16),
                jax.ShapeDtypeStruct((rows, hidden), BF16),
            ),
            in_specs=[SMEM, VMEM, VMEM, VMEM, VMEM, VMEM],
            out_specs=(VMEM, VMEM),
            scratch_shapes=[pltpu.VMEM((d, rows), BF16)],
            compiler_params=pltpu.CompilerParams(vmem_limit_bytes=16 << 20),
            cost_estimate=pl.CostEstimate(
                flops=4 * d * rows * hidden,
                bytes_accessed=8 << 20,
                transcendentals=rows * hidden,
            ),
        )(at, own, mine, other, w_in, hidden_grad)
        pieces = lax.all_to_all(
            wpart.reshape(nz * nx, d // (nz * nx), hidden), DP, 0, 0, tiled=True
        )
        keep, send = pl.pallas_call(
            input_kernel,
            out_shape=(
                jax.ShapeDtypeStruct((2 * ny, feats, rows), F32),
                jax.ShapeDtypeStruct((2 * ny, feats, rows), BF16),
            ),
            in_specs=[SMEM, VMEM, VMEM],
            out_specs=(VMEM, VMEM),
            compiler_params=pltpu.CompilerParams(vmem_limit_bytes=12 << 20),
            cost_estimate=pl.CostEstimate(
                flops=2 * d * rows * hidden, bytes_accessed=5 << 20, transcendentals=0
            ),
        )(at, w_in, pre_grad)
        total = keep + lax.ppermute(send, "c", PAIR).astype(F32)
        steps = [("xl", PAIR)]
        bit = 1
        while bit < ny:
            steps.append(("y", [(i, i ^ bit) for i in range(ny)]))
            bit *= 2
        for axis, pairs in steps:
            half = total.shape[0] // 2
            arrived = lax.ppermute(total[half:].astype(BF16), axis, pairs)
            total = total[:half] + arrived.astype(F32)
        weight_sum = jnp.sum(pieces.astype(F32), axis=0)
        return (total[0].astype(BF16).T, weight_sum.astype(BF16))

    return local


def solution(mesh, sizes=(8, 4, 8)):
    split = Mesh(mesh.devices.reshape(*sizes, 2, 2), DP + MP)
    return jax.shard_map(
        make_local(*sizes),
        mesh=split,
        in_specs=(P(DP, MP), P(None, MP), P(DP, MP)),
        out_specs=(P(DP, MP), P(DP, MP)),
        check_vma=False,
    )
```

time: 482 us -> 160 us (0.33)
  the two profiles are of different devices: /device:TPU:1 before, /device:TPU:514 now
where the time goes in v2:
time: 160 us
  waiting for transfers between devices  91.7 us (57%)
  starting transfers between devices  33.8 us (21%)
  blocking collectives  20.9 us (13%)
  Pallas kernels  5.45 us (3%)
  other arithmetic  3.68 us (2%)
  local copies, waits for them, and re-layouts  3.18 us (2%)
    ppermute x4, waiting for transfers between devices, local(): arrived = lax.ppermute(total[half:].astype(BF16), axis, pairs)  77 us
    all_gather x1, blocking collectives, local(): lax.all_gather(tokens.T, ('y', 'c'), axis=0).reshape(ny, 2, feats, rows)  20.9 us
    all_to_all x1, starting transfers between devices, local(): lax.all_to_all(wpart.reshape(nz * nx, d // (nz * nx), hidden), DP, 0, 0,...  14.3 us
    ppermute x4, starting transfers between devices, local(): arrived = lax.ppermute(total[half:].astype(BF16), axis, pairs)  13.2 us
    ppermute x1, waiting for transfers between devices, local(): lax.ppermute(lax.dynamic_index_in_dim(own, core, 1, False), 'xl', PAIR)  10.8 us
  transfers between devices with their start and end apart: 8, of which 7 were waited for; matrix products, arithmetic and copies ran while one was open for 1% of the time, Pallas kernels for 2%

profile of v2, /device:TPU:514, one launch (start us, length us, event | category | flops | bytes accessed | tf_op | source)
XLA Modules:
  0.0 159.5 jit_solution(10680671309742479909)
XLA Ops:
  0.6 20.9 %all-gather = bf16[1536,256]{1,0:T(8,128)(2,1)S(1)} all-gather(bf16[96,256]{1,0:T(8,128)(2,1)} %bitcast.15), channel_id=2, replica_groups=mesh['z'=8,'xh'=4,'y'=8,'xl'=2,'c'=2] {'y','c'}, dimensions={0}, use_global_device_ids=true | all-gather | bytes 835584 | tf_op jit(solution)/shard_map/all_gather | solution.py:78
  21.6 2.4 %collective-permute-start = (bf16[8,96,256]{2,1,0:T(8,128)(2,1)S(1)}, bf16[8,96,256]{2,1,0:T(8,128)(2,1)S(1)}, u32[]{:S(2)}, u32[]{:S(2)}) collective-permute-start(bf16[8,96,256]{2,1,0:T(8,128)(2,1)S(1)} %dynamic-slice_bitcast_fusion), channel_id=1, source_target_pairs={{0,2},{2,0},{1,3},{3,1},{4,6},{6,4},{5,7},{7,5},{8,10},{10,8},{9,1... | collective-permute-start | bytes 1179656 | tf_op jit(solution)/shard_map/ppermute | solution.py:79
  24.0 10.8 %collective-permute-done.mine_ref = bf16[8,96,256]{2,1,0:T(8,128)(2,1)S(1)} collective-permute-done((bf16[8,96,256]{2,1,0:T(8,128)(2,1)S(1)}, bf16[8,96,256]{2,1,0:T(8,128)(2,1)S(1)}, u32[]{:S(2)}, u32[]{:S(2)}) %collective-permute-start) | collective-permute-done | bytes 393248 | tf_op jit(solution)/shard_map/ppermute | solution.py:79
  34.9 1.9 %collective-permute-start.1 = (bf16[8,96,256]{2,1,0:T(8,128)(2,1)S(1)}, bf16[8,96,256]{2,1,0:T(8,128)(2,1)S(1)}, u32[]{:S(2)}, u32[]{:S(2)}) collective-permute-start(bf16[8,96,256]{2,1,0:T(8,128)(2,1)S(1)} %collective-permute-done.mine_ref), channel_id=1, source_target_pairs={{0,1},{1,0},{2,3},{3,2},{4,5},{5,4},{6,7},{7,6},{8,9},{9,8},{10,11... | collective-permute-start | bytes 1179656 | tf_op jit(solution)/shard_map/ppermute | solution.py:80
  36.9 1.6 %collective-permute-done.1.other_ref = bf16[8,96,256]{2,1,0:T(8,128)(2,1)S(1)} collective-permute-done((bf16[8,96,256]{2,1,0:T(8,128)(2,1)S(1)}, bf16[8,96,256]{2,1,0:T(8,128)(2,1)S(1)}, u32[]{:S(2)}, u32[]{:S(2)}) %collective-permute-start.1) | collective-permute-done | bytes 393248 | tf_op jit(solution)/shard_map/ppermute | solution.py:80
  38.5 1.7 %copy-done = bf16[3072,384]{1,0:T(8,128)(2,1)S(1)} copy-done((bf16[3072,384]{1,0:T(8,128)(2,1)S(1)}, bf16[3072,384]{1,0:T(8,128)(2,1)}, u32[]{:S(2)}) %copy-start) | copy-done | bytes 2359320
  40.1 2.8 %shard_map.50 = (bf16[3072,384]{1,0:T(8,128)(2,1)S(1)}, bf16[256,384]{1,0:T(8,128)(2,1)S(1)}) custom-call(s32[3]{0:T(128)S(1)} %pad_add_fusion.at_ref, bf16[8,2,96,256]{3,2,1,0:T(8,128)(2,1)S(1)} %bitcast.14, bf16[8,96,256]{2,1,0:T(8,128)(2,1)S(1)} %collective-permute-done.mine_ref, bf16[8,96,256]{2,1,0:T(8,128)(2,1)S(1)} %collective-permute-done.1.other_ref, ...), custom_call_target="tpu_custom_call" | custom-call | flops 1207959552 | bytes 8388608 | tf_op jit(solution)/shard_map/pallas_call | solution.py:81
  43.0 1.4 copy-done.2
  44.4 14.3 %all-to-all-start = ((bf16[32,96,384]{2,1,0:T(8,128)(2,1)}), bf16[32,96,384]{2,1,0:T(8,128)(2,1)}, u32[]{:S(2)}, u32[]{:S(2)}) async-start(bf16[32,96,384]{2,1,0:T(8,128)(2,1)} %bitcast.12), calls=%async_computation | async-start | bytes 4718592 | tf_op jit(solution)/shard_map/all_to_all | solution.py:97
  58.7 2.6 %shard_map.51 = (f32[16,96,256]{2,1,0:T(8,128)S(1)}, bf16[16,96,256]{2,1,0:T(8,128)(2,1)S(1)}) custom-call(s32[3]{0:T(128)S(1)} %pad_add_fusion.at_ref, bf16[3072,384]{1,0:T(8,128)(2,1)S(1)} %copy-done.1, bf16[256,384]{1,0:T(8,128)(2,1)S(1)} %get-tuple-element.6.pg_ref), custom_call_target="tpu_custom_call" | custom-call | flops 603979776 | bytes 5242880 | tf_op jit(solution)/shard_map/pallas_call | solution.py:100
  61.3 1.9 %collective-permute-start.2 = (bf16[16,96,256]{2,1,0:T(8,128)(2,1)S(1)}, bf16[16,96,256]{2,1,0:T(8,128)(2,1)S(1)}, u32[]{:S(2)}, u32[]{:S(2)}) collective-permute-start(bf16[16,96,256]{2,1,0:T(8,128)(2,1)S(1)} %get-tuple-element.8), channel_id=1, source_target_pairs={{0,1},{1,0},{2,3},{3,2},{4,5},{5,4},{6,7},{7,6},{8,9},{9,8},{10,11... | collective-permute-start | bytes 2359304 | tf_op jit(solution)/shard_map/ppermute | solution.py:113
  63.3 2.3 %collective-permute-done.2 = bf16[16,96,256]{2,1,0:T(8,128)(2,1)S(1)} collective-permute-done((bf16[16,96,256]{2,1,0:T(8,128)(2,1)S(1)}, bf16[16,96,256]{2,1,0:T(8,128)(2,1)S(1)}, u32[]{:S(2)}, u32[]{:S(2)}) %collective-permute-start.2) | collective-permute-done | bytes 786464 | tf_op jit(solution)/shard_map/ppermute | solution.py:113
  65.5 0.2 convert_add_fusion
  65.7 3.3 %collective-permute-start.3 = (bf16[8,96,256]{2,1,0:T(8,128)(2,1)S(1)}, bf16[8,96,256]{2,1,0:T(8,128)(2,1)S(1)}, u32[]{:S(2)}, u32[]{:S(2)}) collective-permute-start(bf16[8,96,256]{2,1,0:T(8,128)(2,1)S(1)} %slice.56), channel_id=1, source_target_pairs={{0,2},{2,0},{1,3},{3,1},{4,6},{6,4},{5,7},{7,5},{8,10},{10,8},{9,1... | collective-permute-start | bytes 1179656 | tf_op jit(solution)/shard_map/ppermute | solution.py:121
  69.1 60.6 %collective-permute-done.3 = bf16[8,96,256]{2,1,0:T(8,128)(2,1)S(1)} collective-permute-done((bf16[8,96,256]{2,1,0:T(8,128)(2,1)S(1)}, bf16[8,96,256]{2,1,0:T(8,128)(2,1)S(1)}, u32[]{:S(2)}, u32[]{:S(2)}) %collective-permute-start.3) | collective-permute-done | bytes 393248 | tf_op jit(solution)/shard_map/ppermute | solution.py:121
  129.7 0.1 slice_add_fusion
  129.8 2.1 %collective-permute-start.4 = (bf16[4,96,256]{2,1,0:T(8,128)(2,1)S(1)}, bf16[4,96,256]{2,1,0:T(8,128)(2,1)S(1)}, u32[]{:S(2)}, u32[]{:S(2)}) collective-permute-start(bf16[4,96,256]{2,1,0:T(8,128)(2,1)S(1)} %slice.57), channel_id=1, source_target_pairs={{0,4},{4,0},{8,12},{12,8},{16,20},{20,16},{24,28},{28,24},{1,5},{5... | collective-permute-start | bytes 589832 | tf_op jit(solution)/shard_map/ppermute | solution.py:121
  132.0 5.6 %collective-permute-done.4 = bf16[4,96,256]{2,1,0:T(8,128)(2,1)S(1)} collective-permute-done((bf16[4,96,256]{2,1,0:T(8,128)(2,1)S(1)}, bf16[4,96,256]{2,1,0:T(8,128)(2,1)S(1)}, u32[]{:S(2)}, u32[]{:S(2)}) %collective-permute-start.4) | collective-permute-done | bytes 196640 | tf_op jit(solution)/shard_map/ppermute | solution.py:121
  137.6 2.6 %collective-permute-start.5 = (bf16[2,96,256]{2,1,0:T(8,128)(2,1)S(1)}, bf16[2,96,256]{2,1,0:T(8,128)(2,1)S(1)}, u32[]{:S(2)}, u32[]{:S(2)}) collective-permute-start(bf16[2,96,256]{2,1,0:T(8,128)(2,1)S(1)} %slice.58), channel_id=1, source_target_pairs={{0,8},{4,12},{8,0},{12,4},{16,24},{20,28},{24,16},{28,20},{1,9},{5... | collective-permute-start | bytes 294920 | tf_op jit(solution)/shard_map/ppermute | solution.py:121
  140.2 5.6 %collective-permute-done.5 = bf16[2,96,256]{2,1,0:T(8,128)(2,1)S(1)} collective-permute-done((bf16[2,96,256]{2,1,0:T(8,128)(2,1)S(1)}, bf16[2,96,256]{2,1,0:T(8,128)(2,1)S(1)}, u32[]{:S(2)}, u32[]{:S(2)}) %collective-permute-start.5) | collective-permute-done | bytes 98336 | tf_op jit(solution)/shard_map/ppermute | solution.py:121
  145.9 5.2 %collective-permute-start.6 = (bf16[1,96,256]{2,1,0:T(8,128)(2,1)S(1)}, bf16[1,96,256]{2,1,0:T(8,128)(2,1)S(1)}, u32[]{:S(2)}, u32[]{:S(2)}) collective-permute-start(bf16[1,96,256]{2,1,0:T(8,128)(2,1)S(1)} %slice.59), channel_id=1, source_target_pairs={{0,16},{4,20},{8,24},{12,28},{16,0},{20,4},{24,8},{28,12},{1,17},{... | collective-permute-start | bytes 147464 | tf_op jit(solution)/shard_map/ppermute | solution.py:121
  151.1 5.2 %collective-permute-done.6 = bf16[1,96,256]{2,1,0:T(8,128)(2,1)S(1)} collective-permute-done((bf16[1,96,256]{2,1,0:T(8,128)(2,1)S(1)}, bf16[1,96,256]{2,1,0:T(8,128)(2,1)S(1)}, u32[]{:S(2)}, u32[]{:S(2)}) %collective-permute-start.6) | collective-permute-done | bytes 49184 | tf_op jit(solution)/shard_map/ppermute | solution.py:121
  156.2 0.6 fusion.1
  156.9 2.6 %reduce_sum.12 = bf16[96,384]{1,0:T(8,128)(2,1)} reduce(bf16[32,96,384]{2,1,0:T(8,128)(2,1)} %all-to-all-done, bf16[]{:T(256)} %constant.20.clone.1), dimensions={0}, to_apply=%region_0.1 | reduce | flops 1142784 | bytes 2433026 | tf_op jit(solution)/shard_map/reduce_sum | solution.py:123
  (15 shorter events, 0.3 us)
Async XLA Ops:
  0.6 37.8 %copy-start.3 = (bf16[256,384]{1,0:T(8,128)(2,1)S(1)}, bf16[256,384]{1,0:T(8,128)(2,1)}, u32[]{:S(2)}) copy-start(bf16[256,384]{1,0:T(8,128)(2,1)} %g_ref.1) | copy-start | bytes 589828
  21.6 13.3 %collective-permute-start = (bf16[8,96,256]{2,1,0:T(8,128)(2,1)S(1)}, bf16[8,96,256]{2,1,0:T(8,128)(2,1)S(1)}, u32[]{:S(2)}, u32[]{:S(2)}) collective-permute-start(bf16[8,96,256]{2,1,0:T(8,128)(2,1)S(1)} %dynamic-slice_bitcast_fusion), channel_id=1, source_target_pairs={{0,2},{2,0},{1,3},{3,1},{4,6},{6,4},{5,7},{7,5},{8,10},{10,8},{9,1... | collective-permute-start | bytes 1179656 | tf_op jit(solution)/shard_map/ppermute | solution.py:79
  34.9 3.6 %collective-permute-start.1 = (bf16[8,96,256]{2,1,0:T(8,128)(2,1)S(1)}, bf16[8,96,256]{2,1,0:T(8,128)(2,1)S(1)}, u32[]{:S(2)}, u32[]{:S(2)}) collective-permute-start(bf16[8,96,256]{2,1,0:T(8,128)(2,1)S(1)} %collective-permute-done.mine_ref), channel_id=1, source_target_pairs={{0,1},{1,0},{2,3},{3,2},{4,5},{5,4},{6,7},{7,6},{8,9},{9,8},{10,11... | collective-permute-start | bytes 1179656 | tf_op jit(solution)/shard_map/ppermute | solution.py:80
  38.5 1.7 %copy-start = (bf16[3072,384]{1,0:T(8,128)(2,1)S(1)}, bf16[3072,384]{1,0:T(8,128)(2,1)}, u32[]{:S(2)}) copy-start(bf16[3072,384]{1,0:T(8,128)(2,1)} %w_ref.3) | copy-start | bytes 7077892
  43.0 1.4 copy-start.2
  44.4 14.3 %copy-start.1 = (bf16[3072,384]{1,0:T(8,128)(2,1)S(1)}, bf16[3072,384]{1,0:T(8,128)(2,1)}, u32[]{:S(2)}) copy-start(bf16[3072,384]{1,0:T(8,128)(2,1)} %w_ref.3) | copy-start | bytes 7077892
  44.4 112.5 %all-to-all-start = ((bf16[32,96,384]{2,1,0:T(8,128)(2,1)}), bf16[32,96,384]{2,1,0:T(8,128)(2,1)}, u32[]{:S(2)}, u32[]{:S(2)}) async-start(bf16[32,96,384]{2,1,0:T(8,128)(2,1)} %bitcast.12), calls=%async_computation | async-start | bytes 4718592 | tf_op jit(solution)/shard_map/all_to_all | solution.py:97
  61.3 4.2 %collective-permute-start.2 = (bf16[16,96,256]{2,1,0:T(8,128)(2,1)S(1)}, bf16[16,96,256]{2,1,0:T(8,128)(2,1)S(1)}, u32[]{:S(2)}, u32[]{:S(2)}) collective-permute-start(bf16[16,96,256]{2,1,0:T(8,128)(2,1)S(1)} %get-tuple-element.8), channel_id=1, source_target_pairs={{0,1},{1,0},{2,3},{3,2},{4,5},{5,4},{6,7},{7,6},{8,9},{9,8},{10,11... | collective-permute-start | bytes 2359304 | tf_op jit(solution)/shard_map/ppermute | solution.py:113
  65.7 64.0 %collective-permute-start.3 = (bf16[8,96,256]{2,1,0:T(8,128)(2,1)S(1)}, bf16[8,96,256]{2,1,0:T(8,128)(2,1)S(1)}, u32[]{:S(2)}, u32[]{:S(2)}) collective-permute-start(bf16[8,96,256]{2,1,0:T(8,128)(2,1)S(1)} %slice.56), channel_id=1, source_target_pairs={{0,2},{2,0},{1,3},{3,1},{4,6},{6,4},{5,7},{7,5},{8,10},{10,8},{9,1... | collective-permute-start | bytes 1179656 | tf_op jit(solution)/shard_map/ppermute | solution.py:121
  129.8 7.7 %collective-permute-start.4 = (bf16[4,96,256]{2,1,0:T(8,128)(2,1)S(1)}, bf16[4,96,256]{2,1,0:T(8,128)(2,1)S(1)}, u32[]{:S(2)}, u32[]{:S(2)}) collective-permute-start(bf16[4,96,256]{2,1,0:T(8,128)(2,1)S(1)} %slice.57), channel_id=1, source_target_pairs={{0,4},{4,0},{8,12},{12,8},{16,20},{20,16},{24,28},{28,24},{1,5},{5... | collective-permute-start | bytes 589832 | tf_op jit(solution)/shard_map/ppermute | solution.py:121
  137.6 8.2 %collective-permute-start.5 = (bf16[2,96,256]{2,1,0:T(8,128)(2,1)S(1)}, bf16[2,96,256]{2,1,0:T(8,128)(2,1)S(1)}, u32[]{:S(2)}, u32[]{:S(2)}) collective-permute-start(bf16[2,96,256]{2,1,0:T(8,128)(2,1)S(1)} %slice.58), channel_id=1, source_target_pairs={{0,8},{4,12},{8,0},{12,4},{16,24},{20,28},{24,16},{28,20},{1,9},{5... | collective-permute-start | bytes 294920 | tf_op jit(solution)/shard_map/ppermute | solution.py:121
  145.9 10.4 %collective-permute-start.6 = (bf16[1,96,256]{2,1,0:T(8,128)(2,1)S(1)}, bf16[1,96,256]{2,1,0:T(8,128)(2,1)S(1)}, u32[]{:S(2)}, u32[]{:S(2)}) collective-permute-start(bf16[1,96,256]{2,1,0:T(8,128)(2,1)S(1)} %slice.59), channel_id=1, source_target_pairs={{0,16},{4,20},{8,24},{12,28},{16,0},{20,4},{24,8},{28,12},{1,17},{... | collective-permute-start | bytes 147464 | tf_op jit(solution)/shard_map/ppermute | solution.py:121

commit v3 on v2

v3 whole, which is shorter than its diff:
```python
import jax
import jax.numpy as jnp
from jax import lax
from jax.experimental import pallas as pl
from jax.experimental.pallas import tpu as pltpu
from jax.sharding import Mesh, PartitionSpec as P

DP = ("zh", "zl", "xh")
MP = ("y", "xl", "c")
F32 = jnp.float32
BF16 = jnp.bfloat16
VMEM = pl.BlockSpec(memory_space=pltpu.VMEM)
SMEM = pl.BlockSpec(memory_space=pltpu.SMEM)
PAIR = [(0, 1), (1, 0)]


def gelu_slope(pre):
    coef = 0.7978845608028654
    inner = coef * (pre + 0.044715 * pre * pre * pre)
    tval = jnp.tanh(inner)
    return 0.5 * (1.0 + tval) + 0.5 * pre * (1.0 - tval * tval) * coef * (
        1.0 + 3.0 * 0.044715 * pre * pre
    )


def hidden_kernel(
    at_ref, own_ref, mine_ref, other_ref, w_hbm, g_ref, whole, pg_ref, keep_ref, send_ref, w_ref, sem
):
    load = pltpu.make_async_copy(w_hbm, w_ref, sem)
    load.start()
    y_own, xl, core = at_ref[0], at_ref[1], at_ref[2]
    ny, _, feats, _ = own_ref.shape
    bits = ny.bit_length() - 1

    def put(y, x, c, block):
        start = pl.multiple_of((4 * y + 2 * x + c) * feats, feats)
        whole[pl.ds(start, feats), :] = block

    for y in range(ny):
        put(y, xl, 0, own_ref[y, 0])
        put(y, xl, 1, own_ref[y, 1])
        put(y, 1 - xl, core, mine_ref[y])
        put(y, 1 - xl, 1 - core, other_ref[y])
    load.wait()
    pre = lax.dot_general(
        whole[...], w_ref[...], (((0,), (0,)), ((), ())), preferred_element_type=F32
    )
    pg = (g_ref[...].astype(F32) * gelu_slope(pre)).astype(BF16)
    pg_ref[...] = pg
    for r in range(ny):
        at = sum((r >> k & 1) << (bits - 1 - k) for k in range(bits))
        start = lax.bitwise_xor(y_own, jnp.int32(r)) * (4 * feats)
        block = lax.dot_general(
            w_ref[pl.ds(pl.multiple_of(start, 4 * feats), 4 * feats), :],
            pg,
            (((1,), (1,)), ((), ())),
            preferred_element_type=F32,
        )
        for c in range(2):

            @pl.when(core == c)
            def _():
                for x in range(2):
                    to = lax.bitwise_xor(xl, jnp.int32(x)) * ny + at
                    for ref, b in ((keep_ref, 2 * x + c), (send_ref, 2 * x + 1 - c)):
                        rows = block[b * feats : (b + 1) * feats]
                        ref[to] = rows.astype(ref.dtype)


def weight_kernel(at_ref, whole, tmine_ref, tother_ref, pg_ref, pgpair_ref, out_ref):
    xl, core, zl = at_ref[1], at_ref[2], at_ref[3]
    feats = tmine_ref.shape[2]
    for i in range(out_ref.shape[0] // 4):
        for x in range(2):
            for ref, c in ((tmine_ref, core), (tother_ref, 1 - core)):
                b = 2 * lax.bitwise_xor(xl, jnp.int32(x)) + c
                start = pl.multiple_of((4 * (2 * i + zl) + b) * feats, feats)
                total = jnp.dot(
                    whole[pl.ds(start, feats), :], pg_ref[...], preferred_element_type=F32
                ) + jnp.dot(ref[x, i], pgpair_ref[...], preferred_element_type=F32)
                out_ref[4 * i + b] = total.astype(BF16)


def halve(total, axis, pairs):
    half = total.shape[0] // 2
    arrived = lax.ppermute(total[half:].astype(BF16), axis, pairs)
    return total[:half] + arrived.astype(F32)


def make_local(nz, nx, ny):
    nh = nz // 2

    def local(tokens, w_in, hidden_grad):
        rows, feats = tokens.shape
        d, hidden = w_in.shape
        core, zl = lax.axis_index("c"), lax.axis_index("zl")
        at = jnp.stack([lax.axis_index("y"), lax.axis_index("xl"), core, zl]).astype(jnp.int32)

        def pick(array, index, axis):
            return lax.dynamic_index_in_dim(array, index, axis, keepdims=False)

        own = lax.all_gather(tokens.T, ("y", "c"), axis=0).reshape(ny, 2, feats, rows)
        half = pick(own, core, 1)
        mine = lax.ppermute(half, "xl", PAIR)
        other = lax.ppermute(mine, "c", PAIR)
        forth = jnp.stack(
            [pick(a.reshape(nh, 2, feats, rows), 1 - zl, 1) for a in (half, mine)]
        )
        tmine = lax.ppermute(forth, "zl", PAIR)
        tother = lax.ppermute(tmine, "c", PAIR)
        whole, pre_grad, keep, send = pl.pallas_call(
            hidden_kernel,
            out_shape=(
                jax.ShapeDtypeStruct((d, rows), BF16),
                jax.ShapeDtypeStruct((rows, hidden), BF16),
                jax.ShapeDtypeStruct((2 * ny, feats, rows), F32),
                jax.ShapeDtypeStruct((2 * ny, feats, rows), BF16),
            ),
            in_specs=[SMEM, VMEM, VMEM, VMEM, pl.BlockSpec(memory_space=pltpu.HBM), VMEM],
            out_specs=(VMEM, VMEM, VMEM, VMEM),
            scratch_shapes=[pltpu.VMEM((d, hidden), BF16), pltpu.SemaphoreType.DMA],
            compiler_params=pltpu.CompilerParams(vmem_limit_bytes=8 << 20),
            cost_estimate=pl.CostEstimate(
                flops=4 * d * rows * hidden,
                bytes_accessed=8 << 20,
                transcendentals=rows * hidden,
            ),
        )(at, own, mine, other, w_in, hidden_grad)
        pair_grad = lax.ppermute(pre_grad, "zl", PAIR)
        total = keep + lax.ppermute(send, "c", PAIR).astype(F32)
        total = halve(total, "xl", PAIR)
        total, tother = lax.optimization_barrier((total, tother))
        wpart = pl.pallas_call(
            weight_kernel,
            out_shape=jax.ShapeDtypeStruct((4 * nh, feats, hidden), BF16),
            in_specs=[SMEM, VMEM, VMEM, VMEM, VMEM, VMEM],
            out_specs=VMEM,
            compiler_params=pltpu.CompilerParams(vmem_limit_bytes=4 << 20),
            cost_estimate=pl.CostEstimate(
                flops=2 * d * rows * hidden, bytes_accessed=4 << 20, transcendentals=0
            ),
        )(at, whole, tmine, tother, pre_grad, pair_grad)
        wpart = wpart.reshape(nh * nx, -1, hidden)
        pieces = lax.all_to_all(wpart, ("zh", "xh"), 0, 0, tiled=True)
        bit = 1
        while bit < ny:
            total = halve(total, "y", [(i, i ^ bit) for i in range(ny)])
            bit *= 2
        weight_sum = jnp.sum(pieces.astype(F32), axis=0)
        return (total[0].astype(BF16).T, weight_sum.astype(BF16))

    return local


def solution(mesh, sizes=(8, 4, 8)):
    nz, nx, ny = sizes
    split = Mesh(mesh.devices.reshape(nz // 2, 2, nx, ny, 2, 2), DP + MP)
    return jax.shard_map(
        make_local(*sizes),
        mesh=split,
        in_specs=(P(DP, MP), P(None, MP), P(DP, MP)),
        out_specs=(P(DP, MP), P(DP, MP)),
        check_vma=False,
    )
```

time: 160 us -> 137 us (0.86)
  the two profiles are of different devices: /device:TPU:514 before, /device:TPU:1 now
where the time goes in v3:
time: 137 us; the launch traced here: 135 us
  waiting for transfers between devices  50.5 us (37%)
  starting transfers between devices  36.4 us (27%)
  blocking collectives  31.2 us (23%)
  Pallas kernels  8.76 us (6%)
  other arithmetic  3.94 us (3%)
  local copies, waits for them, and re-layouts  3.03 us (2%)
    all_gather x1, blocking collectives, local(): lax.all_gather(tokens.T, ('y', 'c'), axis=0).reshape(ny, 2, feats, rows)  31.2 us
    ppermute x4, waiting for transfers between devices, halve(): arrived = lax.ppermute(total[half:].astype(BF16), axis, pairs)  15.6 us
    all_to_all x1, starting transfers between devices, local(): pieces = lax.all_to_all(wpart, ('zh', 'xh'), 0, 0, tiled=True)  12.3 us
    all_to_all x1, waiting for transfers between devices, local(): pieces = lax.all_to_all(wpart, ('zh', 'xh'), 0, 0, tiled=True)  10.5 us
    ppermute x1, waiting for transfers between devices, local(): mine = lax.ppermute(half, 'xl', PAIR)  10.5 us
    ppermute x4, starting transfers between devices, halve(): arrived = lax.ppermute(total[half:].astype(BF16), axis, pairs)  10.2 us
    ppermute x1, waiting for transfers between devices, local(): tmine = lax.ppermute(forth, 'zl', PAIR)  7.02 us
    pallas_call x1, Pallas kernels, local(): pl.pallas_call(hidden_kernel, out_shape=(jax.ShapeDtypeStruct((d, rows),...  6.07 us
  transfers between devices with their start and end apart: 11, of which 9 were waited for; matrix products, arithmetic and copies ran while one was open for 2% of the time, Pallas kernels for 0%

profile of v3, /device:TPU:1, one launch (start us, length us, event | category | flops | bytes accessed | tf_op | source)
XLA Modules:
  0.0 134.7 jit_solution(12972536917899017292)
XLA Ops:
  0.6 31.2 %all-gather = bf16[1536,256]{1,0:T(8,128)(2,1)S(1)} all-gather(bf16[96,256]{1,0:T(8,128)(2,1)} %bitcast.25), channel_id=2, replica_groups=mesh['zh'=4,'zl'=2,'xh'=4,'y'=8,'xl'=2,'c'=2] {'y','c'}, dimensions={0}, use_global_device_ids=true | all-gather | bytes 835584 | tf_op jit(solution)/shard_map/all_gather | solution.py:102
  31.9 1.9 %collective-permute-start = (bf16[8,96,256]{2,1,0:T(8,128)(2,1)S(1)}, bf16[8,96,256]{2,1,0:T(8,128)(2,1)S(1)}, u32[]{:S(2)}, u32[]{:S(2)}) collective-permute-start(bf16[8,96,256]{2,1,0:T(8,128)(2,1)S(1)} %fusion.2), channel_id=1, source_target_pairs={{0,2},{2,0},{1,3},{3,1},{4,6},{6,4},{5,7},{7,5},{8,10},{10,8},{9,1... | collective-permute-start | bytes 1179656 | tf_op jit(solution)/shard_map/ppermute | solution.py:104
  33.8 10.5 %collective-permute-done.mine_ref = bf16[8,96,256]{2,1,0:T(8,128)(2,1)S(1)} collective-permute-done((bf16[8,96,256]{2,1,0:T(8,128)(2,1)S(1)}, bf16[8,96,256]{2,1,0:T(8,128)(2,1)S(1)}, u32[]{:S(2)}, u32[]{:S(2)}) %collective-permute-start) | collective-permute-done | bytes 393248 | tf_op jit(solution)/shard_map/ppermute | solution.py:104
  44.4 2.9 %collective-permute-start.1 = (bf16[8,96,256]{2,1,0:T(8,128)(2,1)S(1)}, bf16[8,96,256]{2,1,0:T(8,128)(2,1)S(1)}, u32[]{:S(2)}, u32[]{:S(2)}) collective-permute-start(bf16[8,96,256]{2,1,0:T(8,128)(2,1)S(1)} %collective-permute-done.mine_ref), channel_id=1, source_target_pairs={{0,1},{1,0},{2,3},{3,2},{4,5},{5,4},{6,7},{7,6},{8,9},{9,8},{10,11... | collective-permute-start | bytes 1179656 | tf_op jit(solution)/shard_map/ppermute | solution.py:105
  47.3 1.2 collective-permute-done.1.other_ref
  48.6 1.7 %copy-done.2 = bf16[3072,384]{1,0:T(8,128)(2,1)S(1)} copy-done((bf16[3072,384]{1,0:T(8,128)(2,1)S(1)}, bf16[3072,384]{1,0:T(8,128)(2,1)}, u32[]{:S(2)}) %copy-start.2) | copy-done | bytes 2359320
  50.2 6.1 %shard_map.50 = (bf16[3072,256]{1,0:T(8,128)(2,1)S(1)}, bf16[256,384]{1,0:T(8,128)(2,1)S(1)}, f32[16,96,256]{2,1,0:T(8,128)S(1)}, bf16[16,96,256]{2,1,0:T(8,128)(2,1)}) custom-call(s32[4]{0:T(128)S(1)} %pad_add_fusion.at_ref, bf16[8,2,96,256]{3,2,1,0:T(8,128)(2,1)S(1)} %bitcast.21, bf16[8,96,256]{2,1,0:T(8,128)(2,1)S(1)} %collective-permute-done.mine_ref, ...), custom_call_target="tpu_custom_call" | custom-call | flops 1207959552 | bytes 8388608 | tf_op jit(solution)/shard_map/pallas_call | solution.py:111
  57.5 2.2 %collective-permute-start.2 = (bf16[16,96,256]{2,1,0:T(8,128)(2,1)}, bf16[16,96,256]{2,1,0:T(8,128)(2,1)}, u32[]{:S(2)}, u32[]{:S(2)}) collective-permute-start(bf16[16,96,256]{2,1,0:T(8,128)(2,1)} %get-tuple-element.9), channel_id=1, source_target_pairs={{0,1},{1,0},{2,3},{3,2},{4,5},{5,4},{6,7},{7,6},{8,9},{9,8},{10,11... | collective-permute-start | bytes 2359304 | tf_op jit(solution)/shard_map/ppermute | solution.py:130
  59.8 2.1 %collective-permute-start.4 = (bf16[2,4,96,256]{3,2,1,0:T(8,128)(2,1)S(1)}, bf16[2,4,96,256]{3,2,1,0:T(8,128)(2,1)S(1)}, u32[]{:S(2)}, u32[]{:S(2)}) collective-permute-start(bf16[2,4,96,256]{3,2,1,0:T(8,128)(2,1)S(1)} %pad_maximum_fusion), channel_id=1, source_target_pairs={{0,128},{128,0},{1,129},{129,1},{2,130},{130,2},{3,131},{131,3},{4... | collective-permute-start | bytes 1179656 | tf_op jit(solution)/shard_map/ppermute | solution.py:109
  62.0 1.3 convert_add_fusion
  63.4 1.9 %collective-permute-start.3 = (bf16[8,96,256]{2,1,0:T(8,128)(2,1)S(1)}, bf16[8,96,256]{2,1,0:T(8,128)(2,1)S(1)}, u32[]{:S(2)}, u32[]{:S(2)}) collective-permute-start(bf16[8,96,256]{2,1,0:T(8,128)(2,1)S(1)} %slice.55), channel_id=1, source_target_pairs={{0,2},{2,0},{1,3},{3,1},{4,6},{6,4},{5,7},{7,5},{8,10},{10,8},{9,1... | collective-permute-start | bytes 1179656 | tf_op jit(solution)/shard_map/ppermute | solution.py:86
  65.3 7.0 %collective-permute-done.4.tmine_ref = bf16[2,4,96,256]{3,2,1,0:T(8,128)(2,1)S(1)} collective-permute-done((bf16[2,4,96,256]{3,2,1,0:T(8,128)(2,1)S(1)}, bf16[2,4,96,256]{3,2,1,0:T(8,128)(2,1)S(1)}, u32[]{:S(2)}, u32[]{:S(2)}) %collective-permute-start.4) | collective-permute-done | bytes 393248 | tf_op jit(solution)/shard_map/ppermute | solution.py:109
  72.3 2.9 %collective-permute-start.5 = (bf16[2,4,96,256]{3,2,1,0:T(8,128)(2,1)S(1)}, bf16[2,4,96,256]{3,2,1,0:T(8,128)(2,1)S(1)}, u32[]{:S(2)}, u32[]{:S(2)}) collective-permute-start(bf16[2,4,96,256]{3,2,1,0:T(8,128)(2,1)S(1)} %collective-permute-done.4.tmine_ref), channel_id=1, source_target_pairs={{0,1},{1,0},{2,3},{3,2},{4,5},{5,4},{6,7},{7,6},{8,9},{9,8},{10,11... | collective-permute-start | bytes 1179656 | tf_op jit(solution)/shard_map/ppermute | solution.py:110
  75.3 1.9 %collective-permute-start.9 = (bf16[256,384]{1,0:T(8,128)(2,1)S(1)}, bf16[256,384]{1,0:T(8,128)(2,1)S(1)}, u32[]{:S(2)}, u32[]{:S(2)}) collective-permute-start(bf16[256,384]{1,0:T(8,128)(2,1)S(1)} %get-tuple-element.13.pg_ref), channel_id=1, source_target_pairs={{0,128},{128,0},{1,129},{129,1},{2,130},{130,2},{3,131},{131,3},{4... | collective-permute-start | bytes 589832 | tf_op jit(solution)/shard_map/ppermute | solution.py:129
  78.2 5.5 %collective-permute-done.9.pgpair_ref = bf16[256,384]{1,0:T(8,128)(2,1)S(1)} collective-permute-done((bf16[256,384]{1,0:T(8,128)(2,1)S(1)}, bf16[256,384]{1,0:T(8,128)(2,1)S(1)}, u32[]{:S(2)}, u32[]{:S(2)}) %collective-permute-start.9) | collective-permute-done | bytes 196640 | tf_op jit(solution)/shard_map/ppermute | solution.py:129
  83.7 2.7 %shard_map.51 = bf16[16,96,384]{2,1,0:T(8,128)(2,1)} custom-call(s32[4]{0:T(128)S(1)} %pad_add_fusion.at_ref, bf16[3072,256]{1,0:T(8,128)(2,1)S(1)} %get-tuple-element.11.whole, bf16[2,4,96,256]{3,2,1,0:T(8,128)(2,1)S(1)} %collective-permute-done.4.tmine_ref, bf16[2,4,96,256]{3,2,1,0:T(8,128)(2,1)S(1)} %collective-permute-done.5.tother_ref, ...), custom_call_target="tpu_custom_call" | custom-call | flops 603979776 | bytes 4194304 | tf_op jit(solution)/shard_map/pallas_call | solution.py:133
  86.4 12.3 %all-to-all-start = ((bf16[16,96,384]{2,1,0:T(8,128)(2,1)}), bf16[16,96,384]{2,1,0:T(8,128)(2,1)S(1)}, u32[]{:S(2)}, u32[]{:S(2)}) async-start(bf16[16,96,384]{2,1,0:T(8,128)(2,1)} %shard_map.51), calls=%async_computation | async-start | bytes 2359296 | tf_op jit(solution)/shard_map/all_to_all | solution.py:144
  98.8 1.9 %collective-permute-start.6 = (bf16[4,96,256]{2,1,0:T(8,128)(2,1)S(1)}, bf16[4,96,256]{2,1,0:T(8,128)(2,1)S(1)}, u32[]{:S(2)}, u32[]{:S(2)}) collective-permute-start(bf16[4,96,256]{2,1,0:T(8,128)(2,1)S(1)} %slice.56), channel_id=1, source_target_pairs={{0,4},{4,0},{8,12},{12,8},{16,20},{20,16},{24,28},{28,24},{1,5},{5... | collective-permute-start | bytes 589832 | tf_op jit(solution)/shard_map/ppermute | solution.py:86
  100.7 5.3 %collective-permute-done.6 = bf16[4,96,256]{2,1,0:T(8,128)(2,1)S(1)} collective-permute-done((bf16[4,96,256]{2,1,0:T(8,128)(2,1)S(1)}, bf16[4,96,256]{2,1,0:T(8,128)(2,1)S(1)}, u32[]{:S(2)}, u32[]{:S(2)}) %collective-permute-start.6) | collective-permute-done | bytes 196640 | tf_op jit(solution)/shard_map/ppermute | solution.py:86
  106.0 1.9 %collective-permute-start.7 = (bf16[2,96,256]{2,1,0:T(8,128)(2,1)S(1)}, bf16[2,96,256]{2,1,0:T(8,128)(2,1)S(1)}, u32[]{:S(2)}, u32[]{:S(2)}) collective-permute-start(bf16[2,96,256]{2,1,0:T(8,128)(2,1)S(1)} %slice.57), channel_id=1, source_target_pairs={{0,8},{4,12},{8,0},{12,4},{16,24},{20,28},{24,16},{28,20},{1,9},{5... | collective-permute-start | bytes 294920 | tf_op jit(solution)/shard_map/ppermute | solution.py:86
  108.0 5.7 %collective-permute-done.7 = bf16[2,96,256]{2,1,0:T(8,128)(2,1)S(1)} collective-permute-done((bf16[2,96,256]{2,1,0:T(8,128)(2,1)S(1)}, bf16[2,96,256]{2,1,0:T(8,128)(2,1)S(1)}, u32[]{:S(2)}, u32[]{:S(2)}) %collective-permute-start.7) | collective-permute-done | bytes 98336 | tf_op jit(solution)/shard_map/ppermute | solution.py:86
  113.7 4.4 %collective-permute-start.8 = (bf16[1,96,256]{2,1,0:T(8,128)(2,1)S(1)}, bf16[1,96,256]{2,1,0:T(8,128)(2,1)S(1)}, u32[]{:S(2)}, u32[]{:S(2)}) collective-permute-start(bf16[1,96,256]{2,1,0:T(8,128)(2,1)S(1)} %slice.58), channel_id=1, source_target_pairs={{0,16},{4,20},{8,24},{12,28},{16,0},{20,4},{24,8},{28,12},{1,17},{... | collective-permute-start | bytes 147464 | tf_op jit(solution)/shard_map/ppermute | solution.py:86
  118.1 4.6 %collective-permute-done.8 = bf16[1,96,256]{2,1,0:T(8,128)(2,1)S(1)} collective-permute-done((bf16[1,96,256]{2,1,0:T(8,128)(2,1)S(1)}, bf16[1,96,256]{2,1,0:T(8,128)(2,1)S(1)}, u32[]{:S(2)}, u32[]{:S(2)}) %collective-permute-start.8) | collective-permute-done | bytes 49184 | tf_op jit(solution)/shard_map/ppermute | solution.py:86
  123.4 10.5 %all-to-all-done = bf16[16,96,384]{2,1,0:T(8,128)(2,1)S(1)} async-done(((bf16[16,96,384]{2,1,0:T(8,128)(2,1)}), bf16[16,96,384]{2,1,0:T(8,128)(2,1)S(1)}, u32[]{:S(2)}, u32[]{:S(2)}) %all-to-all-start) | async-done | bytes 1179680 | tf_op jit(solution)/shard_map/all_to_all | solution.py:144
  (27 shorter events, 4.1 us)
Async XLA Ops:
  0.6 47.9 %copy-start.3 = (bf16[256,384]{1,0:T(8,128)(2,1)S(1)}, bf16[256,384]{1,0:T(8,128)(2,1)}, u32[]{:S(2)}) copy-start(bf16[256,384]{1,0:T(8,128)(2,1)} %g_ref.1) | copy-start | bytes 589828
  31.9 12.5 %collective-permute-start = (bf16[8,96,256]{2,1,0:T(8,128)(2,1)S(1)}, bf16[8,96,256]{2,1,0:T(8,128)(2,1)S(1)}, u32[]{:S(2)}, u32[]{:S(2)}) collective-permute-start(bf16[8,96,256]{2,1,0:T(8,128)(2,1)S(1)} %fusion.2), channel_id=1, source_target_pairs={{0,2},{2,0},{1,3},{3,1},{4,6},{6,4},{5,7},{7,5},{8,10},{10,8},{9,1... | collective-permute-start | bytes 1179656 | tf_op jit(solution)/shard_map/ppermute | solution.py:104
  44.4 4.2 %collective-permute-start.1 = (bf16[8,96,256]{2,1,0:T(8,128)(2,1)S(1)}, bf16[8,96,256]{2,1,0:T(8,128)(2,1)S(1)}, u32[]{:S(2)}, u32[]{:S(2)}) collective-permute-start(bf16[8,96,256]{2,1,0:T(8,128)(2,1)S(1)} %collective-permute-done.mine_ref), channel_id=1, source_target_pairs={{0,1},{1,0},{2,3},{3,2},{4,5},{5,4},{6,7},{7,6},{8,9},{9,8},{10,11... | collective-permute-start | bytes 1179656 | tf_op jit(solution)/shard_map/ppermute | solution.py:105
  48.6 1.7 %copy-start.2 = (bf16[3072,384]{1,0:T(8,128)(2,1)S(1)}, bf16[3072,384]{1,0:T(8,128)(2,1)}, u32[]{:S(2)}) copy-start(bf16[3072,384]{1,0:T(8,128)(2,1)} %w_hbm.1) | copy-start | bytes 7077892
  56.3 1.2 copy-start
  57.5 4.5 %collective-permute-start.2 = (bf16[16,96,256]{2,1,0:T(8,128)(2,1)}, bf16[16,96,256]{2,1,0:T(8,128)(2,1)}, u32[]{:S(2)}, u32[]{:S(2)}) collective-permute-start(bf16[16,96,256]{2,1,0:T(8,128)(2,1)} %get-tuple-element.9), channel_id=1, source_target_pairs={{0,1},{1,0},{2,3},{3,2},{4,5},{5,4},{6,7},{7,6},{8,9},{9,8},{10,11... | collective-permute-start | bytes 2359304 | tf_op jit(solution)/shard_map/ppermute | solution.py:130
  59.7 2.3 %copy-start.1 = (f32[16,96,256]{2,1,0:T(8,128)S(1)}, f32[16,96,256]{2,1,0:T(8,128)}, u32[]{:S(2)}) copy-start(f32[16,96,256]{2,1,0:T(8,128)} %copy-done) | copy-start | bytes 4718596
  59.8 12.5 %collective-permute-start.4 = (bf16[2,4,96,256]{3,2,1,0:T(8,128)(2,1)S(1)}, bf16[2,4,96,256]{3,2,1,0:T(8,128)(2,1)S(1)}, u32[]{:S(2)}, u32[]{:S(2)}) collective-permute-start(bf16[2,4,96,256]{3,2,1,0:T(8,128)(2,1)S(1)} %pad_maximum_fusion), channel_id=1, source_target_pairs={{0,128},{128,0},{1,129},{129,1},{2,130},{130,2},{3,131},{131,3},{4... | collective-permute-start | bytes 1179656 | tf_op jit(solution)/shard_map/ppermute | solution.py:109
  63.4 13.8 %collective-permute-start.3 = (bf16[8,96,256]{2,1,0:T(8,128)(2,1)S(1)}, bf16[8,96,256]{2,1,0:T(8,128)(2,1)S(1)}, u32[]{:S(2)}, u32[]{:S(2)}) collective-permute-start(bf16[8,96,256]{2,1,0:T(8,128)(2,1)S(1)} %slice.55), channel_id=1, source_target_pairs={{0,2},{2,0},{1,3},{3,1},{4,6},{6,4},{5,7},{7,5},{8,10},{10,8},{9,1... | collective-permute-start | bytes 1179656 | tf_op jit(solution)/shard_map/ppermute | solution.py:86
  72.3 5.9 %collective-permute-start.5 = (bf16[2,4,96,256]{3,2,1,0:T(8,128)(2,1)S(1)}, bf16[2,4,96,256]{3,2,1,0:T(8,128)(2,1)S(1)}, u32[]{:S(2)}, u32[]{:S(2)}) collective-permute-start(bf16[2,4,96,256]{3,2,1,0:T(8,128)(2,1)S(1)} %collective-permute-done.4.tmine_ref), channel_id=1, source_target_pairs={{0,1},{1,0},{2,3},{3,2},{4,5},{5,4},{6,7},{7,6},{8,9},{9,8},{10,11... | collective-permute-start | bytes 1179656 | tf_op jit(solution)/shard_map/ppermute | solution.py:110
  75.3 8.4 %collective-permute-start.9 = (bf16[256,384]{1,0:T(8,128)(2,1)S(1)}, bf16[256,384]{1,0:T(8,128)(2,1)S(1)}, u32[]{:S(2)}, u32[]{:S(2)}) collective-permute-start(bf16[256,384]{1,0:T(8,128)(2,1)S(1)} %get-tuple-element.13.pg_ref), channel_id=1, source_target_pairs={{0,128},{128,0},{1,129},{129,1},{2,130},{130,2},{3,131},{131,3},{4... | collective-permute-start | bytes 589832 | tf_op jit(solution)/shard_map/ppermute | solution.py:129
  86.4 12.3 %copy-start.4 = (f32[8,96,256]{2,1,0:T(8,128)S(1)}, f32[8,96,256]{2,1,0:T(8,128)}, u32[]{:S(2)}) copy-start(f32[8,96,256]{2,1,0:T(8,128)} %slice_add_fusion) | copy-start | bytes 2359300
  86.4 47.5 %all-to-all-start = ((bf16[16,96,384]{2,1,0:T(8,128)(2,1)}), bf16[16,96,384]{2,1,0:T(8,128)(2,1)S(1)}, u32[]{:S(2)}, u32[]{:S(2)}) async-start(bf16[16,96,384]{2,1,0:T(8,128)(2,1)} %shard_map.51), calls=%async_computation | async-start | bytes 2359296 | tf_op jit(solution)/shard_map/all_to_all | solution.py:144
  98.8 7.2 %collective-permute-start.6 = (bf16[4,96,256]{2,1,0:T(8,128)(2,1)S(1)}, bf16[4,96,256]{2,1,0:T(8,128)(2,1)S(1)}, u32[]{:S(2)}, u32[]{:S(2)}) collective-permute-start(bf16[4,96,256]{2,1,0:T(8,128)(2,1)S(1)} %slice.56), channel_id=1, source_target_pairs={{0,4},{4,0},{8,12},{12,8},{16,20},{20,16},{24,28},{28,24},{1,5},{5... | collective-permute-start | bytes 589832 | tf_op jit(solution)/shard_map/ppermute | solution.py:86
  106.0 7.6 %collective-permute-start.7 = (bf16[2,96,256]{2,1,0:T(8,128)(2,1)S(1)}, bf16[2,96,256]{2,1,0:T(8,128)(2,1)S(1)}, u32[]{:S(2)}, u32[]{:S(2)}) collective-permute-start(bf16[2,96,256]{2,1,0:T(8,128)(2,1)S(1)} %slice.57), channel_id=1, source_target_pairs={{0,8},{4,12},{8,0},{12,4},{16,24},{20,28},{24,16},{28,20},{1,9},{5... | collective-permute-start | bytes 294920 | tf_op jit(solution)/shard_map/ppermute | solution.py:86
  113.7 9.0 %collective-permute-start.8 = (bf16[1,96,256]{2,1,0:T(8,128)(2,1)S(1)}, bf16[1,96,256]{2,1,0:T(8,128)(2,1)S(1)}, u32[]{:S(2)}, u32[]{:S(2)}) collective-permute-start(bf16[1,96,256]{2,1,0:T(8,128)(2,1)S(1)} %slice.58), channel_id=1, source_target_pairs={{0,16},{4,20},{8,24},{12,28},{16,0},{20,4},{24,8},{28,12},{1,17},{... | collective-permute-start | bytes 147464 | tf_op jit(solution)/shard_map/ppermute | solution.py:86

commit v4 on v3

--- a/solution.py
+++ b/solution.py
@@ -24,10 +24,8 @@
 
 
 def hidden_kernel(
-    at_ref, own_ref, mine_ref, other_ref, w_hbm, g_ref, whole, pg_ref, keep_ref, send_ref, w_ref, sem
+    at_ref, own_ref, mine_ref, other_ref, w_ref, g_ref, whole, pg_ref, keep_ref, send_ref
 ):
-    load = pltpu.make_async_copy(w_hbm, w_ref, sem)
-    load.start()
     y_own, xl, core = at_ref[0], at_ref[1], at_ref[2]
     ny, _, feats, _ = own_ref.shape
     bits = ny.bit_length() - 1
@@ -41,7 +39,6 @@
         put(y, xl, 1, own_ref[y, 1])
         put(y, 1 - xl, core, mine_ref[y])
         put(y, 1 - xl, 1 - core, other_ref[y])
-    load.wait()
     pre = lax.dot_general(
         whole[...], w_ref[...], (((0,), (0,)), ((), ())), preferred_element_type=F32
     )
@@ -61,7 +58,7 @@
             @pl.when(core == c)
             def _():
                 for x in range(2):
-                    to = lax.bitwise_xor(xl, jnp.int32(x)) * ny + at
+                    to = 2 * at + lax.bitwise_xor(xl, jnp.int32(x))
                     for ref, b in ((keep_ref, 2 * x + c), (send_ref, 2 * x + 1 - c)):
                         rows = block[b * feats : (b + 1) * feats]
                         ref[to] = rows.astype(ref.dtype)
@@ -107,7 +104,6 @@
             [pick(a.reshape(nh, 2, feats, rows), 1 - zl, 1) for a in (half, mine)]
         )
         tmine = lax.ppermute(forth, "zl", PAIR)
-        tother = lax.ppermute(tmine, "c", PAIR)
         whole, pre_grad, keep, send = pl.pallas_call(
             hidden_kernel,
             out_shape=(
@@ -116,9 +112,8 @@
                 jax.ShapeDtypeStruct((2 * ny, feats, rows), F32),
                 jax.ShapeDtypeStruct((2 * ny, feats, rows), BF16),
             ),
-            in_specs=[SMEM, VMEM, VMEM, VMEM, pl.BlockSpec(memory_space=pltpu.HBM), VMEM],
+            in_specs=[SMEM, VMEM, VMEM, VMEM, VMEM, VMEM],
             out_specs=(VMEM, VMEM, VMEM, VMEM),
-            scratch_shapes=[pltpu.VMEM((d, hidden), BF16), pltpu.SemaphoreType.DMA],
             compiler_params=pltpu.CompilerParams(vmem_limit_bytes=8 << 20),
             cost_estimate=pl.CostEstimate(
                 flops=4 * d * rows * hidden,
@@ -126,9 +121,10 @@
                 transcendentals=rows * hidden,
             ),
         )(at, own, mine, other, w_in, hidden_grad)
+        pre_grad, send, tmine = lax.optimization_barrier((pre_grad, send, tmine))
         pair_grad = lax.ppermute(pre_grad, "zl", PAIR)
+        tother = lax.ppermute(tmine, "c", PAIR)
         total = keep + lax.ppermute(send, "c", PAIR).astype(F32)
-        total = halve(total, "xl", PAIR)
         total, tother = lax.optimization_barrier((total, tother))
         wpart = pl.pallas_call(
             weight_kernel,
@@ -146,6 +142,7 @@
         while bit < ny:
             total = halve(total, "y", [(i, i ^ bit) for i in range(ny)])
             bit *= 2
+        total = halve(total, "xl", PAIR)
         weight_sum = jnp.sum(pieces.astype(F32), axis=0)
         return (total[0].astype(BF16).T, weight_sum.astype(BF16))
 

time: 137 us -> 130 us (0.949)
  other arithmetic: 3.94 us -> 1.89 us
    ppermute x4, waiting for transfers between devices: 15.6 us -> 29.5 us  [halve(): arrived = lax.ppermute(total[half:].astype(BF16), axis, pairs)]
    all_to_all x1, waiting for transfers between devices: 10.5 us -> 0.01 us  [local(): pieces = lax.all_to_all(wpart, ('zh', 'xh'), 0, 0, tiled=True)]
    ppermute x1, waiting for transfers between devices: 7.02 us -> 3.93 us  [local(): tmine = lax.ppermute(forth, 'zl', PAIR)]
    unnamed x10 -> x4, local copies, waits for them, and re-layouts: 2.83 us -> 1.67 us
  transfers between devices with their start and end apart: 11 -> 11, of which waited for: 9 -> 7; matrix products, arithmetic and copies ran while one was open for 2% -> 1% of each run, Pallas kernels for 0% -> 4%
where the time goes in v4:
time: 130 us; the launch traced here: 129 us
  waiting for transfers between devices  49.6 us (38%)
  starting transfers between devices  35.9 us (28%)
  blocking collectives  31.1 us (24%)
  Pallas kernels  7.7 us (6%)
  other arithmetic  1.89 us (1%)
  local copies, waits for them, and re-layouts  1.85 us (1%)
    all_gather x1, blocking collectives, local(): lax.all_gather(tokens.T, ('y', 'c'), axis=0).reshape(ny, 2, feats, rows)  31.1 us
    ppermute x4, waiting for transfers between devices, halve(): arrived = lax.ppermute(total[half:].astype(BF16), axis, pairs)  29.5 us
    all_to_all x1, starting transfers between devices, local(): pieces = lax.all_to_all(wpart, ('zh', 'xh'), 0, 0, tiled=True)  12.2 us
    ppermute x1, waiting for transfers between devices, local(): mine = lax.ppermute(half, 'xl', PAIR)  10.5 us
    ppermute x4, starting transfers between devices, halve(): arrived = lax.ppermute(total[half:].astype(BF16), axis, pairs)  10.3 us
    ppermute x1, waiting for transfers between devices, local(): pair_grad = lax.ppermute(pre_grad, 'zl', PAIR)  5.71 us
    pallas_call x1, Pallas kernels, local(): pl.pallas_call(hidden_kernel, out_shape=(jax.ShapeDtypeStruct((d, rows),...  5 us
    ppermute x1, waiting for transfers between devices, local(): tmine = lax.ppermute(forth, 'zl', PAIR)  3.93 us
  transfers between devices with their start and end apart: 11, of which 7 were waited for; matrix products, arithmetic and copies ran while one was open for 1% of the time, Pallas kernels for 4%

profile of v4, /device:TPU:1, one launch (start us, length us, event | category | flops | bytes accessed | tf_op | source)
XLA Modules:
  0.0 128.9 jit_solution(14258173326454638606)
XLA Ops:
  0.6 31.1 %all-gather = bf16[1536,256]{1,0:T(8,128)(2,1)S(1)} all-gather(bf16[96,256]{1,0:T(8,128)(2,1)} %bitcast.25), channel_id=2, replica_groups=mesh['zh'=4,'zl'=2,'xh'=4,'y'=8,'xl'=2,'c'=2] {'y','c'}, dimensions={0}, use_global_device_ids=true | all-gather | bytes 835584 | tf_op jit(solution)/shard_map/all_gather | solution.py:99
  31.8 2.1 %collective-permute-start = (bf16[8,96,256]{2,1,0:T(8,128)(2,1)S(1)}, bf16[8,96,256]{2,1,0:T(8,128)(2,1)S(1)}, u32[]{:S(2)}, u32[]{:S(2)}) collective-permute-start(bf16[8,96,256]{2,1,0:T(8,128)(2,1)S(1)} %fusion.2), channel_id=1, source_target_pairs={{0,2},{2,0},{1,3},{3,1},{4,6},{6,4},{5,7},{7,5},{8,10},{10,8},{9,1... | collective-permute-start | bytes 1179656 | tf_op jit(solution)/shard_map/ppermute | solution.py:101
  33.9 10.5 %collective-permute-done.mine_ref = bf16[8,96,256]{2,1,0:T(8,128)(2,1)S(1)} collective-permute-done((bf16[8,96,256]{2,1,0:T(8,128)(2,1)S(1)}, bf16[8,96,256]{2,1,0:T(8,128)(2,1)S(1)}, u32[]{:S(2)}, u32[]{:S(2)}) %collective-permute-start) | collective-permute-done | bytes 393248 | tf_op jit(solution)/shard_map/ppermute | solution.py:101
  44.4 2.9 %collective-permute-start.1 = (bf16[8,96,256]{2,1,0:T(8,128)(2,1)S(1)}, bf16[8,96,256]{2,1,0:T(8,128)(2,1)S(1)}, u32[]{:S(2)}, u32[]{:S(2)}) collective-permute-start(bf16[8,96,256]{2,1,0:T(8,128)(2,1)S(1)} %collective-permute-done.mine_ref), channel_id=1, source_target_pairs={{0,1},{1,0},{2,3},{3,2},{4,5},{5,4},{6,7},{7,6},{8,9},{9,8},{10,11... | collective-permute-start | bytes 1179656 | tf_op jit(solution)/shard_map/ppermute | solution.py:102
  47.3 1.9 %collective-permute-start.2 = (bf16[2,4,96,256]{3,2,1,0:T(8,128)(2,1)S(1)}, bf16[2,4,96,256]{3,2,1,0:T(8,128)(2,1)S(1)}, u32[]{:S(2)}, u32[]{:S(2)}) collective-permute-start(bf16[2,4,96,256]{3,2,1,0:T(8,128)(2,1)S(1)} %pad_maximum_fusion), channel_id=1, source_target_pairs={{0,128},{128,0},{1,129},{129,1},{2,130},{130,2},{3,131},{131,3},{4... | collective-permute-start | bytes 1179656 | tf_op jit(solution)/shard_map/ppermute | solution.py:106
  49.3 1.7 %copy-done = bf16[3072,384]{1,0:T(8,128)(2,1)S(1)} copy-done((bf16[3072,384]{1,0:T(8,128)(2,1)S(1)}, bf16[3072,384]{1,0:T(8,128)(2,1)}, u32[]{:S(2)}) %copy-start) | copy-done | bytes 2359320
  51.0 5.0 %shard_map.50 = (bf16[3072,256]{1,0:T(8,128)(2,1)S(1)}, bf16[256,384]{1,0:T(8,128)(2,1)S(1)}, f32[16,96,256]{2,1,0:T(8,128)S(1)}, bf16[16,96,256]{2,1,0:T(8,128)(2,1)S(1)}) custom-call(s32[4]{0:T(128)S(1)} %pad_add_fusion.at_ref, bf16[8,2,96,256]{3,2,1,0:T(8,128)(2,1)S(1)} %bitcast.22, bf16[8,96,256]{2,1,0:T(8,128)(2,1)S(1)} %collective-permute-done.mine_ref, ...), custom_call_target="tpu_custom_call" | custom-call | flops 1207959552 | bytes 8388608 | tf_op jit(solution)/shard_map/pallas_call | solution.py:107
  56.0 3.9 %collective-permute-done.2.tmine_ref = bf16[2,4,96,256]{3,2,1,0:T(8,128)(2,1)S(1)} collective-permute-done((bf16[2,4,96,256]{3,2,1,0:T(8,128)(2,1)S(1)}, bf16[2,4,96,256]{3,2,1,0:T(8,128)(2,1)S(1)}, u32[]{:S(2)}, u32[]{:S(2)}) %collective-permute-start.2) | collective-permute-done | bytes 393248 | tf_op jit(solution)/shard_map/ppermute | solution.py:106
  59.9 2.7 %collective-permute-start.3 = (bf16[16,96,256]{2,1,0:T(8,128)(2,1)S(1)}, bf16[16,96,256]{2,1,0:T(8,128)(2,1)S(1)}, u32[]{:S(2)}, u32[]{:S(2)}) collective-permute-start(bf16[16,96,256]{2,1,0:T(8,128)(2,1)S(1)} %get-tuple-element.14), channel_id=1, source_target_pairs={{0,1},{1,0},{2,3},{3,2},{4,5},{5,4},{6,7},{7,6},{8,9},{9,8},{10,11... | collective-permute-start | bytes 2359304 | tf_op jit(solution)/shard_map/ppermute | solution.py:127
  62.6 1.9 %collective-permute-start.4 = (bf16[2,4,96,256]{3,2,1,0:T(8,128)(2,1)S(1)}, bf16[2,4,96,256]{3,2,1,0:T(8,128)(2,1)S(1)}, u32[]{:S(2)}, u32[]{:S(2)}) collective-permute-start(bf16[2,4,96,256]{3,2,1,0:T(8,128)(2,1)S(1)} %collective-permute-done.2.tmine_ref), channel_id=1, source_target_pairs={{0,1},{1,0},{2,3},{3,2},{4,5},{5,4},{6,7},{7,6},{8,9},{9,8},{10,11... | collective-permute-start | bytes 1179656 | tf_op jit(solution)/shard_map/ppermute | solution.py:126
  64.6 1.9 %collective-permute-start.9 = (bf16[256,384]{1,0:T(8,128)(2,1)S(1)}, bf16[256,384]{1,0:T(8,128)(2,1)S(1)}, u32[]{:S(2)}, u32[]{:S(2)}) collective-permute-start(bf16[256,384]{1,0:T(8,128)(2,1)S(1)} %get-tuple-element.19.pg_ref), channel_id=1, source_target_pairs={{0,128},{128,0},{1,129},{129,1},{2,130},{130,2},{3,131},{131,3},{4... | collective-permute-start | bytes 589832 | tf_op jit(solution)/shard_map/ppermute | solution.py:125
  66.7 5.7 %collective-permute-done.9.pgpair_ref = bf16[256,384]{1,0:T(8,128)(2,1)S(1)} collective-permute-done((bf16[256,384]{1,0:T(8,128)(2,1)S(1)}, bf16[256,384]{1,0:T(8,128)(2,1)S(1)}, u32[]{:S(2)}, u32[]{:S(2)}) %collective-permute-start.9) | collective-permute-done | bytes 196640 | tf_op jit(solution)/shard_map/ppermute | solution.py:125
  72.4 2.7 %shard_map.51 = bf16[16,96,384]{2,1,0:T(8,128)(2,1)} custom-call(s32[4]{0:T(128)S(1)} %pad_add_fusion.at_ref, bf16[3072,256]{1,0:T(8,128)(2,1)S(1)} %get-tuple-element.17.whole, bf16[2,4,96,256]{3,2,1,0:T(8,128)(2,1)S(1)} %collective-permute-done.2.tmine_ref, bf16[2,4,96,256]{3,2,1,0:T(8,128)(2,1)S(1)} %collective-permute-done.4.tother_ref, ...), custom_call_target="tpu_custom_call" | custom-call | flops 603979776 | bytes 4194304 | tf_op jit(solution)/shard_map/pallas_call | solution.py:129
  75.1 12.2 %all-to-all-start = ((bf16[16,96,384]{2,1,0:T(8,128)(2,1)}), bf16[16,96,384]{2,1,0:T(8,128)(2,1)S(1)}, u32[]{:S(2)}, u32[]{:S(2)}) async-start(bf16[16,96,384]{2,1,0:T(8,128)(2,1)} %shard_map.51), calls=%async_computation | async-start | bytes 2359296 | tf_op jit(solution)/shard_map/all_to_all | solution.py:140
  87.4 1.9 %collective-permute-start.5 = (bf16[8,96,256]{2,1,0:T(8,128)(2,1)S(1)}, bf16[8,96,256]{2,1,0:T(8,128)(2,1)S(1)}, u32[]{:S(2)}, u32[]{:S(2)}) collective-permute-start(bf16[8,96,256]{2,1,0:T(8,128)(2,1)S(1)} %slice.55), channel_id=1, source_target_pairs={{0,4},{4,0},{8,12},{12,8},{16,20},{20,16},{24,28},{28,24},{1,5},{5... | collective-permute-start | bytes 1179656 | tf_op jit(solution)/shard_map/ppermute | solution.py:83
  89.3 8.9 %collective-permute-done.5 = bf16[8,96,256]{2,1,0:T(8,128)(2,1)S(1)} collective-permute-done((bf16[8,96,256]{2,1,0:T(8,128)(2,1)S(1)}, bf16[8,96,256]{2,1,0:T(8,128)(2,1)S(1)}, u32[]{:S(2)}, u32[]{:S(2)}) %collective-permute-start.5) | collective-permute-done | bytes 393248 | tf_op jit(solution)/shard_map/ppermute | solution.py:83
  98.4 1.9 %collective-permute-start.6 = (bf16[4,96,256]{2,1,0:T(8,128)(2,1)S(1)}, bf16[4,96,256]{2,1,0:T(8,128)(2,1)S(1)}, u32[]{:S(2)}, u32[]{:S(2)}) collective-permute-start(bf16[4,96,256]{2,1,0:T(8,128)(2,1)S(1)} %slice.56), channel_id=1, source_target_pairs={{0,8},{4,12},{8,0},{12,4},{16,24},{20,28},{24,16},{28,20},{1,9},{5... | collective-permute-start | bytes 589832 | tf_op jit(solution)/shard_map/ppermute | solution.py:83
  100.3 11.2 %collective-permute-done.6 = bf16[4,96,256]{2,1,0:T(8,128)(2,1)S(1)} collective-permute-done((bf16[4,96,256]{2,1,0:T(8,128)(2,1)S(1)}, bf16[4,96,256]{2,1,0:T(8,128)(2,1)S(1)}, u32[]{:S(2)}, u32[]{:S(2)}) %collective-permute-start.6) | collective-permute-done | bytes 196640 | tf_op jit(solution)/shard_map/ppermute | solution.py:83
  111.6 4.3 %collective-permute-start.7 = (bf16[2,96,256]{2,1,0:T(8,128)(2,1)S(1)}, bf16[2,96,256]{2,1,0:T(8,128)(2,1)S(1)}, u32[]{:S(2)}, u32[]{:S(2)}) collective-permute-start(bf16[2,96,256]{2,1,0:T(8,128)(2,1)S(1)} %slice.57), channel_id=1, source_target_pairs={{0,16},{4,20},{8,24},{12,28},{16,0},{20,4},{24,8},{28,12},{1,17},{... | collective-permute-start | bytes 294920 | tf_op jit(solution)/shard_map/ppermute | solution.py:83
  115.8 6.8 %collective-permute-done.7 = bf16[2,96,256]{2,1,0:T(8,128)(2,1)S(1)} collective-permute-done((bf16[2,96,256]{2,1,0:T(8,128)(2,1)S(1)}, bf16[2,96,256]{2,1,0:T(8,128)(2,1)S(1)}, u32[]{:S(2)}, u32[]{:S(2)}) %collective-permute-start.7) | collective-permute-done | bytes 98336 | tf_op jit(solution)/shard_map/ppermute | solution.py:83
  122.6 2.2 %collective-permute-start.8 = (bf16[1,96,256]{2,1,0:T(8,128)(2,1)S(1)}, bf16[1,96,256]{2,1,0:T(8,128)(2,1)S(1)}, u32[]{:S(2)}, u32[]{:S(2)}) collective-permute-start(bf16[1,96,256]{2,1,0:T(8,128)(2,1)S(1)} %slice.58), channel_id=1, source_target_pairs={{0,2},{2,0},{1,3},{3,1},{4,6},{6,4},{5,7},{7,5},{8,10},{10,8},{9,1... | collective-permute-start | bytes 147464 | tf_op jit(solution)/shard_map/ppermute | solution.py:83
  124.9 2.6 %collective-permute-done.8 = bf16[1,96,256]{2,1,0:T(8,128)(2,1)S(1)} collective-permute-done((bf16[1,96,256]{2,1,0:T(8,128)(2,1)S(1)}, bf16[1,96,256]{2,1,0:T(8,128)(2,1)S(1)}, u32[]{:S(2)}, u32[]{:S(2)}) %collective-permute-start.8) | collective-permute-done | bytes 49184 | tf_op jit(solution)/shard_map/ppermute | solution.py:83
  127.5 0.6 fusion.1
  128.1 0.8 reduce_sum.12
  (21 shorter events, 0.7 us)
Async XLA Ops:
  31.7 17.6 %copy-start.1 = (bf16[256,384]{1,0:T(8,128)(2,1)S(1)}, bf16[256,384]{1,0:T(8,128)(2,1)}, u32[]{:S(2)}) copy-start(bf16[256,384]{1,0:T(8,128)(2,1)} %g_ref.1) | copy-start | bytes 589828
  31.8 12.6 %collective-permute-start = (bf16[8,96,256]{2,1,0:T(8,128)(2,1)S(1)}, bf16[8,96,256]{2,1,0:T(8,128)(2,1)S(1)}, u32[]{:S(2)}, u32[]{:S(2)}) collective-permute-start(bf16[8,96,256]{2,1,0:T(8,128)(2,1)S(1)} %fusion.2), channel_id=1, source_target_pairs={{0,2},{2,0},{1,3},{3,1},{4,6},{6,4},{5,7},{7,5},{8,10},{10,8},{9,1... | collective-permute-start | bytes 1179656 | tf_op jit(solution)/shard_map/ppermute | solution.py:101
  44.4 4.9 %collective-permute-start.1 = (bf16[8,96,256]{2,1,0:T(8,128)(2,1)S(1)}, bf16[8,96,256]{2,1,0:T(8,128)(2,1)S(1)}, u32[]{:S(2)}, u32[]{:S(2)}) collective-permute-start(bf16[8,96,256]{2,1,0:T(8,128)(2,1)S(1)} %collective-permute-done.mine_ref), channel_id=1, source_target_pairs={{0,1},{1,0},{2,3},{3,2},{4,5},{5,4},{6,7},{7,6},{8,9},{9,8},{10,11... | collective-permute-start | bytes 1179656 | tf_op jit(solution)/shard_map/ppermute | solution.py:102
  47.3 12.6 %collective-permute-start.2 = (bf16[2,4,96,256]{3,2,1,0:T(8,128)(2,1)S(1)}, bf16[2,4,96,256]{3,2,1,0:T(8,128)(2,1)S(1)}, u32[]{:S(2)}, u32[]{:S(2)}) collective-permute-start(bf16[2,4,96,256]{3,2,1,0:T(8,128)(2,1)S(1)} %pad_maximum_fusion), channel_id=1, source_target_pairs={{0,128},{128,0},{1,129},{129,1},{2,130},{130,2},{3,131},{131,3},{4... | collective-permute-start | bytes 1179656 | tf_op jit(solution)/shard_map/ppermute | solution.py:106
  49.3 1.7 %copy-start = (bf16[3072,384]{1,0:T(8,128)(2,1)S(1)}, bf16[3072,384]{1,0:T(8,128)(2,1)}, u32[]{:S(2)}) copy-start(bf16[3072,384]{1,0:T(8,128)(2,1)} %w_ref.1) | copy-start | bytes 7077892
  59.9 6.6 %collective-permute-start.3 = (bf16[16,96,256]{2,1,0:T(8,128)(2,1)S(1)}, bf16[16,96,256]{2,1,0:T(8,128)(2,1)S(1)}, u32[]{:S(2)}, u32[]{:S(2)}) collective-permute-start(bf16[16,96,256]{2,1,0:T(8,128)(2,1)S(1)} %get-tuple-element.14), channel_id=1, source_target_pairs={{0,1},{1,0},{2,3},{3,2},{4,5},{5,4},{6,7},{7,6},{8,9},{9,8},{10,11... | collective-permute-start | bytes 2359304 | tf_op jit(solution)/shard_map/ppermute | solution.py:127
  62.6 4.1 %collective-permute-start.4 = (bf16[2,4,96,256]{3,2,1,0:T(8,128)(2,1)S(1)}, bf16[2,4,96,256]{3,2,1,0:T(8,128)(2,1)S(1)}, u32[]{:S(2)}, u32[]{:S(2)}) collective-permute-start(bf16[2,4,96,256]{3,2,1,0:T(8,128)(2,1)S(1)} %collective-permute-done.2.tmine_ref), channel_id=1, source_target_pairs={{0,1},{1,0},{2,3},{3,2},{4,5},{5,4},{6,7},{7,6},{8,9},{9,8},{10,11... | collective-permute-start | bytes 1179656 | tf_op jit(solution)/shard_map/ppermute | solution.py:126
  64.6 7.9 %collective-permute-start.9 = (bf16[256,384]{1,0:T(8,128)(2,1)S(1)}, bf16[256,384]{1,0:T(8,128)(2,1)S(1)}, u32[]{:S(2)}, u32[]{:S(2)}) collective-permute-start(bf16[256,384]{1,0:T(8,128)(2,1)S(1)} %get-tuple-element.19.pg_ref), channel_id=1, source_target_pairs={{0,128},{128,0},{1,129},{129,1},{2,130},{130,2},{3,131},{131,3},{4... | collective-permute-start | bytes 589832 | tf_op jit(solution)/shard_map/ppermute | solution.py:125
  75.1 53.0 %all-to-all-start = ((bf16[16,96,384]{2,1,0:T(8,128)(2,1)}), bf16[16,96,384]{2,1,0:T(8,128)(2,1)S(1)}, u32[]{:S(2)}, u32[]{:S(2)}) async-start(bf16[16,96,384]{2,1,0:T(8,128)(2,1)} %shard_map.51), calls=%async_computation | async-start | bytes 2359296 | tf_op jit(solution)/shard_map/all_to_all | solution.py:140
  87.4 10.9 %collective-permute-start.5 = (bf16[8,96,256]{2,1,0:T(8,128)(2,1)S(1)}, bf16[8,96,256]{2,1,0:T(8,128)(2,1)S(1)}, u32[]{:S(2)}, u32[]{:S(2)}) collective-permute-start(bf16[8,96,256]{2,1,0:T(8,128)(2,1)S(1)} %slice.55), channel_id=1, source_target_pairs={{0,4},{4,0},{8,12},{12,8},{16,20},{20,16},{24,28},{28,24},{1,5},{5... | collective-permute-start | bytes 1179656 | tf_op jit(solution)/shard_map/ppermute | solution.py:83
  98.4 13.1 %collective-permute-start.6 = (bf16[4,96,256]{2,1,0:T(8,128)(2,1)S(1)}, bf16[4,96,256]{2,1,0:T(8,128)(2,1)S(1)}, u32[]{:S(2)}, u32[]{:S(2)}) collective-permute-start(bf16[4,96,256]{2,1,0:T(8,128)(2,1)S(1)} %slice.56), channel_id=1, source_target_pairs={{0,8},{4,12},{8,0},{12,4},{16,24},{20,28},{24,16},{28,20},{1,9},{5... | collective-permute-start | bytes 589832 | tf_op jit(solution)/shard_map/ppermute | solution.py:83
  111.6 11.0 %collective-permute-start.7 = (bf16[2,96,256]{2,1,0:T(8,128)(2,1)S(1)}, bf16[2,96,256]{2,1,0:T(8,128)(2,1)S(1)}, u32[]{:S(2)}, u32[]{:S(2)}) collective-permute-start(bf16[2,96,256]{2,1,0:T(8,128)(2,1)S(1)} %slice.57), channel_id=1, source_target_pairs={{0,16},{4,20},{8,24},{12,28},{16,0},{20,4},{24,8},{28,12},{1,17},{... | collective-permute-start | bytes 294920 | tf_op jit(solution)/shard_map/ppermute | solution.py:83
  122.6 4.8 %collective-permute-start.8 = (bf16[1,96,256]{2,1,0:T(8,128)(2,1)S(1)}, bf16[1,96,256]{2,1,0:T(8,128)(2,1)S(1)}, u32[]{:S(2)}, u32[]{:S(2)}) collective-permute-start(bf16[1,96,256]{2,1,0:T(8,128)(2,1)S(1)} %slice.58), channel_id=1, source_target_pairs={{0,2},{2,0},{1,3},{3,1},{4,6},{6,4},{5,7},{7,5},{8,10},{10,8},{9,1... | collective-permute-start | bytes 147464 | tf_op jit(solution)/shard_map/ppermute | solution.py:83

commit v5 on v4

v5 whole, which is shorter than its diff:
```python
import jax
import jax.numpy as jnp
from jax import lax
from jax.experimental import pallas as pl
from jax.experimental.pallas import tpu as pltpu
from jax.sharding import Mesh, PartitionSpec as P

DP = ("zh", "zl", "xh")
MP = ("y", "xl", "c")
F32 = jnp.float32
BF16 = jnp.bfloat16
VMEM = pl.BlockSpec(memory_space=pltpu.VMEM)
SMEM = pl.BlockSpec(memory_space=pltpu.SMEM)
PAIR = [(0, 1), (1, 0)]


def gelu_slope(pre):
    coef = 0.7978845608028654
    inner = coef * (pre + 0.044715 * pre * pre * pre)
    tval = jnp.tanh(inner)
    return 0.5 * (1.0 + tval) + 0.5 * pre * (1.0 - tval * tval) * coef * (
        1.0 + 3.0 * 0.044715 * pre * pre
    )


def pre_kernel(at_ref, tok_ref, w_ref, pre_ref, w_half):
    pre_ref[...] = half_pre(at_ref[1], tok_ref, w_ref, w_half)


def half_pre(x, tok_ref, w_ref, w_half):
    ny, _, feats, rows = tok_ref.shape
    for y in range(ny):
        start = pl.multiple_of((4 * y + 2 * x) * feats, 2 * feats)
        w_half[pl.ds(2 * y * feats, 2 * feats), :] = w_ref[pl.ds(start, 2 * feats), :]
    return lax.dot_general(
        tok_ref[...].reshape(2 * ny * feats, rows),
        w_half[...],
        (((0,), (0,)), ((), ())),
        preferred_element_type=F32,
    )


def hidden_kernel(
    at_ref, mine_ref, other_ref, w_ref, g_ref, pre_ref, rest, pg_ref, keep_ref, send_ref, w_half
):
    y_own, xl, core = at_ref[0], at_ref[1], at_ref[2]
    ny, feats, _ = mine_ref.shape
    bits = ny.bit_length() - 1
    for y in range(ny):
        rest[y, core] = mine_ref[y]
        rest[y, 1 - core] = other_ref[y]
    pre = pre_ref[...] + half_pre(1 - xl, rest, w_ref, w_half)
    pg = (g_ref[...].astype(F32) * gelu_slope(pre)).astype(BF16)
    pg_ref[...] = pg
    for r in range(ny):
        at = sum((r >> k & 1) << (bits - 1 - k) for k in range(bits))
        start = lax.bitwise_xor(y_own, jnp.int32(r)) * (4 * feats)
        block = lax.dot_general(
            w_ref[pl.ds(pl.multiple_of(start, 4 * feats), 4 * feats), :],
            pg,
            (((1,), (1,)), ((), ())),
            preferred_element_type=F32,
        )
        for c in range(2):

            @pl.when(core == c)
            def _():
                for x in range(2):
                    to = lax.bitwise_xor(xl, jnp.int32(x)) * ny + at
                    for ref, b in ((keep_ref, 2 * x + c), (send_ref, 2 * x + 1 - c)):
                        part = block[b * feats : (b + 1) * feats]
                        ref[to] = part.astype(ref.dtype)


def weight_kernel(at_ref, own, rest, t1_ref, t2_ref, tother_ref, pg_ref, pgpair_ref, out_ref):
    xl, core, zl = at_ref[1], at_ref[2], at_ref[3]
    nh = t1_ref.shape[0]
    for i in range(nh):
        for x, (tok, mine) in enumerate(((own, t1_ref), (rest, t2_ref))):
            for c, pair in ((core, mine[i]), (1 - core, tother_ref[x * nh + i])):
                total = jnp.dot(
                    tok[2 * i + zl, c], pg_ref[...], preferred_element_type=F32
                ) + jnp.dot(pair, pgpair_ref[...], preferred_element_type=F32)
                out_ref[4 * i + 2 * lax.bitwise_xor(xl, jnp.int32(x)) + c] = total.astype(BF16)


def halve(total, axis, pairs):
    half = total.shape[0] // 2
    arrived = lax.ppermute(total[half:].astype(BF16), axis, pairs)
    return total[:half] + arrived.astype(F32)


def make_local(nz, nx, ny):
    nh = nz // 2

    def local(tokens, w_in, hidden_grad):
        rows, feats = tokens.shape
        d, hidden = w_in.shape
        core, zl = lax.axis_index("c"), lax.axis_index("zl")
        at = jnp.stack([lax.axis_index("y"), lax.axis_index("xl"), core, zl]).astype(jnp.int32)

        def pick(array, index, axis):
            return lax.dynamic_index_in_dim(array, index, axis, keepdims=False)

        own = lax.all_gather(tokens.T, ("y", "c"), axis=0).reshape(ny, 2, feats, rows)
        half = pick(own, core, 1)
        mine = lax.ppermute(half, "xl", PAIR)
        t1 = lax.ppermute(pick(half.reshape(nh, 2, feats, rows), 1 - zl, 1), "zl", PAIR)
        pre = pl.pallas_call(
            pre_kernel,
            out_shape=jax.ShapeDtypeStruct((rows, hidden), F32),
            in_specs=[SMEM, VMEM, VMEM],
            out_specs=VMEM,
            scratch_shapes=[pltpu.VMEM((d // 2, hidden), BF16)],
            compiler_params=pltpu.CompilerParams(vmem_limit_bytes=8 << 20),
            cost_estimate=pl.CostEstimate(
                flops=d * rows * hidden, bytes_accessed=4 << 20, transcendentals=0
            ),
        )(at, own, w_in)
        mine, t1, pre = lax.optimization_barrier((mine, t1, pre))
        other = lax.ppermute(mine, "c", PAIR)
        t2 = lax.ppermute(pick(mine.reshape(nh, 2, feats, rows), 1 - zl, 1), "zl", PAIR)
        rest, pre_grad, keep, send = pl.pallas_call(
            hidden_kernel,
            out_shape=(
                jax.ShapeDtypeStruct((ny, 2, feats, rows), BF16),
                jax.ShapeDtypeStruct((rows, hidden), BF16),
                jax.ShapeDtypeStruct((2 * ny, feats, rows), F32),
                jax.ShapeDtypeStruct((2 * ny, feats, rows), BF16),
            ),
            in_specs=[SMEM, VMEM, VMEM, VMEM, VMEM, VMEM],
            out_specs=(VMEM, VMEM, VMEM, VMEM),
            scratch_shapes=[pltpu.VMEM((d // 2, hidden), BF16)],
            compiler_params=pltpu.CompilerParams(vmem_limit_bytes=8 << 20),
            cost_estimate=pl.CostEstimate(
                flops=3 * d * rows * hidden,
                bytes_accessed=8 << 20,
                transcendentals=rows * hidden,
            ),
        )(at, mine, other, w_in, hidden_grad, pre)
        pre_grad, send, t1, t2 = lax.optimization_barrier((pre_grad, send, t1, t2))
        pair_grad = lax.ppermute(pre_grad, "zl", PAIR)
        swapped = lax.ppermute(jnp.concatenate([send, t1, t2]), "c", PAIR)
        total = keep + swapped[: 2 * ny].astype(F32)
        total, tother = lax.optimization_barrier((total, swapped[2 * ny :]))
        wpart = pl.pallas_call(
            weight_kernel,
            out_shape=jax.ShapeDtypeStruct((4 * nh, feats, hidden), BF16),
            in_specs=[SMEM] + [VMEM] * 7,
            out_specs=VMEM,
            compiler_params=pltpu.CompilerParams(vmem_limit_bytes=4 << 20),
            cost_estimate=pl.CostEstimate(
                flops=2 * d * rows * hidden, bytes_accessed=4 << 20, transcendentals=0
            ),
        )(at, own, rest, t1, t2, tother, pre_grad, pair_grad)
        pieces = lax.all_to_all(wpart.reshape(nh, -1, hidden), "zh", 0, 0, tiled=True)
        steps = [("xl", PAIR)]
        bit = 1
        while bit < ny:
            steps.append(("y", [(i, i ^ bit) for i in range(ny)]))
            bit *= 2
        for n, (axis, pairs) in enumerate(steps):
            if n == len(steps) - 1:
                total, pieces = lax.optimization_barrier((total, pieces))
            total = halve(total, axis, pairs)
        sums = jnp.sum(pieces.astype(F32), axis=0).astype(BF16)
        pieces = lax.all_to_all(sums.reshape(nx, -1, hidden), "xh", 0, 0, tiled=True)
        weight_sum = jnp.sum(pieces.astype(F32), axis=0)
        return (total[0].astype(BF16).T, weight_sum.astype(BF16))

    return local


def solution(mesh, sizes=(8, 4, 8)):
    nz, nx, ny = sizes
    split = Mesh(mesh.devices.reshape(nz // 2, 2, nx, ny, 2, 2), DP + MP)
    return jax.shard_map(
        make_local(*sizes),
        mesh=split,
        in_specs=(P(DP, MP), P(None, MP), P(DP, MP)),
        out_specs=(P(DP, MP), P(DP, MP)),
        check_vma=False,
    )
```

time: 130 us -> 128 us (0.985)
  the two profiles are of different devices: /device:TPU:1 before, /device:TPU:132 now
where the time goes in v5:
time: 128 us; the launch traced here: 127 us
  starting transfers between devices  47.6 us (37%)
  waiting for transfers between devices  43.9 us (34%)
  blocking collectives  20.9 us (16%)
  Pallas kernels  8.8 us (7%)
  other arithmetic  3.75 us (3%)
  local copies, waits for them, and re-layouts  1.64 us (1%)
    ppermute x4, waiting for transfers between devices, halve(): arrived = lax.ppermute(total[half:].astype(BF16), axis, pairs)  26 us
    all_gather x1, blocking collectives, local(): lax.all_gather(tokens.T, ('y', 'c'), axis=0).reshape(ny, 2, feats, rows)  20.9 us
    all_to_all x1, starting transfers between devices, local(): lax.all_to_all(wpart.reshape(nh, -1, hidden), 'zh', 0, 0, tiled=True)  14.9 us
    ppermute x4, starting transfers between devices, halve(): arrived = lax.ppermute(total[half:].astype(BF16), axis, pairs)  12.2 us
    all_to_all x1, starting transfers between devices, local(): lax.all_to_all(sums.reshape(nx, -1, hidden), 'xh', 0, 0, tiled=True)  7.25 us
    ppermute x1, waiting for transfers between devices, local(): pair_grad = lax.ppermute(pre_grad, 'zl', PAIR)  6.14 us
    ppermute x1, waiting for transfers between devices, local(): lax.ppermute(pick(half.reshape(nh, 2, feats, rows), 1 - zl, 1), 'zl', PAIR)  5.9 us
    pallas_call x1, Pallas kernels, local(): pl.pallas_call(hidden_kernel, out_shape=(jax.ShapeDtypeStruct((ny, 2, fea...  4.46 us
  transfers between devices with their start and end apart: 12, of which 10 were waited for; matrix products, arithmetic and copies ran while one was open for 2% of the time, Pallas kernels for 4%

profile of v5, /device:TPU:132, one launch (start us, length us, event | category | flops | bytes accessed | tf_op | source)
XLA Modules:
  0.0 127.4 jit_solution(7676453978029834059)
XLA Ops:
  0.6 20.9 %all-gather = bf16[1536,256]{1,0:T(8,128)(2,1)S(1)} all-gather(bf16[96,256]{1,0:T(8,128)(2,1)} %bitcast.28), channel_id=2, replica_groups=mesh['zh'=4,'zl'=2,'xh'=4,'y'=8,'xl'=2,'c'=2] {'y','c'}, dimensions={0}, use_global_device_ids=true | all-gather | bytes 835584 | tf_op jit(solution)/shard_map/all_gather | solution.py:105
  22.3 3.4 %collective-permute-start = (bf16[8,96,256]{2,1,0:T(8,128)(2,1)}, bf16[8,96,256]{2,1,0:T(8,128)(2,1)S(1)}, u32[]{:S(2)}, u32[]{:S(2)}) collective-permute-start(bf16[8,96,256]{2,1,0:T(8,128)(2,1)} %fusion.1), channel_id=1, source_target_pairs={{0,2},{2,0},{1,3},{3,1},{4,6},{6,4},{5,7},{7,5},{8,10},{10,8},{9,1... | collective-permute-start | bytes 1179656 | tf_op jit(solution)/shard_map/ppermute | solution.py:107
  26.5 1.9 %collective-permute-start.1 = (bf16[4,96,256]{2,1,0:T(8,128)(2,1)}, bf16[4,96,256]{2,1,0:T(8,128)(2,1)}, u32[]{:S(2)}, u32[]{:S(2)}) collective-permute-start(bf16[4,96,256]{2,1,0:T(8,128)(2,1)} %dynamic-slice_bitcast_fusion.1), channel_id=1, source_target_pairs={{0,128},{128,0},{1,129},{129,1},{2,130},{130,2},{3,131},{131,3},{4... | collective-permute-start | bytes 589832 | tf_op jit(solution)/shard_map/ppermute | solution.py:108
  28.5 1.2 shard_map.50.pre_ref
  29.6 5.9 %collective-permute-done.1.t1_ref = bf16[4,96,256]{2,1,0:T(8,128)(2,1)} collective-permute-done((bf16[4,96,256]{2,1,0:T(8,128)(2,1)}, bf16[4,96,256]{2,1,0:T(8,128)(2,1)}, u32[]{:S(2)}, u32[]{:S(2)}) %collective-permute-start.1) | collective-permute-done | bytes 196640 | tf_op jit(solution)/shard_map/ppermute | solution.py:108
  35.8 1.9 %collective-permute-start.2 = (bf16[8,96,256]{2,1,0:T(8,128)(2,1)S(1)}, bf16[8,96,256]{2,1,0:T(8,128)(2,1)S(1)}, u32[]{:S(2)}, u32[]{:S(2)}) collective-permute-start(bf16[8,96,256]{2,1,0:T(8,128)(2,1)S(1)} %collective-permute-done.mine_ref), channel_id=1, source_target_pairs={{0,1},{1,0},{2,3},{3,2},{4,5},{5,4},{6,7},{7,6},{8,9},{9,8},{10,11... | collective-permute-start | bytes 1179656 | tf_op jit(solution)/shard_map/ppermute | solution.py:121
  37.7 2.0 %collective-permute-start.3 = (bf16[4,96,256]{2,1,0:T(8,128)(2,1)S(1)}, bf16[4,96,256]{2,1,0:T(8,128)(2,1)S(1)}, u32[]{:S(2)}, u32[]{:S(2)}) collective-permute-start(bf16[4,96,256]{2,1,0:T(8,128)(2,1)S(1)} %dynamic-slice_bitcast_fusion), channel_id=1, source_target_pairs={{0,128},{128,0},{1,129},{129,1},{2,130},{130,2},{3,131},{131,3},{4... | collective-permute-start | bytes 589832 | tf_op jit(solution)/shard_map/ppermute | solution.py:122
  39.7 4.5 %shard_map.51 = (bf16[8,2,96,256]{3,2,1,0:T(8,128)(2,1)S(1)}, bf16[256,384]{1,0:T(8,128)(2,1)S(1)}, f32[16,96,256]{2,1,0:T(8,128)S(1)}, bf16[16,96,256]{2,1,0:T(8,128)(2,1)S(1)}) custom-call(s32[4]{0:T(128)S(1)} %pad_add_fusion.at_ref, bf16[8,96,256]{2,1,0:T(8,128)(2,1)S(1)} %collective-permute-done.mine_ref, ...), custom_call_target="tpu_custom_call" | custom-call | flops 905969664 | bytes 8388608 | tf_op jit(solution)/shard_map/pallas_call | solution.py:123
  44.2 2.7 %collective-permute-done.3.t2_ref = bf16[4,96,256]{2,1,0:T(8,128)(2,1)S(1)} collective-permute-done((bf16[4,96,256]{2,1,0:T(8,128)(2,1)S(1)}, bf16[4,96,256]{2,1,0:T(8,128)(2,1)S(1)}, u32[]{:S(2)}, u32[]{:S(2)}) %collective-permute-start.3) | collective-permute-done | bytes 196640 | tf_op jit(solution)/shard_map/ppermute | solution.py:122
  48.0 1.9 %collective-permute-start.4 = (bf16[24,96,256]{2,1,0:T(8,128)(2,1)S(1)}, bf16[24,96,256]{2,1,0:T(8,128)(2,1)S(1)}, u32[]{:S(2)}, u32[]{:S(2)}) collective-permute-start(bf16[24,96,256]{2,1,0:T(8,128)(2,1)S(1)} %pad_maximum_fusion), channel_id=1, source_target_pairs={{0,1},{1,0},{2,3},{3,2},{4,5},{5,4},{6,7},{7,6},{8,9},{9,8},{10,11... | collective-permute-start | bytes 3538952 | tf_op jit(solution)/shard_map/ppermute | solution.py:143
  49.9 2.2 %collective-permute-start.8 = (bf16[256,384]{1,0:T(8,128)(2,1)S(1)}, bf16[256,384]{1,0:T(8,128)(2,1)S(1)}, u32[]{:S(2)}, u32[]{:S(2)}) collective-permute-start(bf16[256,384]{1,0:T(8,128)(2,1)S(1)} %get-tuple-element.29.pg_ref), channel_id=1, source_target_pairs={{0,128},{128,0},{1,129},{129,1},{2,130},{130,2},{3,131},{131,3},{4... | collective-permute-start | bytes 589832 | tf_op jit(solution)/shard_map/ppermute | solution.py:142
  53.0 6.1 %collective-permute-done.8.pgpair_ref = bf16[256,384]{1,0:T(8,128)(2,1)S(1)} collective-permute-done((bf16[256,384]{1,0:T(8,128)(2,1)S(1)}, bf16[256,384]{1,0:T(8,128)(2,1)S(1)}, u32[]{:S(2)}, u32[]{:S(2)}) %collective-permute-start.8) | collective-permute-done | bytes 196640 | tf_op jit(solution)/shard_map/ppermute | solution.py:142
  59.1 3.2 %shard_map.52 = bf16[16,96,384]{2,1,0:T(8,128)(2,1)} custom-call(s32[4]{0:T(128)S(1)} %pad_add_fusion.at_ref, bf16[8,2,96,256]{3,2,1,0:T(8,128)(2,1)S(1)} %bitcast.25, bf16[8,2,96,256]{3,2,1,0:T(8,128)(2,1)S(1)} %get-tuple-element.27.rest, bf16[4,96,256]{2,1,0:T(8,128)(2,1)} %collective-permute-done.1.t1_ref, ...), custom_call_target="tpu_custom_call" | custom-call | flops 603979776 | bytes 4194304 | tf_op jit(solution)/shard_map/pallas_call | solution.py:146
  62.3 14.9 %all-to-all-start = ((bf16[4,384,384]{2,1,0:T(8,128)(2,1)}), bf16[4,384,384]{2,1,0:T(8,128)(2,1)S(1)}, u32[]{:S(2)}, u32[]{:S(2)}) async-start(bf16[4,384,384]{2,1,0:T(8,128)(2,1)} %bitcast.11), calls=%async_computation | async-start | bytes 2359296 | tf_op jit(solution)/shard_map/all_to_all | solution.py:156
  77.2 3.4 %collective-permute-start.5 = (bf16[8,96,256]{2,1,0:T(8,128)(2,1)S(1)}, bf16[8,96,256]{2,1,0:T(8,128)(2,1)S(1)}, u32[]{:S(2)}, u32[]{:S(2)}) collective-permute-start(bf16[8,96,256]{2,1,0:T(8,128)(2,1)S(1)} %slice.63), channel_id=1, source_target_pairs={{0,2},{2,0},{1,3},{3,1},{4,6},{6,4},{5,7},{7,5},{8,10},{10,8},{9,1... | collective-permute-start | bytes 1179656 | tf_op jit(solution)/shard_map/ppermute | solution.py:89
  80.6 8.9 %collective-permute-done.5 = bf16[8,96,256]{2,1,0:T(8,128)(2,1)S(1)} collective-permute-done((bf16[8,96,256]{2,1,0:T(8,128)(2,1)S(1)}, bf16[8,96,256]{2,1,0:T(8,128)(2,1)S(1)}, u32[]{:S(2)}, u32[]{:S(2)}) %collective-permute-start.5) | collective-permute-done | bytes 393248 | tf_op jit(solution)/shard_map/ppermute | solution.py:89
  89.7 1.9 %collective-permute-start.6 = (bf16[4,96,256]{2,1,0:T(8,128)(2,1)S(1)}, bf16[4,96,256]{2,1,0:T(8,128)(2,1)S(1)}, u32[]{:S(2)}, u32[]{:S(2)}) collective-permute-start(bf16[4,96,256]{2,1,0:T(8,128)(2,1)S(1)} %slice.64), channel_id=1, source_target_pairs={{0,4},{4,0},{8,12},{12,8},{16,20},{20,16},{24,28},{28,24},{1,5},{5... | collective-permute-start | bytes 589832 | tf_op jit(solution)/shard_map/ppermute | solution.py:89
  91.6 5.6 %collective-permute-done.6 = bf16[4,96,256]{2,1,0:T(8,128)(2,1)S(1)} collective-permute-done((bf16[4,96,256]{2,1,0:T(8,128)(2,1)S(1)}, bf16[4,96,256]{2,1,0:T(8,128)(2,1)S(1)}, u32[]{:S(2)}, u32[]{:S(2)}) %collective-permute-start.6) | collective-permute-done | bytes 196640 | tf_op jit(solution)/shard_map/ppermute | solution.py:89
  97.3 2.2 %collective-permute-start.7 = (bf16[2,96,256]{2,1,0:T(8,128)(2,1)S(1)}, bf16[2,96,256]{2,1,0:T(8,128)(2,1)S(1)}, u32[]{:S(2)}, u32[]{:S(2)}) collective-permute-start(bf16[2,96,256]{2,1,0:T(8,128)(2,1)S(1)} %slice.65), channel_id=1, source_target_pairs={{0,8},{4,12},{8,0},{12,4},{16,24},{20,28},{24,16},{28,20},{1,9},{5... | collective-permute-start | bytes 294920 | tf_op jit(solution)/shard_map/ppermute | solution.py:89
  99.5 5.7 %collective-permute-done.7 = bf16[2,96,256]{2,1,0:T(8,128)(2,1)S(1)} collective-permute-done((bf16[2,96,256]{2,1,0:T(8,128)(2,1)S(1)}, bf16[2,96,256]{2,1,0:T(8,128)(2,1)S(1)}, u32[]{:S(2)}, u32[]{:S(2)}) %collective-permute-start.7) | collective-permute-done | bytes 98336 | tf_op jit(solution)/shard_map/ppermute | solution.py:89
  105.3 2.2 %all-to-all-done = bf16[4,384,384]{2,1,0:T(8,128)(2,1)S(1)} async-done(((bf16[4,384,384]{2,1,0:T(8,128)(2,1)}), bf16[4,384,384]{2,1,0:T(8,128)(2,1)S(1)}, u32[]{:S(2)}, u32[]{:S(2)}) %all-to-all-start) | async-done | bytes 1179680 | tf_op jit(solution)/shard_map/all_to_all | solution.py:156
  108.4 7.3 %all-to-all-start.1 = ((bf16[4,96,384]{2,1,0:T(8,128)(2,1)}), bf16[4,96,384]{2,1,0:T(8,128)(2,1)S(1)}, u32[]{:S(2)}, u32[]{:S(2)}) async-start(bf16[4,96,384]{2,1,0:T(8,128)(2,1)} %bitcast.14), calls=%async_computation.1 | async-start | bytes 589824 | tf_op jit(solution)/shard_map/all_to_all | solution.py:167
  115.7 4.7 %collective-permute-start.9 = (bf16[1,96,256]{2,1,0:T(8,128)(2,1)S(1)}, bf16[1,96,256]{2,1,0:T(8,128)(2,1)S(1)}, u32[]{:S(2)}, u32[]{:S(2)}) collective-permute-start(bf16[1,96,256]{2,1,0:T(8,128)(2,1)S(1)} %slice.66), channel_id=1, source_target_pairs={{0,16},{4,20},{8,24},{12,28},{16,0},{20,4},{24,8},{28,12},{1,17},{... | collective-permute-start | bytes 147464 | tf_op jit(solution)/shard_map/ppermute | solution.py:89
  120.4 5.7 %collective-permute-done.9 = bf16[1,96,256]{2,1,0:T(8,128)(2,1)S(1)} collective-permute-done((bf16[1,96,256]{2,1,0:T(8,128)(2,1)S(1)}, bf16[1,96,256]{2,1,0:T(8,128)(2,1)S(1)}, u32[]{:S(2)}, u32[]{:S(2)}) %collective-permute-start.9) | collective-permute-done | bytes 49184 | tf_op jit(solution)/shard_map/ppermute | solution.py:89
  (26 shorter events, 6.2 us)
Async XLA Ops:
  0.6 27.8 %copy-start = (bf16[3072,384]{1,0:T(8,128)(2,1)S(1)}, bf16[3072,384]{1,0:T(8,128)(2,1)}, u32[]{:S(2)}) copy-start(bf16[3072,384]{1,0:T(8,128)(2,1)} %w_ref.3) | copy-start | bytes 7077892
  22.3 13.5 %collective-permute-start = (bf16[8,96,256]{2,1,0:T(8,128)(2,1)}, bf16[8,96,256]{2,1,0:T(8,128)(2,1)S(1)}, u32[]{:S(2)}, u32[]{:S(2)}) collective-permute-start(bf16[8,96,256]{2,1,0:T(8,128)(2,1)} %fusion.1), channel_id=1, source_target_pairs={{0,2},{2,0},{1,3},{3,1},{4,6},{6,4},{5,7},{7,5},{8,10},{10,8},{9,1... | collective-permute-start | bytes 1179656 | tf_op jit(solution)/shard_map/ppermute | solution.py:107
  26.5 9.1 %collective-permute-start.1 = (bf16[4,96,256]{2,1,0:T(8,128)(2,1)}, bf16[4,96,256]{2,1,0:T(8,128)(2,1)}, u32[]{:S(2)}, u32[]{:S(2)}) collective-permute-start(bf16[4,96,256]{2,1,0:T(8,128)(2,1)} %dynamic-slice_bitcast_fusion.1), channel_id=1, source_target_pairs={{0,128},{128,0},{1,129},{129,1},{2,130},{130,2},{3,131},{131,3},{4... | collective-permute-start | bytes 589832 | tf_op jit(solution)/shard_map/ppermute | solution.py:108
  28.5 11.2 %copy-start.1 = (bf16[256,384]{1,0:T(8,128)(2,1)S(1)}, bf16[256,384]{1,0:T(8,128)(2,1)}, u32[]{:S(2)}) copy-start(bf16[256,384]{1,0:T(8,128)(2,1)} %g_ref.1) | copy-start | bytes 589828
  35.8 3.9 %collective-permute-start.2 = (bf16[8,96,256]{2,1,0:T(8,128)(2,1)S(1)}, bf16[8,96,256]{2,1,0:T(8,128)(2,1)S(1)}, u32[]{:S(2)}, u32[]{:S(2)}) collective-permute-start(bf16[8,96,256]{2,1,0:T(8,128)(2,1)S(1)} %collective-permute-done.mine_ref), channel_id=1, source_target_pairs={{0,1},{1,0},{2,3},{3,2},{4,5},{5,4},{6,7},{7,6},{8,9},{9,8},{10,11... | collective-permute-start | bytes 1179656 | tf_op jit(solution)/shard_map/ppermute | solution.py:121
  37.7 9.2 %collective-permute-start.3 = (bf16[4,96,256]{2,1,0:T(8,128)(2,1)S(1)}, bf16[4,96,256]{2,1,0:T(8,128)(2,1)S(1)}, u32[]{:S(2)}, u32[]{:S(2)}) collective-permute-start(bf16[4,96,256]{2,1,0:T(8,128)(2,1)S(1)} %dynamic-slice_bitcast_fusion), channel_id=1, source_target_pairs={{0,128},{128,0},{1,129},{129,1},{2,130},{130,2},{3,131},{131,3},{4... | collective-permute-start | bytes 589832 | tf_op jit(solution)/shard_map/ppermute | solution.py:122
  48.0 4.7 %collective-permute-start.4 = (bf16[24,96,256]{2,1,0:T(8,128)(2,1)S(1)}, bf16[24,96,256]{2,1,0:T(8,128)(2,1)S(1)}, u32[]{:S(2)}, u32[]{:S(2)}) collective-permute-start(bf16[24,96,256]{2,1,0:T(8,128)(2,1)S(1)} %pad_maximum_fusion), channel_id=1, source_target_pairs={{0,1},{1,0},{2,3},{3,2},{4,5},{5,4},{6,7},{7,6},{8,9},{9,8},{10,11... | collective-permute-start | bytes 3538952 | tf_op jit(solution)/shard_map/ppermute | solution.py:143
  49.9 9.2 %collective-permute-start.8 = (bf16[256,384]{1,0:T(8,128)(2,1)S(1)}, bf16[256,384]{1,0:T(8,128)(2,1)S(1)}, u32[]{:S(2)}, u32[]{:S(2)}) collective-permute-start(bf16[256,384]{1,0:T(8,128)(2,1)S(1)} %get-tuple-element.29.pg_ref), channel_id=1, source_target_pairs={{0,128},{128,0},{1,129},{129,1},{2,130},{130,2},{3,131},{131,3},{4... | collective-permute-start | bytes 589832 | tf_op jit(solution)/shard_map/ppermute | solution.py:142
  62.3 45.2 %all-to-all-start = ((bf16[4,384,384]{2,1,0:T(8,128)(2,1)}), bf16[4,384,384]{2,1,0:T(8,128)(2,1)S(1)}, u32[]{:S(2)}, u32[]{:S(2)}) async-start(bf16[4,384,384]{2,1,0:T(8,128)(2,1)} %bitcast.11), calls=%async_computation | async-start | bytes 2359296 | tf_op jit(solution)/shard_map/all_to_all | solution.py:156
  77.2 12.3 %collective-permute-start.5 = (bf16[8,96,256]{2,1,0:T(8,128)(2,1)S(1)}, bf16[8,96,256]{2,1,0:T(8,128)(2,1)S(1)}, u32[]{:S(2)}, u32[]{:S(2)}) collective-permute-start(bf16[8,96,256]{2,1,0:T(8,128)(2,1)S(1)} %slice.63), channel_id=1, source_target_pairs={{0,2},{2,0},{1,3},{3,1},{4,6},{6,4},{5,7},{7,5},{8,10},{10,8},{9,1... | collective-permute-start | bytes 1179656 | tf_op jit(solution)/shard_map/ppermute | solution.py:89
  89.7 7.6 %collective-permute-start.6 = (bf16[4,96,256]{2,1,0:T(8,128)(2,1)S(1)}, bf16[4,96,256]{2,1,0:T(8,128)(2,1)S(1)}, u32[]{:S(2)}, u32[]{:S(2)}) collective-permute-start(bf16[4,96,256]{2,1,0:T(8,128)(2,1)S(1)} %slice.64), channel_id=1, source_target_pairs={{0,4},{4,0},{8,12},{12,8},{16,20},{20,16},{24,28},{28,24},{1,5},{5... | collective-permute-start | bytes 589832 | tf_op jit(solution)/shard_map/ppermute | solution.py:89
  97.3 7.9 %collective-permute-start.7 = (bf16[2,96,256]{2,1,0:T(8,128)(2,1)S(1)}, bf16[2,96,256]{2,1,0:T(8,128)(2,1)S(1)}, u32[]{:S(2)}, u32[]{:S(2)}) collective-permute-start(bf16[2,96,256]{2,1,0:T(8,128)(2,1)S(1)} %slice.65), channel_id=1, source_target_pairs={{0,8},{4,12},{8,0},{12,4},{16,24},{20,28},{24,16},{28,20},{1,9},{5... | collective-permute-start | bytes 294920 | tf_op jit(solution)/shard_map/ppermute | solution.py:89
  108.4 18.3 %all-to-all-start.1 = ((bf16[4,96,384]{2,1,0:T(8,128)(2,1)}), bf16[4,96,384]{2,1,0:T(8,128)(2,1)S(1)}, u32[]{:S(2)}, u32[]{:S(2)}) async-start(bf16[4,96,384]{2,1,0:T(8,128)(2,1)} %bitcast.14), calls=%async_computation.1 | async-start | bytes 589824 | tf_op jit(solution)/shard_map/all_to_all | solution.py:167
  115.7 10.4 %collective-permute-start.9 = (bf16[1,96,256]{2,1,0:T(8,128)(2,1)S(1)}, bf16[1,96,256]{2,1,0:T(8,128)(2,1)S(1)}, u32[]{:S(2)}, u32[]{:S(2)}) collective-permute-start(bf16[1,96,256]{2,1,0:T(8,128)(2,1)S(1)} %slice.66), channel_id=1, source_target_pairs={{0,16},{4,20},{8,24},{12,28},{16,0},{20,4},{24,8},{28,12},{1,17},{... | collective-permute-start | bytes 147464 | tf_op jit(solution)/shard_map/ppermute | solution.py:89

commit v6 on v5

--- a/solution.py
+++ b/solution.py
@@ -12,6 +12,7 @@
 VMEM = pl.BlockSpec(memory_space=pltpu.VMEM)
 SMEM = pl.BlockSpec(memory_space=pltpu.SMEM)
 PAIR = [(0, 1), (1, 0)]
+EARLY_FLOPS = 60_000_000_000
 
 
 def gelu_slope(pre):
@@ -41,17 +42,21 @@
 
 
 def hidden_kernel(
-    at_ref, mine_ref, other_ref, w_ref, g_ref, pre_ref, rest, pg_ref, keep_ref, send_ref, w_half
+    at_ref, mine_ref, other_ref, w_ref, g_ref, pre_ref, rest, pg_ref, w_half
 ):
-    y_own, xl, core = at_ref[0], at_ref[1], at_ref[2]
-    ny, feats, _ = mine_ref.shape
-    bits = ny.bit_length() - 1
-    for y in range(ny):
+    xl, core = at_ref[1], at_ref[2]
+    for y in range(mine_ref.shape[0]):
         rest[y, core] = mine_ref[y]
         rest[y, 1 - core] = other_ref[y]
     pre = pre_ref[...] + half_pre(1 - xl, rest, w_ref, w_half)
-    pg = (g_ref[...].astype(F32) * gelu_slope(pre)).astype(BF16)
-    pg_ref[...] = pg
+    pg_ref[...] = (g_ref[...].astype(F32) * gelu_slope(pre)).astype(BF16)
+
+
+def input_kernel(at_ref, w_ref, pg_ref, keep_ref, send_ref):
+    y_own, xl, core = at_ref[0], at_ref[1], at_ref[2]
+    ny, feats = keep_ref.shape[0] // 2, keep_ref.shape[1]
+    bits = ny.bit_length() - 1
+    pg = pg_ref[...]
     for r in range(ny):
         at = sum((r >> k & 1) << (bits - 1 - k) for k in range(bits))
         start = lax.bitwise_xor(y_own, jnp.int32(r)) * (4 * feats)
@@ -72,16 +77,46 @@
                         ref[to] = part.astype(ref.dtype)
 
 
-def weight_kernel(at_ref, own, rest, t1_ref, t2_ref, tother_ref, pg_ref, pgpair_ref, out_ref):
+def own_kernel(at_ref, own, rest, pg_ref, acc_ref):
     xl, core, zl = at_ref[1], at_ref[2], at_ref[3]
+    for i in range(acc_ref.shape[0] // 4):
+        for x, tok in ((xl, own), (1 - xl, rest)):
+            for c in (core, 1 - core):
+                acc_ref[4 * i + 2 * x + c] = jnp.dot(
+                    tok[2 * i + zl, c], pg_ref[...], preferred_element_type=F32
+                )
+
+
+def weight_kernel(at_ref, acc_ref, t1_ref, t2_ref, tother_ref, pgpair_ref, out_ref):
+    xl, core = at_ref[1], at_ref[2]
     nh = t1_ref.shape[0]
     for i in range(nh):
-        for x, (tok, mine) in enumerate(((own, t1_ref), (rest, t2_ref))):
-            for c, pair in ((core, mine[i]), (1 - core, tother_ref[x * nh + i])):
-                total = jnp.dot(
-                    tok[2 * i + zl, c], pg_ref[...], preferred_element_type=F32
-                ) + jnp.dot(pair, pgpair_ref[...], preferred_element_type=F32)
-                out_ref[4 * i + 2 * lax.bitwise_xor(xl, jnp.int32(x)) + c] = total.astype(BF16)
+        for x, mine in ((0, t1_ref), (1, t2_ref)):
+            for c, tok in ((core, mine[i]), (1 - core, tother_ref[x * nh + i])):
+                at = 4 * i + 2 * lax.bitwise_xor(xl, jnp.int32(x)) + c
+                total = acc_ref[at] + jnp.dot(
+                    tok, pgpair_ref[...], preferred_element_type=F32
+                )
+                out_ref[at] = total.astype(BF16)
+
+
+def add_kernel(keep_ref, arrived_ref, out_ref):
+    out_ref[...] = keep_ref[...] + arrived_ref[...].astype(F32)
+
+
+def halve_early(total, axis, pairs):
+    half = total.shape[0] // 2
+    arrived = lax.ppermute(total[half:].astype(BF16), axis, pairs)
+    return pl.pallas_call(
+        add_kernel,
+        out_shape=jax.ShapeDtypeStruct(arrived.shape, F32),
+        in_specs=[VMEM, VMEM],
+        out_specs=VMEM,
+        compiler_params=pltpu.CompilerParams(vmem_limit_bytes=4 << 20),
+        cost_estimate=pl.CostEstimate(
+            flops=EARLY_FLOPS, bytes_accessed=2 << 20, transcendentals=0
+        ),
+    )(total[:half], arrived)
 
 
 def halve(total, axis, pairs):
@@ -120,51 +155,67 @@
         mine, t1, pre = lax.optimization_barrier((mine, t1, pre))
         other = lax.ppermute(mine, "c", PAIR)
         t2 = lax.ppermute(pick(mine.reshape(nh, 2, feats, rows), 1 - zl, 1), "zl", PAIR)
-        rest, pre_grad, keep, send = pl.pallas_call(
+        rest, pre_grad = pl.pallas_call(
             hidden_kernel,
             out_shape=(
                 jax.ShapeDtypeStruct((ny, 2, feats, rows), BF16),
                 jax.ShapeDtypeStruct((rows, hidden), BF16),
+            ),
+            in_specs=[SMEM] + [VMEM] * 5,
+            out_specs=(VMEM, VMEM),
+            scratch_shapes=[pltpu.VMEM((d // 2, hidden), BF16)],
+            compiler_params=pltpu.CompilerParams(vmem_limit_bytes=8 << 20),
+            cost_estimate=pl.CostEstimate(
+                flops=d * rows * hidden,
+                bytes_accessed=5 << 20,
+                transcendentals=rows * hidden,
+            ),
+        )(at, mine, other, w_in, hidden_grad, pre)
+        pair_grad = lax.ppermute(pre_grad, "zl", PAIR)
+        keep, send = pl.pallas_call(
+            input_kernel,
+            out_shape=(
                 jax.ShapeDtypeStruct((2 * ny, feats, rows), F32),
                 jax.ShapeDtypeStruct((2 * ny, feats, rows), BF16),
             ),
-            in_specs=[SMEM, VMEM, VMEM, VMEM, VMEM, VMEM],
-            out_specs=(VMEM, VMEM, VMEM, VMEM),
-            scratch_shapes=[pltpu.VMEM((d // 2, hidden), BF16)],
+            in_specs=[SMEM, VMEM, VMEM],
+            out_specs=(VMEM, VMEM),
             compiler_params=pltpu.CompilerParams(vmem_limit_bytes=8 << 20),
             cost_estimate=pl.CostEstimate(
-                flops=3 * d * rows * hidden,
-                bytes_accessed=8 << 20,
-                transcendentals=rows * hidden,
-            ),
-        )(at, mine, other, w_in, hidden_grad, pre)
-        pre_grad, send, t1, t2 = lax.optimization_barrier((pre_grad, send, t1, t2))
-        pair_grad = lax.ppermute(pre_grad, "zl", PAIR)
+                flops=2 * d * rows * hidden, bytes_accessed=5 << 20, transcendentals=0
+            ),
+        )(at, w_in, pre_grad)
+        acc = pl.pallas_call(
+            own_kernel,
+            out_shape=jax.ShapeDtypeStruct((4 * nh, feats, hidden), F32),
+            in_specs=[SMEM] + [VMEM] * 3,
+            out_specs=VMEM,
+            compiler_params=pltpu.CompilerParams(vmem_limit_bytes=4 << 20),
+            cost_estimate=pl.CostEstimate(
+                flops=d * rows * hidden, bytes_accessed=4 << 20, transcendentals=0
+            ),
+        )(at, own, rest, pre_grad)
+        send, t1, t2, pair_grad, acc = lax.optimization_barrier((send, t1, t2, pair_grad, acc))
         swapped = lax.ppermute(jnp.concatenate([send, t1, t2]), "c", PAIR)
         total = keep + swapped[: 2 * ny].astype(F32)
         total, tother = lax.optimization_barrier((total, swapped[2 * ny :]))
         wpart = pl.pallas_call(
             weight_kernel,
             out_shape=jax.ShapeDtypeStruct((4 * nh, feats, hidden), BF16),
-            in_specs=[SMEM] + [VMEM] * 7,
+            in_specs=[SMEM] + [VMEM] * 5,
             out_specs=VMEM,
             compiler_params=pltpu.CompilerParams(vmem_limit_bytes=4 << 20),
             cost_estimate=pl.CostEstimate(
-                flops=2 * d * rows * hidden, bytes_accessed=4 << 20, transcendentals=0
-            ),
-        )(at, own, rest, t1, t2, tother, pre_grad, pair_grad)
-        pieces = lax.all_to_all(wpart.reshape(nh, -1, hidden), "zh", 0, 0, tiled=True)
-        steps = [("xl", PAIR)]
+                flops=d * rows * hidden, bytes_accessed=4 << 20, transcendentals=0
+            ),
+        )(at, acc, t1, t2, tother, pair_grad)
+        wpart = wpart.reshape(nh * nx, -1, hidden)
+        pieces = lax.all_to_all(wpart, ("zh", "xh"), 0, 0, tiled=True)
+        total = halve_early(total, "xl", PAIR)
         bit = 1
         while bit < ny:
-            steps.append(("y", [(i, i ^ bit) for i in range(ny)]))
+            total = halve(total, "y", [(i, i ^ bit) for i in range(ny)])
             bit *= 2
-        for n, (axis, pairs) in enumerate(steps):
-            if n == len(steps) - 1:
-                total, pieces = lax.optimization_barrier((total, pieces))
-            total = halve(total, axis, pairs)
-        sums = jnp.sum(pieces.astype(F32), axis=0).astype(BF16)
-        pieces = lax.all_to_all(sums.reshape(nx, -1, hidden), "xh", 0, 0, tiled=True)
         weight_sum = jnp.sum(pieces.astype(F32), axis=0)
         return (total[0].astype(BF16).T, weight_sum.astype(BF16))
 

time: 128 us -> 124 us (0.969)
  the two profiles are of different devices: /device:TPU:132 before, /device:TPU:7 now
where the time goes in v6:
time: 124 us; the launch traced here: 123 us
  starting transfers between devices  49.6 us (40%)
  waiting for transfers between devices  36.5 us (29%)
  blocking collectives  21.4 us (17%)
  Pallas kernels  10.2 us (8%)
  other arithmetic  2.83 us (2%)
  local copies, waits for them, and re-layouts  1.69 us (1%)
    all_gather x1, blocking collectives, local(): lax.all_gather(tokens.T, ('y', 'c'), axis=0).reshape(ny, 2, feats, rows)  21.4 us
    all_to_all x1, starting transfers between devices, local(): pieces = lax.all_to_all(wpart, ('zh', 'xh'), 0, 0, tiled=True)  19.7 us
    ppermute x3, waiting for transfers between devices, halve(): arrived = lax.ppermute(total[half:].astype(BF16), axis, pairs)  15.4 us
    all_to_all x1, waiting for transfers between devices, local(): pieces = lax.all_to_all(wpart, ('zh', 'xh'), 0, 0, tiled=True)  13.5 us
    ppermute x3, starting transfers between devices, halve(): arrived = lax.ppermute(total[half:].astype(BF16), axis, pairs)  8.28 us
    ppermute x1, starting transfers between devices, local(): lax.ppermute(pick(half.reshape(nh, 2, feats, rows), 1 - zl, 1), 'zl', PAIR)  4.9 us
    ppermute x1, starting transfers between devices, local(): lax.ppermute(pick(mine.reshape(nh, 2, feats, rows), 1 - zl, 1), 'zl', PAIR)  4.57 us
    ppermute x1, waiting for transfers between devices, local(): lax.ppermute(pick(half.reshape(nh, 2, feats, rows), 1 - zl, 1), 'zl', PAIR)  3.95 us
  transfers between devices with their start and end apart: 11, of which 7 were waited for; matrix products, arithmetic and copies ran while one was open for 1% of the time, Pallas kernels for 8%

profile of v6, /device:TPU:7, one launch (start us, length us, event | category | flops | bytes accessed | tf_op | source)
XLA Modules:
  0.0 123.1 jit_solution(1106378150142235210)
XLA Ops:
  0.6 21.4 %all-gather = bf16[1536,256]{1,0:T(8,128)(2,1)S(1)} all-gather(bf16[96,256]{1,0:T(8,128)(2,1)} %bitcast.26), channel_id=2, replica_groups=mesh['zh'=4,'zl'=2,'xh'=4,'y'=8,'xl'=2,'c'=2] {'y','c'}, dimensions={0}, use_global_device_ids=true | all-gather | bytes 835584 | tf_op jit(solution)/shard_map/all_gather | solution.py:140
  22.8 2.2 %collective-permute-start = (bf16[8,96,256]{2,1,0:T(8,128)(2,1)}, bf16[8,96,256]{2,1,0:T(8,128)(2,1)S(1)}, u32[]{:S(2)}, u32[]{:S(2)}) collective-permute-start(bf16[8,96,256]{2,1,0:T(8,128)(2,1)} %fusion.2), channel_id=1, source_target_pairs={{0,2},{2,0},{1,3},{3,1},{4,6},{6,4},{5,7},{7,5},{8,10},{10,8},{9,1... | collective-permute-start | bytes 1179656 | tf_op jit(solution)/shard_map/ppermute | solution.py:142
  25.7 4.9 %collective-permute-start.1 = (bf16[4,96,256]{2,1,0:T(8,128)(2,1)}, bf16[4,96,256]{2,1,0:T(8,128)(2,1)}, u32[]{:S(2)}, u32[]{:S(2)}) collective-permute-start(bf16[4,96,256]{2,1,0:T(8,128)(2,1)} %dynamic-slice_bitcast_fusion.1), channel_id=1, source_target_pairs={{0,128},{128,0},{1,129},{129,1},{2,130},{130,2},{3,131},{131,3},{4... | collective-permute-start | bytes 589832 | tf_op jit(solution)/shard_map/ppermute | solution.py:143
  30.7 1.2 shard_map.50.pre_ref
  31.9 3.9 %collective-permute-done.1.t1_ref = bf16[4,96,256]{2,1,0:T(8,128)(2,1)} collective-permute-done((bf16[4,96,256]{2,1,0:T(8,128)(2,1)}, bf16[4,96,256]{2,1,0:T(8,128)(2,1)}, u32[]{:S(2)}, u32[]{:S(2)}) %collective-permute-start.1) | collective-permute-done | bytes 196640 | tf_op jit(solution)/shard_map/ppermute | solution.py:143
  35.8 2.9 %collective-permute-start.2 = (bf16[8,96,256]{2,1,0:T(8,128)(2,1)S(1)}, bf16[8,96,256]{2,1,0:T(8,128)(2,1)S(1)}, u32[]{:S(2)}, u32[]{:S(2)}) collective-permute-start(bf16[8,96,256]{2,1,0:T(8,128)(2,1)S(1)} %collective-permute-done.mine_ref), channel_id=1, source_target_pairs={{0,1},{1,0},{2,3},{3,2},{4,5},{5,4},{6,7},{7,6},{8,9},{9,8},{10,11... | collective-permute-start | bytes 1179656 | tf_op jit(solution)/shard_map/ppermute | solution.py:156
  38.7 4.6 %collective-permute-start.3 = (bf16[4,96,256]{2,1,0:T(8,128)(2,1)S(1)}, bf16[4,96,256]{2,1,0:T(8,128)(2,1)S(1)}, u32[]{:S(2)}, u32[]{:S(2)}) collective-permute-start(bf16[4,96,256]{2,1,0:T(8,128)(2,1)S(1)} %dynamic-slice_bitcast_fusion), channel_id=1, source_target_pairs={{0,128},{128,0},{1,129},{129,1},{2,130},{130,2},{3,131},{131,3},{4... | collective-permute-start | bytes 589832 | tf_op jit(solution)/shard_map/ppermute | solution.py:157
  43.3 1.5 %shard_map.51 = (bf16[8,2,96,256]{3,2,1,0:T(8,128)(2,1)S(1)}, bf16[256,384]{1,0:T(8,128)(2,1)S(1)}) custom-call(s32[4]{0:T(128)S(1)} %pad_add_fusion.at_ref, bf16[8,96,256]{2,1,0:T(8,128)(2,1)S(1)} %collective-permute-done.mine_ref, bf16[8,96,256]{2,1,0:T(8,128)(2,1)S(1)} %collective-permute-done.2.other_ref, bf16[3072,384]{1,0:T(8,128)(2,1)S(1)} %copy-done, ...), custom_call_target="tpu_custom_call" | custom-call | flops 301989888 | bytes 5242880 | tf_op jit(solution)/shard_map/pallas_call | solution.py:158
  44.8 1.9 %collective-permute-start.4 = (bf16[256,384]{1,0:T(8,128)(2,1)S(1)}, bf16[256,384]{1,0:T(8,128)(2,1)S(1)}, u32[]{:S(2)}, u32[]{:S(2)}) collective-permute-start(bf16[256,384]{1,0:T(8,128)(2,1)S(1)} %get-tuple-element.18.pg_ref), channel_id=1, source_target_pairs={{0,128},{128,0},{1,129},{129,1},{2,130},{130,2},{3,131},{131,3},{4... | collective-permute-start | bytes 589832 | tf_op jit(solution)/shard_map/ppermute | solution.py:174
  46.8 1.2 shard_map.53.acc_ref
  47.9 3.8 %shard_map.52 = (f32[16,96,256]{2,1,0:T(8,128)S(1)}, bf16[16,96,256]{2,1,0:T(8,128)(2,1)S(1)}) custom-call(s32[4]{0:T(128)S(1)} %pad_add_fusion.at_ref, bf16[3072,384]{1,0:T(8,128)(2,1)S(1)} %copy-done, bf16[256,384]{1,0:T(8,128)(2,1)S(1)} %get-tuple-element.18.pg_ref), custom_call_target="tpu_custom_call" | custom-call | flops 603979776 | bytes 5242880 | tf_op jit(solution)/shard_map/pallas_call | solution.py:175
  51.7 1.2 collective-permute-done.4.pgpair_ref
  54.0 3.0 %collective-permute-start.5 = (bf16[24,96,256]{2,1,0:T(8,128)(2,1)S(1)}, bf16[24,96,256]{2,1,0:T(8,128)(2,1)S(1)}, u32[]{:S(2)}, u32[]{:S(2)}) collective-permute-start(bf16[24,96,256]{2,1,0:T(8,128)(2,1)S(1)} %pad_maximum_fusion), channel_id=1, source_target_pairs={{0,1},{1,0},{2,3},{3,2},{4,5},{5,4},{6,7},{7,6},{8,9},{9,8},{10,11... | collective-permute-start | bytes 3538952 | tf_op jit(solution)/shard_map/ppermute | solution.py:199
  57.0 2.5 %collective-permute-done.5 = bf16[24,96,256]{2,1,0:T(8,128)(2,1)S(1)} collective-permute-done((bf16[24,96,256]{2,1,0:T(8,128)(2,1)S(1)}, bf16[24,96,256]{2,1,0:T(8,128)(2,1)S(1)}, u32[]{:S(2)}, u32[]{:S(2)}) %collective-permute-start.5) | collective-permute-done | bytes 1179680 | tf_op jit(solution)/shard_map/ppermute | solution.py:199
  59.7 2.2 %collective-permute-start.6 = (bf16[8,96,256]{2,1,0:T(8,128)(2,1)S(1)}, bf16[8,96,256]{2,1,0:T(8,128)(2,1)S(1)}, u32[]{:S(2)}, u32[]{:S(2)}) collective-permute-start(bf16[8,96,256]{2,1,0:T(8,128)(2,1)S(1)} %slice.65), channel_id=1, source_target_pairs={{0,2},{2,0},{1,3},{3,1},{4,6},{6,4},{5,7},{7,5},{8,10},{10,8},{9,1... | collective-permute-start | bytes 1179656 | tf_op jit(solution)/shard_map/ppermute | solution.py:109
  62.0 2.6 %shard_map.55 = bf16[16,96,384]{2,1,0:T(8,128)(2,1)} custom-call(s32[4]{0:T(128)S(1)} %pad_add_fusion.at_ref, f32[16,96,384]{2,1,0:T(8,128)S(1)} %shard_map.53.acc_ref, bf16[4,96,256]{2,1,0:T(8,128)(2,1)} %collective-permute-done.1.t1_ref, bf16[4,96,256]{2,1,0:T(8,128)(2,1)S(1)} %collective-permute-done.3.t2_ref, bf16[8,96,256]{2,1,0:T(8,128)(2,1)S(1)} %slice.45.tother_ref, ...), custom_call_target="tpu_custom_call" | custom-call | flops 301989888 | bytes 4194304 | tf_op jit(solution)/shard_map/pallas_call | solution.py:202
  64.6 19.7 %all-to-all-start = ((bf16[16,96,384]{2,1,0:T(8,128)(2,1)}), bf16[16,96,384]{2,1,0:T(8,128)(2,1)S(1)}, u32[]{:S(2)}, u32[]{:S(2)}) async-start(bf16[16,96,384]{2,1,0:T(8,128)(2,1)} %shard_map.55), calls=%async_computation | async-start | bytes 2359296 | tf_op jit(solution)/shard_map/all_to_all | solution.py:213
  84.4 1.9 %collective-permute-start.7 = (bf16[4,96,256]{2,1,0:T(8,128)(2,1)S(1)}, bf16[4,96,256]{2,1,0:T(8,128)(2,1)S(1)}, u32[]{:S(2)}, u32[]{:S(2)}) collective-permute-start(bf16[4,96,256]{2,1,0:T(8,128)(2,1)S(1)} %slice.66), channel_id=1, source_target_pairs={{0,4},{4,0},{8,12},{12,8},{16,20},{20,16},{24,28},{28,24},{1,5},{5... | collective-permute-start | bytes 589832 | tf_op jit(solution)/shard_map/ppermute | solution.py:124
  86.4 5.1 %collective-permute-done.7 = bf16[4,96,256]{2,1,0:T(8,128)(2,1)S(1)} collective-permute-done((bf16[4,96,256]{2,1,0:T(8,128)(2,1)S(1)}, bf16[4,96,256]{2,1,0:T(8,128)(2,1)S(1)}, u32[]{:S(2)}, u32[]{:S(2)}) %collective-permute-start.7) | collective-permute-done | bytes 196640 | tf_op jit(solution)/shard_map/ppermute | solution.py:124
  91.6 1.9 %collective-permute-start.8 = (bf16[2,96,256]{2,1,0:T(8,128)(2,1)S(1)}, bf16[2,96,256]{2,1,0:T(8,128)(2,1)S(1)}, u32[]{:S(2)}, u32[]{:S(2)}) collective-permute-start(bf16[2,96,256]{2,1,0:T(8,128)(2,1)S(1)} %slice.67), channel_id=1, source_target_pairs={{0,8},{4,12},{8,0},{12,4},{16,24},{20,28},{24,16},{28,20},{1,9},{5... | collective-permute-start | bytes 294920 | tf_op jit(solution)/shard_map/ppermute | solution.py:124
  93.5 5.7 %collective-permute-done.8 = bf16[2,96,256]{2,1,0:T(8,128)(2,1)S(1)} collective-permute-done((bf16[2,96,256]{2,1,0:T(8,128)(2,1)S(1)}, bf16[2,96,256]{2,1,0:T(8,128)(2,1)S(1)}, u32[]{:S(2)}, u32[]{:S(2)}) %collective-permute-start.8) | collective-permute-done | bytes 98336 | tf_op jit(solution)/shard_map/ppermute | solution.py:124
  99.2 4.4 %collective-permute-start.9 = (bf16[1,96,256]{2,1,0:T(8,128)(2,1)S(1)}, bf16[1,96,256]{2,1,0:T(8,128)(2,1)S(1)}, u32[]{:S(2)}, u32[]{:S(2)}) collective-permute-start(bf16[1,96,256]{2,1,0:T(8,128)(2,1)S(1)} %slice.68), channel_id=1, source_target_pairs={{0,16},{4,20},{8,24},{12,28},{16,0},{20,4},{24,8},{28,12},{1,17},{... | collective-permute-start | bytes 147464 | tf_op jit(solution)/shard_map/ppermute | solution.py:124
  103.7 4.6 %collective-permute-done.9 = bf16[1,96,256]{2,1,0:T(8,128)(2,1)S(1)} collective-permute-done((bf16[1,96,256]{2,1,0:T(8,128)(2,1)S(1)}, bf16[1,96,256]{2,1,0:T(8,128)(2,1)S(1)}, u32[]{:S(2)}, u32[]{:S(2)}) %collective-permute-start.9) | collective-permute-done | bytes 49184 | tf_op jit(solution)/shard_map/ppermute | solution.py:124
  108.9 13.5 %all-to-all-done = bf16[16,96,384]{2,1,0:T(8,128)(2,1)S(1)} async-done(((bf16[16,96,384]{2,1,0:T(8,128)(2,1)}), bf16[16,96,384]{2,1,0:T(8,128)(2,1)S(1)}, u32[]{:S(2)}, u32[]{:S(2)}) %all-to-all-start) | async-done | bytes 1179680 | tf_op jit(solution)/shard_map/all_to_all | solution.py:213
  (26 shorter events, 4.6 us)
Async XLA Ops:
  0.6 30.1 %copy-start = (bf16[3072,384]{1,0:T(8,128)(2,1)S(1)}, bf16[3072,384]{1,0:T(8,128)(2,1)}, u32[]{:S(2)}) copy-start(bf16[3072,384]{1,0:T(8,128)(2,1)} %w_ref.5) | copy-start | bytes 7077892
  22.8 13.0 %collective-permute-start = (bf16[8,96,256]{2,1,0:T(8,128)(2,1)}, bf16[8,96,256]{2,1,0:T(8,128)(2,1)S(1)}, u32[]{:S(2)}, u32[]{:S(2)}) collective-permute-start(bf16[8,96,256]{2,1,0:T(8,128)(2,1)} %fusion.2), channel_id=1, source_target_pairs={{0,2},{2,0},{1,3},{3,1},{4,6},{6,4},{5,7},{7,5},{8,10},{10,8},{9,1... | collective-permute-start | bytes 1179656 | tf_op jit(solution)/shard_map/ppermute | solution.py:142
  25.7 10.1 %collective-permute-start.1 = (bf16[4,96,256]{2,1,0:T(8,128)(2,1)}, bf16[4,96,256]{2,1,0:T(8,128)(2,1)}, u32[]{:S(2)}, u32[]{:S(2)}) collective-permute-start(bf16[4,96,256]{2,1,0:T(8,128)(2,1)} %dynamic-slice_bitcast_fusion.1), channel_id=1, source_target_pairs={{0,128},{128,0},{1,129},{129,1},{2,130},{130,2},{3,131},{131,3},{4... | collective-permute-start | bytes 589832 | tf_op jit(solution)/shard_map/ppermute | solution.py:143
  30.7 12.6 %copy-start.1 = (bf16[256,384]{1,0:T(8,128)(2,1)S(1)}, bf16[256,384]{1,0:T(8,128)(2,1)}, u32[]{:S(2)}) copy-start(bf16[256,384]{1,0:T(8,128)(2,1)} %g_ref.1) | copy-start | bytes 589828
  35.8 7.5 %collective-permute-start.2 = (bf16[8,96,256]{2,1,0:T(8,128)(2,1)S(1)}, bf16[8,96,256]{2,1,0:T(8,128)(2,1)S(1)}, u32[]{:S(2)}, u32[]{:S(2)}) collective-permute-start(bf16[8,96,256]{2,1,0:T(8,128)(2,1)S(1)} %collective-permute-done.mine_ref), channel_id=1, source_target_pairs={{0,1},{1,0},{2,3},{3,2},{4,5},{5,4},{6,7},{7,6},{8,9},{9,8},{10,11... | collective-permute-start | bytes 1179656 | tf_op jit(solution)/shard_map/ppermute | solution.py:156
  38.7 13.0 %collective-permute-start.3 = (bf16[4,96,256]{2,1,0:T(8,128)(2,1)S(1)}, bf16[4,96,256]{2,1,0:T(8,128)(2,1)S(1)}, u32[]{:S(2)}, u32[]{:S(2)}) collective-permute-start(bf16[4,96,256]{2,1,0:T(8,128)(2,1)S(1)} %dynamic-slice_bitcast_fusion), channel_id=1, source_target_pairs={{0,128},{128,0},{1,129},{129,1},{2,130},{130,2},{3,131},{131,3},{4... | collective-permute-start | bytes 589832 | tf_op jit(solution)/shard_map/ppermute | solution.py:157
  44.8 8.1 %collective-permute-start.4 = (bf16[256,384]{1,0:T(8,128)(2,1)S(1)}, bf16[256,384]{1,0:T(8,128)(2,1)S(1)}, u32[]{:S(2)}, u32[]{:S(2)}) collective-permute-start(bf16[256,384]{1,0:T(8,128)(2,1)S(1)} %get-tuple-element.18.pg_ref), channel_id=1, source_target_pairs={{0,128},{128,0},{1,129},{129,1},{2,130},{130,2},{3,131},{131,3},{4... | collective-permute-start | bytes 589832 | tf_op jit(solution)/shard_map/ppermute | solution.py:174
  54.0 5.5 %collective-permute-start.5 = (bf16[24,96,256]{2,1,0:T(8,128)(2,1)S(1)}, bf16[24,96,256]{2,1,0:T(8,128)(2,1)S(1)}, u32[]{:S(2)}, u32[]{:S(2)}) collective-permute-start(bf16[24,96,256]{2,1,0:T(8,128)(2,1)S(1)} %pad_maximum_fusion), channel_id=1, source_target_pairs={{0,1},{1,0},{2,3},{3,2},{4,5},{5,4},{6,7},{7,6},{8,9},{9,8},{10,11... | collective-permute-start | bytes 3538952 | tf_op jit(solution)/shard_map/ppermute | solution.py:199
  59.7 24.6 %collective-permute-start.6 = (bf16[8,96,256]{2,1,0:T(8,128)(2,1)S(1)}, bf16[8,96,256]{2,1,0:T(8,128)(2,1)S(1)}, u32[]{:S(2)}, u32[]{:S(2)}) collective-permute-start(bf16[8,96,256]{2,1,0:T(8,128)(2,1)S(1)} %slice.65), channel_id=1, source_target_pairs={{0,2},{2,0},{1,3},{3,1},{4,6},{6,4},{5,7},{7,5},{8,10},{10,8},{9,1... | collective-permute-start | bytes 1179656 | tf_op jit(solution)/shard_map/ppermute | solution.py:109
  64.6 57.8 %all-to-all-start = ((bf16[16,96,384]{2,1,0:T(8,128)(2,1)}), bf16[16,96,384]{2,1,0:T(8,128)(2,1)S(1)}, u32[]{:S(2)}, u32[]{:S(2)}) async-start(bf16[16,96,384]{2,1,0:T(8,128)(2,1)} %shard_map.55), calls=%async_computation | async-start | bytes 2359296 | tf_op jit(solution)/shard_map/all_to_all | solution.py:213
  84.4 7.1 %collective-permute-start.7 = (bf16[4,96,256]{2,1,0:T(8,128)(2,1)S(1)}, bf16[4,96,256]{2,1,0:T(8,128)(2,1)S(1)}, u32[]{:S(2)}, u32[]{:S(2)}) collective-permute-start(bf16[4,96,256]{2,1,0:T(8,128)(2,1)S(1)} %slice.66), channel_id=1, source_target_pairs={{0,4},{4,0},{8,12},{12,8},{16,20},{20,16},{24,28},{28,24},{1,5},{5... | collective-permute-start | bytes 589832 | tf_op jit(solution)/shard_map/ppermute | solution.py:124
  91.6 7.6 %collective-permute-start.8 = (bf16[2,96,256]{2,1,0:T(8,128)(2,1)S(1)}, bf16[2,96,256]{2,1,0:T(8,128)(2,1)S(1)}, u32[]{:S(2)}, u32[]{:S(2)}) collective-permute-start(bf16[2,96,256]{2,1,0:T(8,128)(2,1)S(1)} %slice.67), channel_id=1, source_target_pairs={{0,8},{4,12},{8,0},{12,4},{16,24},{20,28},{24,16},{28,20},{1,9},{5... | collective-permute-start | bytes 294920 | tf_op jit(solution)/shard_map/ppermute | solution.py:124
  99.2 9.0 %collective-permute-start.9 = (bf16[1,96,256]{2,1,0:T(8,128)(2,1)S(1)}, bf16[1,96,256]{2,1,0:T(8,128)(2,1)S(1)}, u32[]{:S(2)}, u32[]{:S(2)}) collective-permute-start(bf16[1,96,256]{2,1,0:T(8,128)(2,1)S(1)} %slice.68), channel_id=1, source_target_pairs={{0,16},{4,20},{8,24},{12,28},{16,0},{20,4},{24,8},{28,12},{1,17},{... | collective-permute-start | bytes 147464 | tf_op jit(solution)/shard_map/ppermute | solution.py:124

commit v7 on v6

--- a/solution.py
+++ b/solution.py
@@ -52,10 +52,13 @@
     pg_ref[...] = (g_ref[...].astype(F32) * gelu_slope(pre)).astype(BF16)
 
 
-def input_kernel(at_ref, w_ref, pg_ref, keep_ref, send_ref):
+def input_kernel(at_ref, w_ref, pg_ref, t1_ref, t2_ref, keep_ref, send_ref):
     y_own, xl, core = at_ref[0], at_ref[1], at_ref[2]
     ny, feats = keep_ref.shape[0] // 2, keep_ref.shape[1]
+    nh = t1_ref.shape[0]
     bits = ny.bit_length() - 1
+    send_ref[2 * ny : 2 * ny + nh] = t1_ref[...]
+    send_ref[2 * ny + nh :] = t2_ref[...]
     pg = pg_ref[...]
     for r in range(ny):
         at = sum((r >> k & 1) << (bits - 1 - k) for k in range(bits))
@@ -140,7 +143,8 @@
         own = lax.all_gather(tokens.T, ("y", "c"), axis=0).reshape(ny, 2, feats, rows)
         half = pick(own, core, 1)
         mine = lax.ppermute(half, "xl", PAIR)
-        t1 = lax.ppermute(pick(half.reshape(nh, 2, feats, rows), 1 - zl, 1), "zl", PAIR)
+        t1 = pick(pick(own.reshape(nh, 2, 2, feats, rows), 1 - zl, 1), core, 1)
+        t1 = lax.ppermute(t1, "zl", PAIR)
         pre = pl.pallas_call(
             pre_kernel,
             out_shape=jax.ShapeDtypeStruct((rows, hidden), F32),
@@ -176,15 +180,15 @@
             input_kernel,
             out_shape=(
                 jax.ShapeDtypeStruct((2 * ny, feats, rows), F32),
-                jax.ShapeDtypeStruct((2 * ny, feats, rows), BF16),
-            ),
-            in_specs=[SMEM, VMEM, VMEM],
+                jax.ShapeDtypeStruct((2 * ny + 2 * nh, feats, rows), BF16),
+            ),
+            in_specs=[SMEM] + [VMEM] * 4,
             out_specs=(VMEM, VMEM),
             compiler_params=pltpu.CompilerParams(vmem_limit_bytes=8 << 20),
             cost_estimate=pl.CostEstimate(
                 flops=2 * d * rows * hidden, bytes_accessed=5 << 20, transcendentals=0
             ),
-        )(at, w_in, pre_grad)
+        )(at, w_in, pre_grad, t1, t2)
         acc = pl.pallas_call(
             own_kernel,
             out_shape=jax.ShapeDtypeStruct((4 * nh, feats, hidden), F32),
@@ -195,8 +199,8 @@
                 flops=d * rows * hidden, bytes_accessed=4 << 20, transcendentals=0
             ),
         )(at, own, rest, pre_grad)
-        send, t1, t2, pair_grad, acc = lax.optimization_barrier((send, t1, t2, pair_grad, acc))
-        swapped = lax.ppermute(jnp.concatenate([send, t1, t2]), "c", PAIR)
+        send, pair_grad, acc = lax.optimization_barrier((send, pair_grad, acc))
+        swapped = lax.ppermute(send, "c", PAIR)
         total = keep + swapped[: 2 * ny].astype(F32)
         total, tother = lax.optimization_barrier((total, swapped[2 * ny :]))
         wpart = pl.pallas_call(

time: 124 us -> 121 us (0.976)
  waiting for transfers between devices: 36.5 us -> 35.1 us
    ppermute x2, waiting for transfers between devices: 6.4 us -> 4.4 us  [the longest x1 2.45 us: local(): swapped = lax.ppermute(send, 'c', PAIR)]
    unnamed x4 -> x6, local copies, waits for them, and re-layouts: 0.01 us -> 1.67 us
    squeeze x3, local copies, waits for them, and re-layouts: 1.48 us -> 0.07 us  [pick(): return lax.dynamic_index_in_dim(array, index, axis, keepdims=False)]
  transfers between devices with their start and end apart: 11 -> 11, of which waited for: 7 -> 9; matrix products, arithmetic and copies ran while one was open for 1% -> 1% of each run, Pallas kernels for 8% -> 8%
where the time goes in v7:
time: 121 us
  starting transfers between devices  50 us (41%)
  waiting for transfers between devices  35.1 us (29%)
  blocking collectives  21.3 us (18%)
  Pallas kernels  9.92 us (8%)
  local copies, waits for them, and re-layouts  1.93 us (2%)
  other arithmetic  1.76 us (1%)
    all_gather x1, blocking collectives, local(): lax.all_gather(tokens.T, ('y', 'c'), axis=0).reshape(ny, 2, feats, rows)  21.3 us
    all_to_all x1, starting transfers between devices, local(): pieces = lax.all_to_all(wpart, ('zh', 'xh'), 0, 0, tiled=True)  19.7 us
    ppermute x3, waiting for transfers between devices, halve(): arrived = lax.ppermute(total[half:].astype(BF16), axis, pairs)  15.4 us
    all_to_all x1, waiting for transfers between devices, local(): pieces = lax.all_to_all(wpart, ('zh', 'xh'), 0, 0, tiled=True)  13.7 us
    ppermute x3, starting transfers between devices, halve(): arrived = lax.ppermute(total[half:].astype(BF16), axis, pairs)  8.28 us
    ppermute x1, starting transfers between devices, local(): t1 = lax.ppermute(t1, 'zl', PAIR)  4.91 us
    ppermute x1, starting transfers between devices, local(): lax.ppermute(pick(mine.reshape(nh, 2, feats, rows), 1 - zl, 1), 'zl', PAIR)  4.91 us
    pallas_call x1, Pallas kernels, local(): pl.pallas_call(input_kernel, out_shape=(jax.ShapeDtypeStruct((2 * ny, fea...  3.83 us
  transfers between devices with their start and end apart: 11, of which 9 were waited for; matrix products, arithmetic and copies ran while one was open for 1% of the time, Pallas kernels for 8%

profile of v7, /device:TPU:7, one launch (start us, length us, event | category | flops | bytes accessed | tf_op | source)
XLA Modules:
  0.0 120.8 jit_solution(3356123135767106955)
XLA Ops:
  0.6 21.3 %all-gather = bf16[1536,256]{1,0:T(8,128)(2,1)S(1)} all-gather(bf16[96,256]{1,0:T(8,128)(2,1)} %bitcast.27), channel_id=2, replica_groups=mesh['zh'=4,'zl'=2,'xh'=4,'y'=8,'xl'=2,'c'=2] {'y','c'}, dimensions={0}, use_global_device_ids=true | all-gather | bytes 835584 | tf_op jit(solution)/shard_map/all_gather | solution.py:143
  22.0 2.2 %collective-permute-start = (bf16[8,96,256]{2,1,0:T(8,128)(2,1)S(1)}, bf16[8,96,256]{2,1,0:T(8,128)(2,1)S(1)}, u32[]{:S(2)}, u32[]{:S(2)}) collective-permute-start(bf16[8,96,256]{2,1,0:T(8,128)(2,1)S(1)} %dynamic-slice_bitcast_fusion), channel_id=1, source_target_pairs={{0,2},{2,0},{1,3},{3,1},{4,6},{6,4},{5,7},{7,5},{8,10},{10,8},{9,1... | collective-permute-start | bytes 1179656 | tf_op jit(solution)/shard_map/ppermute | solution.py:145
  24.2 4.9 %collective-permute-start.1 = (bf16[4,96,256]{2,1,0:T(8,128)(2,1)S(1)}, bf16[4,96,256]{2,1,0:T(8,128)(2,1)S(1)}, u32[]{:S(2)}, u32[]{:S(2)}) collective-permute-start(bf16[4,96,256]{2,1,0:T(8,128)(2,1)S(1)} %dynamic-slice_bitcast_fusion.2), channel_id=1, source_target_pairs={{0,128},{128,0},{1,129},{129,1},{2,130},{130,2},{3,131},{131,3},{4... | collective-permute-start | bytes 589832 | tf_op jit(solution)/shard_map/ppermute | solution.py:147
  29.2 1.7 %copy-done = bf16[3072,384]{1,0:T(8,128)(2,1)S(1)} copy-done((bf16[3072,384]{1,0:T(8,128)(2,1)S(1)}, bf16[3072,384]{1,0:T(8,128)(2,1)}, u32[]{:S(2)}) %copy-start) | copy-done | bytes 2359320
  30.9 1.2 shard_map.50.pre_ref
  32.0 2.0 %collective-permute-done.1.t1_ref = bf16[4,96,256]{2,1,0:T(8,128)(2,1)S(1)} collective-permute-done((bf16[4,96,256]{2,1,0:T(8,128)(2,1)S(1)}, bf16[4,96,256]{2,1,0:T(8,128)(2,1)S(1)}, u32[]{:S(2)}, u32[]{:S(2)}) %collective-permute-start.1) | collective-permute-done | bytes 196640 | tf_op jit(solution)/shard_map/ppermute | solution.py:147
  34.4 2.9 %collective-permute-start.2 = (bf16[8,96,256]{2,1,0:T(8,128)(2,1)S(1)}, bf16[8,96,256]{2,1,0:T(8,128)(2,1)S(1)}, u32[]{:S(2)}, u32[]{:S(2)}) collective-permute-start(bf16[8,96,256]{2,1,0:T(8,128)(2,1)S(1)} %collective-permute-done.mine_ref), channel_id=1, source_target_pairs={{0,1},{1,0},{2,3},{3,2},{4,5},{5,4},{6,7},{7,6},{8,9},{9,8},{10,11... | collective-permute-start | bytes 1179656 | tf_op jit(solution)/shard_map/ppermute | solution.py:160
  37.3 4.9 %collective-permute-start.3 = (bf16[4,96,256]{2,1,0:T(8,128)(2,1)S(1)}, bf16[4,96,256]{2,1,0:T(8,128)(2,1)S(1)}, u32[]{:S(2)}, u32[]{:S(2)}) collective-permute-start(bf16[4,96,256]{2,1,0:T(8,128)(2,1)S(1)} %dynamic-slice_bitcast_fusion.1), channel_id=1, source_target_pairs={{0,128},{128,0},{1,129},{129,1},{2,130},{130,2},{3,131},{131,3},{4... | collective-permute-start | bytes 589832 | tf_op jit(solution)/shard_map/ppermute | solution.py:161
  42.3 1.4 %shard_map.51 = (bf16[8,2,96,256]{3,2,1,0:T(8,128)(2,1)S(1)}, bf16[256,384]{1,0:T(8,128)(2,1)S(1)}) custom-call(s32[4]{0:T(128)S(1)} %pad_add_fusion.at_ref, bf16[8,96,256]{2,1,0:T(8,128)(2,1)S(1)} %collective-permute-done.mine_ref, bf16[8,96,256]{2,1,0:T(8,128)(2,1)S(1)} %collective-permute-done.2.other_ref, bf16[3072,384]{1,0:T(8,128)(2,1)S(1)} %copy-done.1, ...), custom_call_target="tpu_custom_call" | custom-call | flops 301989888 | bytes 5242880 | tf_op jit(solution)/shard_map/pallas_call | solution.py:162
  43.7 1.9 %collective-permute-start.4 = (bf16[256,384]{1,0:T(8,128)(2,1)S(1)}, bf16[256,384]{1,0:T(8,128)(2,1)S(1)}, u32[]{:S(2)}, u32[]{:S(2)}) collective-permute-start(bf16[256,384]{1,0:T(8,128)(2,1)S(1)} %get-tuple-element.16.pg_ref), channel_id=1, source_target_pairs={{0,128},{128,0},{1,129},{129,1},{2,130},{130,2},{3,131},{131,3},{4... | collective-permute-start | bytes 589832 | tf_op jit(solution)/shard_map/ppermute | solution.py:178
  45.7 1.2 shard_map.53.acc_ref
  47.5 3.8 %shard_map.52 = (f32[16,96,256]{2,1,0:T(8,128)S(1)}, bf16[24,96,256]{2,1,0:T(8,128)(2,1)S(1)}) custom-call(s32[4]{0:T(128)S(1)} %pad_add_fusion.at_ref, bf16[3072,384]{1,0:T(8,128)(2,1)S(1)} %copy-done.1, bf16[256,384]{1,0:T(8,128)(2,1)S(1)} %get-tuple-element.16.pg_ref, bf16[4,96,256]{2,1,0:T(8,128)(2,1)S(1)} %collective-permute-done.1.t1_ref, ...), custom_call_target="tpu_custom_call" | custom-call | flops 603979776 | bytes 5242880 | tf_op jit(solution)/shard_map/pallas_call | solution.py:179
  51.8 3.0 %collective-permute-start.5 = (bf16[24,96,256]{2,1,0:T(8,128)(2,1)S(1)}, bf16[24,96,256]{2,1,0:T(8,128)(2,1)S(1)}, u32[]{:S(2)}, u32[]{:S(2)}) collective-permute-start(bf16[24,96,256]{2,1,0:T(8,128)(2,1)S(1)} %get-tuple-element.21), channel_id=1, source_target_pairs={{0,1},{1,0},{2,3},{3,2},{4,5},{5,4},{6,7},{7,6},{8,9},{9,8},{10,11... | collective-permute-start | bytes 3538952 | tf_op jit(solution)/shard_map/ppermute | solution.py:203
  54.8 2.5 %collective-permute-done.5 = bf16[24,96,256]{2,1,0:T(8,128)(2,1)S(1)} collective-permute-done((bf16[24,96,256]{2,1,0:T(8,128)(2,1)S(1)}, bf16[24,96,256]{2,1,0:T(8,128)(2,1)S(1)}, u32[]{:S(2)}, u32[]{:S(2)}) %collective-permute-start.5) | collective-permute-done | bytes 1179680 | tf_op jit(solution)/shard_map/ppermute | solution.py:203
  57.6 2.2 %collective-permute-start.6 = (bf16[8,96,256]{2,1,0:T(8,128)(2,1)S(1)}, bf16[8,96,256]{2,1,0:T(8,128)(2,1)S(1)}, u32[]{:S(2)}, u32[]{:S(2)}) collective-permute-start(bf16[8,96,256]{2,1,0:T(8,128)(2,1)S(1)} %slice.65), channel_id=1, source_target_pairs={{0,2},{2,0},{1,3},{3,1},{4,6},{6,4},{5,7},{7,5},{8,10},{10,8},{9,1... | collective-permute-start | bytes 1179656 | tf_op jit(solution)/shard_map/ppermute | solution.py:112
  59.8 2.2 %shard_map.55 = bf16[16,96,384]{2,1,0:T(8,128)(2,1)} custom-call(s32[4]{0:T(128)S(1)} %pad_add_fusion.at_ref, f32[16,96,384]{2,1,0:T(8,128)S(1)} %shard_map.53.acc_ref, bf16[4,96,256]{2,1,0:T(8,128)(2,1)S(1)} %collective-permute-done.1.t1_ref, bf16[4,96,256]{2,1,0:T(8,128)(2,1)S(1)} %collective-permute-done.3.t2_ref, ...), custom_call_target="tpu_custom_call" | custom-call | flops 301989888 | bytes 4194304 | tf_op jit(solution)/shard_map/pallas_call | solution.py:206
  62.1 19.7 %all-to-all-start = ((bf16[16,96,384]{2,1,0:T(8,128)(2,1)}), bf16[16,96,384]{2,1,0:T(8,128)(2,1)S(1)}, u32[]{:S(2)}, u32[]{:S(2)}) async-start(bf16[16,96,384]{2,1,0:T(8,128)(2,1)} %shard_map.55), calls=%async_computation | async-start | bytes 2359296 | tf_op jit(solution)/shard_map/all_to_all | solution.py:217
  81.9 1.9 %collective-permute-start.7 = (bf16[4,96,256]{2,1,0:T(8,128)(2,1)S(1)}, bf16[4,96,256]{2,1,0:T(8,128)(2,1)S(1)}, u32[]{:S(2)}, u32[]{:S(2)}) collective-permute-start(bf16[4,96,256]{2,1,0:T(8,128)(2,1)S(1)} %slice.66), channel_id=1, source_target_pairs={{0,4},{4,0},{8,12},{12,8},{16,20},{20,16},{24,28},{28,24},{1,5},{5... | collective-permute-start | bytes 589832 | tf_op jit(solution)/shard_map/ppermute | solution.py:127
  83.8 5.1 %collective-permute-done.7 = bf16[4,96,256]{2,1,0:T(8,128)(2,1)S(1)} collective-permute-done((bf16[4,96,256]{2,1,0:T(8,128)(2,1)S(1)}, bf16[4,96,256]{2,1,0:T(8,128)(2,1)S(1)}, u32[]{:S(2)}, u32[]{:S(2)}) %collective-permute-start.7) | collective-permute-done | bytes 196640 | tf_op jit(solution)/shard_map/ppermute | solution.py:127
  89.1 1.9 %collective-permute-start.8 = (bf16[2,96,256]{2,1,0:T(8,128)(2,1)S(1)}, bf16[2,96,256]{2,1,0:T(8,128)(2,1)S(1)}, u32[]{:S(2)}, u32[]{:S(2)}) collective-permute-start(bf16[2,96,256]{2,1,0:T(8,128)(2,1)S(1)} %slice.67), channel_id=1, source_target_pairs={{0,8},{4,12},{8,0},{12,4},{16,24},{20,28},{24,16},{28,20},{1,9},{5... | collective-permute-start | bytes 294920 | tf_op jit(solution)/shard_map/ppermute | solution.py:127
  91.0 5.7 %collective-permute-done.8 = bf16[2,96,256]{2,1,0:T(8,128)(2,1)S(1)} collective-permute-done((bf16[2,96,256]{2,1,0:T(8,128)(2,1)S(1)}, bf16[2,96,256]{2,1,0:T(8,128)(2,1)S(1)}, u32[]{:S(2)}, u32[]{:S(2)}) %collective-permute-start.8) | collective-permute-done | bytes 98336 | tf_op jit(solution)/shard_map/ppermute | solution.py:127
  96.7 4.4 %collective-permute-start.9 = (bf16[1,96,256]{2,1,0:T(8,128)(2,1)S(1)}, bf16[1,96,256]{2,1,0:T(8,128)(2,1)S(1)}, u32[]{:S(2)}, u32[]{:S(2)}) collective-permute-start(bf16[1,96,256]{2,1,0:T(8,128)(2,1)S(1)} %slice.68), channel_id=1, source_target_pairs={{0,16},{4,20},{8,24},{12,28},{16,0},{20,4},{24,8},{28,12},{1,17},{... | collective-permute-start | bytes 147464 | tf_op jit(solution)/shard_map/ppermute | solution.py:127
  101.2 4.6 %collective-permute-done.9 = bf16[1,96,256]{2,1,0:T(8,128)(2,1)S(1)} collective-permute-done((bf16[1,96,256]{2,1,0:T(8,128)(2,1)S(1)}, bf16[1,96,256]{2,1,0:T(8,128)(2,1)S(1)}, u32[]{:S(2)}, u32[]{:S(2)}) %collective-permute-start.9) | collective-permute-done | bytes 49184 | tf_op jit(solution)/shard_map/ppermute | solution.py:127
  106.4 13.7 %all-to-all-done = bf16[16,96,384]{2,1,0:T(8,128)(2,1)S(1)} async-done(((bf16[16,96,384]{2,1,0:T(8,128)(2,1)}), bf16[16,96,384]{2,1,0:T(8,128)(2,1)S(1)}, u32[]{:S(2)}, u32[]{:S(2)}) %all-to-all-start) | async-done | bytes 1179680 | tf_op jit(solution)/shard_map/all_to_all | solution.py:217
  (26 shorter events, 3.7 us)
Async XLA Ops:
  22.0 12.5 %collective-permute-start = (bf16[8,96,256]{2,1,0:T(8,128)(2,1)S(1)}, bf16[8,96,256]{2,1,0:T(8,128)(2,1)S(1)}, u32[]{:S(2)}, u32[]{:S(2)}) collective-permute-start(bf16[8,96,256]{2,1,0:T(8,128)(2,1)S(1)} %dynamic-slice_bitcast_fusion), channel_id=1, source_target_pairs={{0,2},{2,0},{1,3},{3,1},{4,6},{6,4},{5,7},{7,5},{8,10},{10,8},{9,1... | collective-permute-start | bytes 1179656 | tf_op jit(solution)/shard_map/ppermute | solution.py:145
  24.2 9.8 %collective-permute-start.1 = (bf16[4,96,256]{2,1,0:T(8,128)(2,1)S(1)}, bf16[4,96,256]{2,1,0:T(8,128)(2,1)S(1)}, u32[]{:S(2)}, u32[]{:S(2)}) collective-permute-start(bf16[4,96,256]{2,1,0:T(8,128)(2,1)S(1)} %dynamic-slice_bitcast_fusion.2), channel_id=1, source_target_pairs={{0,128},{128,0},{1,129},{129,1},{2,130},{130,2},{3,131},{131,3},{4... | collective-permute-start | bytes 589832 | tf_op jit(solution)/shard_map/ppermute | solution.py:147
  29.2 1.7 %copy-start = (bf16[3072,384]{1,0:T(8,128)(2,1)S(1)}, bf16[3072,384]{1,0:T(8,128)(2,1)}, u32[]{:S(2)}) copy-start(bf16[3072,384]{1,0:T(8,128)(2,1)} %w_ref.5) | copy-start | bytes 7077892
  30.9 11.4 %copy-start.1 = (bf16[3072,384]{1,0:T(8,128)(2,1)S(1)}, bf16[3072,384]{1,0:T(8,128)(2,1)}, u32[]{:S(2)}) copy-start(bf16[3072,384]{1,0:T(8,128)(2,1)} %w_ref.5) | copy-start | bytes 7077892
  30.9 11.4 %copy-start.2 = (bf16[256,384]{1,0:T(8,128)(2,1)S(1)}, bf16[256,384]{1,0:T(8,128)(2,1)}, u32[]{:S(2)}) copy-start(bf16[256,384]{1,0:T(8,128)(2,1)} %g_ref.1) | copy-start | bytes 589828
  34.4 7.8 %collective-permute-start.2 = (bf16[8,96,256]{2,1,0:T(8,128)(2,1)S(1)}, bf16[8,96,256]{2,1,0:T(8,128)(2,1)S(1)}, u32[]{:S(2)}, u32[]{:S(2)}) collective-permute-start(bf16[8,96,256]{2,1,0:T(8,128)(2,1)S(1)} %collective-permute-done.mine_ref), channel_id=1, source_target_pairs={{0,1},{1,0},{2,3},{3,2},{4,5},{5,4},{6,7},{7,6},{8,9},{9,8},{10,11... | collective-permute-start | bytes 1179656 | tf_op jit(solution)/shard_map/ppermute | solution.py:160
  37.3 10.2 %collective-permute-start.3 = (bf16[4,96,256]{2,1,0:T(8,128)(2,1)S(1)}, bf16[4,96,256]{2,1,0:T(8,128)(2,1)S(1)}, u32[]{:S(2)}, u32[]{:S(2)}) collective-permute-start(bf16[4,96,256]{2,1,0:T(8,128)(2,1)S(1)} %dynamic-slice_bitcast_fusion.1), channel_id=1, source_target_pairs={{0,128},{128,0},{1,129},{129,1},{2,130},{130,2},{3,131},{131,3},{4... | collective-permute-start | bytes 589832 | tf_op jit(solution)/shard_map/ppermute | solution.py:161
  43.7 8.1 %collective-permute-start.4 = (bf16[256,384]{1,0:T(8,128)(2,1)S(1)}, bf16[256,384]{1,0:T(8,128)(2,1)S(1)}, u32[]{:S(2)}, u32[]{:S(2)}) collective-permute-start(bf16[256,384]{1,0:T(8,128)(2,1)S(1)} %get-tuple-element.16.pg_ref), channel_id=1, source_target_pairs={{0,128},{128,0},{1,129},{129,1},{2,130},{130,2},{3,131},{131,3},{4... | collective-permute-start | bytes 589832 | tf_op jit(solution)/shard_map/ppermute | solution.py:178
  51.8 5.5 %collective-permute-start.5 = (bf16[24,96,256]{2,1,0:T(8,128)(2,1)S(1)}, bf16[24,96,256]{2,1,0:T(8,128)(2,1)S(1)}, u32[]{:S(2)}, u32[]{:S(2)}) collective-permute-start(bf16[24,96,256]{2,1,0:T(8,128)(2,1)S(1)} %get-tuple-element.21), channel_id=1, source_target_pairs={{0,1},{1,0},{2,3},{3,2},{4,5},{5,4},{6,7},{7,6},{8,9},{9,8},{10,11... | collective-permute-start | bytes 3538952 | tf_op jit(solution)/shard_map/ppermute | solution.py:203
  57.6 24.2 %collective-permute-start.6 = (bf16[8,96,256]{2,1,0:T(8,128)(2,1)S(1)}, bf16[8,96,256]{2,1,0:T(8,128)(2,1)S(1)}, u32[]{:S(2)}, u32[]{:S(2)}) collective-permute-start(bf16[8,96,256]{2,1,0:T(8,128)(2,1)S(1)} %slice.65), channel_id=1, source_target_pairs={{0,2},{2,0},{1,3},{3,1},{4,6},{6,4},{5,7},{7,5},{8,10},{10,8},{9,1... | collective-permute-start | bytes 1179656 | tf_op jit(solution)/shard_map/ppermute | solution.py:112
  62.1 58.0 %all-to-all-start = ((bf16[16,96,384]{2,1,0:T(8,128)(2,1)}), bf16[16,96,384]{2,1,0:T(8,128)(2,1)S(1)}, u32[]{:S(2)}, u32[]{:S(2)}) async-start(bf16[16,96,384]{2,1,0:T(8,128)(2,1)} %shard_map.55), calls=%async_computation | async-start | bytes 2359296 | tf_op jit(solution)/shard_map/all_to_all | solution.py:217
  81.9 7.1 %collective-permute-start.7 = (bf16[4,96,256]{2,1,0:T(8,128)(2,1)S(1)}, bf16[4,96,256]{2,1,0:T(8,128)(2,1)S(1)}, u32[]{:S(2)}, u32[]{:S(2)}) collective-permute-start(bf16[4,96,256]{2,1,0:T(8,128)(2,1)S(1)} %slice.66), channel_id=1, source_target_pairs={{0,4},{4,0},{8,12},{12,8},{16,20},{20,16},{24,28},{28,24},{1,5},{5... | collective-permute-start | bytes 589832 | tf_op jit(solution)/shard_map/ppermute | solution.py:127
  89.1 7.6 %collective-permute-start.8 = (bf16[2,96,256]{2,1,0:T(8,128)(2,1)S(1)}, bf16[2,96,256]{2,1,0:T(8,128)(2,1)S(1)}, u32[]{:S(2)}, u32[]{:S(2)}) collective-permute-start(bf16[2,96,256]{2,1,0:T(8,128)(2,1)S(1)} %slice.67), channel_id=1, source_target_pairs={{0,8},{4,12},{8,0},{12,4},{16,24},{20,28},{24,16},{28,20},{1,9},{5... | collective-permute-start | bytes 294920 | tf_op jit(solution)/shard_map/ppermute | solution.py:127
  96.7 9.0 %collective-permute-start.9 = (bf16[1,96,256]{2,1,0:T(8,128)(2,1)S(1)}, bf16[1,96,256]{2,1,0:T(8,128)(2,1)S(1)}, u32[]{:S(2)}, u32[]{:S(2)}) collective-permute-start(bf16[1,96,256]{2,1,0:T(8,128)(2,1)S(1)} %slice.68), channel_id=1, source_target_pairs={{0,16},{4,20},{8,24},{12,28},{16,0},{20,4},{24,8},{28,12},{1,17},{... | collective-permute-start | bytes 147464 | tf_op jit(solution)/shard_map/ppermute | solution.py:127

commit v8 on v7

--- a/solution.py
+++ b/solution.py
@@ -74,7 +74,7 @@
             @pl.when(core == c)
             def _():
                 for x in range(2):
-                    to = lax.bitwise_xor(xl, jnp.int32(x)) * ny + at
+                    to = 2 * at + lax.bitwise_xor(xl, jnp.int32(x))
                     for ref, b in ((keep_ref, 2 * x + c), (send_ref, 2 * x + 1 - c)):
                         part = block[b * feats : (b + 1) * feats]
                         ref[to] = part.astype(ref.dtype)
@@ -215,11 +215,12 @@
         )(at, acc, t1, t2, tother, pair_grad)
         wpart = wpart.reshape(nh * nx, -1, hidden)
         pieces = lax.all_to_all(wpart, ("zh", "xh"), 0, 0, tiled=True)
-        total = halve_early(total, "xl", PAIR)
-        bit = 1
+        total = halve_early(total, "y", [(i, i ^ 1) for i in range(ny)])
+        bit = 2
         while bit < ny:
             total = halve(total, "y", [(i, i ^ bit) for i in range(ny)])
             bit *= 2
+        total = halve(total, "xl", PAIR)
         weight_sum = jnp.sum(pieces.astype(F32), axis=0)
         return (total[0].astype(BF16).T, weight_sum.astype(BF16))
 

time: 121 us -> 122 us (level)
  the two profiles are of different devices: /device:TPU:7 before, /device:TPU:1 now
where the time goes in v8:
time: 122 us; the launch traced here: 121 us
  starting transfers between devices  40.9 us (34%)
  waiting for transfers between devices  34.8 us (29%)
  blocking collectives  31.1 us (25%)
  Pallas kernels  9.92 us (8%)
  local copies, waits for them, and re-layouts  1.93 us (2%)
  other arithmetic  1.76 us (1%)
    all_gather x1, blocking collectives, local(): lax.all_gather(tokens.T, ('y', 'c'), axis=0).reshape(ny, 2, feats, rows)  31.1 us
    ppermute x3, waiting for transfers between devices, halve(): arrived = lax.ppermute(total[half:].astype(BF16), axis, pairs)  16.7 us
    all_to_all x1, starting transfers between devices, local(): pieces = lax.all_to_all(wpart, ('zh', 'xh'), 0, 0, tiled=True)  11.7 us
    ppermute x3, starting transfers between devices, halve(): arrived = lax.ppermute(total[half:].astype(BF16), axis, pairs)  11.5 us
    all_to_all x1, waiting for transfers between devices, local(): pieces = lax.all_to_all(wpart, ('zh', 'xh'), 0, 0, tiled=True)  9.16 us
    pallas_call x1, Pallas kernels, local(): pl.pallas_call(input_kernel, out_shape=(jax.ShapeDtypeStruct((2 * ny, fea...  3.83 us
    ppermute x1, waiting for transfers between devices, local(): t1 = lax.ppermute(t1, 'zl', PAIR)  3.39 us
    ppermute x1, starting transfers between devices, local(): pair_grad = lax.ppermute(pre_grad, 'zl', PAIR)  3.36 us
  transfers between devices with their start and end apart: 11, of which 9 were waited for; matrix products, arithmetic and copies ran while one was open for 1% of the time, Pallas kernels for 8%

profile of v8, /device:TPU:1, one launch (start us, length us, event | category | flops | bytes accessed | tf_op | source)
XLA Modules:
  0.0 121.3 jit_solution(1258749284045627250)
XLA Ops:
  0.6 31.1 %all-gather = bf16[1536,256]{1,0:T(8,128)(2,1)S(1)} all-gather(bf16[96,256]{1,0:T(8,128)(2,1)} %bitcast.27), channel_id=2, replica_groups=mesh['zh'=4,'zl'=2,'xh'=4,'y'=8,'xl'=2,'c'=2] {'y','c'}, dimensions={0}, use_global_device_ids=true | all-gather | bytes 835584 | tf_op jit(solution)/shard_map/all_gather | solution.py:143
  31.8 1.9 %collective-permute-start = (bf16[8,96,256]{2,1,0:T(8,128)(2,1)S(1)}, bf16[8,96,256]{2,1,0:T(8,128)(2,1)S(1)}, u32[]{:S(2)}, u32[]{:S(2)}) collective-permute-start(bf16[8,96,256]{2,1,0:T(8,128)(2,1)S(1)} %dynamic-slice_bitcast_fusion), channel_id=1, source_target_pairs={{0,2},{2,0},{1,3},{3,1},{4,6},{6,4},{5,7},{7,5},{8,10},{10,8},{9,1... | collective-permute-start | bytes 1179656 | tf_op jit(solution)/shard_map/ppermute | solution.py:145
  33.7 1.9 %collective-permute-start.1 = (bf16[4,96,256]{2,1,0:T(8,128)(2,1)S(1)}, bf16[4,96,256]{2,1,0:T(8,128)(2,1)S(1)}, u32[]{:S(2)}, u32[]{:S(2)}) collective-permute-start(bf16[4,96,256]{2,1,0:T(8,128)(2,1)S(1)} %dynamic-slice_bitcast_fusion.2), channel_id=1, source_target_pairs={{0,128},{128,0},{1,129},{129,1},{2,130},{130,2},{3,131},{131,3},{4... | collective-permute-start | bytes 589832 | tf_op jit(solution)/shard_map/ppermute | solution.py:147
  35.8 1.7 %copy-done = bf16[3072,384]{1,0:T(8,128)(2,1)S(1)} copy-done((bf16[3072,384]{1,0:T(8,128)(2,1)S(1)}, bf16[3072,384]{1,0:T(8,128)(2,1)}, u32[]{:S(2)}) %copy-start) | copy-done | bytes 2359320
  38.6 3.4 %collective-permute-done.1.t1_ref = bf16[4,96,256]{2,1,0:T(8,128)(2,1)S(1)} collective-permute-done((bf16[4,96,256]{2,1,0:T(8,128)(2,1)S(1)}, bf16[4,96,256]{2,1,0:T(8,128)(2,1)S(1)}, u32[]{:S(2)}, u32[]{:S(2)}) %collective-permute-start.1) | collective-permute-done | bytes 196640 | tf_op jit(solution)/shard_map/ppermute | solution.py:147
  42.0 2.2 %collective-permute-done.mine_ref = bf16[8,96,256]{2,1,0:T(8,128)(2,1)S(1)} collective-permute-done((bf16[8,96,256]{2,1,0:T(8,128)(2,1)S(1)}, bf16[8,96,256]{2,1,0:T(8,128)(2,1)S(1)}, u32[]{:S(2)}, u32[]{:S(2)}) %collective-permute-start) | collective-permute-done | bytes 393248 | tf_op jit(solution)/shard_map/ppermute | solution.py:145
  44.2 2.9 %collective-permute-start.2 = (bf16[8,96,256]{2,1,0:T(8,128)(2,1)S(1)}, bf16[8,96,256]{2,1,0:T(8,128)(2,1)S(1)}, u32[]{:S(2)}, u32[]{:S(2)}) collective-permute-start(bf16[8,96,256]{2,1,0:T(8,128)(2,1)S(1)} %collective-permute-done.mine_ref), channel_id=1, source_target_pairs={{0,1},{1,0},{2,3},{3,2},{4,5},{5,4},{6,7},{7,6},{8,9},{9,8},{10,11... | collective-permute-start | bytes 1179656 | tf_op jit(solution)/shard_map/ppermute | solution.py:160
  47.1 1.9 %collective-permute-start.3 = (bf16[4,96,256]{2,1,0:T(8,128)(2,1)S(1)}, bf16[4,96,256]{2,1,0:T(8,128)(2,1)S(1)}, u32[]{:S(2)}, u32[]{:S(2)}) collective-permute-start(bf16[4,96,256]{2,1,0:T(8,128)(2,1)S(1)} %dynamic-slice_bitcast_fusion.1), channel_id=1, source_target_pairs={{0,128},{128,0},{1,129},{129,1},{2,130},{130,2},{3,131},{131,3},{4... | collective-permute-start | bytes 589832 | tf_op jit(solution)/shard_map/ppermute | solution.py:161
  49.1 1.4 %shard_map.51 = (bf16[8,2,96,256]{3,2,1,0:T(8,128)(2,1)S(1)}, bf16[256,384]{1,0:T(8,128)(2,1)S(1)}) custom-call(s32[4]{0:T(128)S(1)} %pad_add_fusion.at_ref, bf16[8,96,256]{2,1,0:T(8,128)(2,1)S(1)} %collective-permute-done.mine_ref, bf16[8,96,256]{2,1,0:T(8,128)(2,1)S(1)} %collective-permute-done.2.other_ref, bf16[3072,384]{1,0:T(8,128)(2,1)S(1)} %copy-done.1, ...), custom_call_target="tpu_custom_call" | custom-call | flops 301989888 | bytes 5242880 | tf_op jit(solution)/shard_map/pallas_call | solution.py:162
  50.5 3.4 %collective-permute-start.4 = (bf16[256,384]{1,0:T(8,128)(2,1)S(1)}, bf16[256,384]{1,0:T(8,128)(2,1)S(1)}, u32[]{:S(2)}, u32[]{:S(2)}) collective-permute-start(bf16[256,384]{1,0:T(8,128)(2,1)S(1)} %get-tuple-element.16.pg_ref), channel_id=1, source_target_pairs={{0,128},{128,0},{1,129},{129,1},{2,130},{130,2},{3,131},{131,3},{4... | collective-permute-start | bytes 589832 | tf_op jit(solution)/shard_map/ppermute | solution.py:178
  53.9 1.2 shard_map.53.acc_ref
  55.5 3.8 %shard_map.52 = (f32[16,96,256]{2,1,0:T(8,128)S(1)}, bf16[24,96,256]{2,1,0:T(8,128)(2,1)S(1)}) custom-call(s32[4]{0:T(128)S(1)} %pad_add_fusion.at_ref, bf16[3072,384]{1,0:T(8,128)(2,1)S(1)} %copy-done.1, bf16[256,384]{1,0:T(8,128)(2,1)S(1)} %get-tuple-element.16.pg_ref, bf16[4,96,256]{2,1,0:T(8,128)(2,1)S(1)} %collective-permute-done.1.t1_ref, ...), custom_call_target="tpu_custom_call" | custom-call | flops 603979776 | bytes 5242880 | tf_op jit(solution)/shard_map/pallas_call | solution.py:179
  59.8 2.7 %collective-permute-start.5 = (bf16[24,96,256]{2,1,0:T(8,128)(2,1)S(1)}, bf16[24,96,256]{2,1,0:T(8,128)(2,1)S(1)}, u32[]{:S(2)}, u32[]{:S(2)}) collective-permute-start(bf16[24,96,256]{2,1,0:T(8,128)(2,1)S(1)} %get-tuple-element.21), channel_id=1, source_target_pairs={{0,1},{1,0},{2,3},{3,2},{4,5},{5,4},{6,7},{7,6},{8,9},{9,8},{10,11... | collective-permute-start | bytes 3538952 | tf_op jit(solution)/shard_map/ppermute | solution.py:203
  62.5 2.5 %collective-permute-done.5 = bf16[24,96,256]{2,1,0:T(8,128)(2,1)S(1)} collective-permute-done((bf16[24,96,256]{2,1,0:T(8,128)(2,1)S(1)}, bf16[24,96,256]{2,1,0:T(8,128)(2,1)S(1)}, u32[]{:S(2)}, u32[]{:S(2)}) %collective-permute-start.5) | collective-permute-done | bytes 1179680 | tf_op jit(solution)/shard_map/ppermute | solution.py:203
  65.2 3.0 %collective-permute-start.6 = (bf16[8,96,256]{2,1,0:T(8,128)(2,1)S(1)}, bf16[8,96,256]{2,1,0:T(8,128)(2,1)S(1)}, u32[]{:S(2)}, u32[]{:S(2)}) collective-permute-start(bf16[8,96,256]{2,1,0:T(8,128)(2,1)S(1)} %slice.65), channel_id=1, source_target_pairs={{0,4},{4,0},{8,12},{12,8},{16,20},{20,16},{24,28},{28,24},{1,5},{5... | collective-permute-start | bytes 1179656 | tf_op jit(solution)/shard_map/ppermute | solution.py:112
  68.3 2.2 %shard_map.55 = bf16[16,96,384]{2,1,0:T(8,128)(2,1)} custom-call(s32[4]{0:T(128)S(1)} %pad_add_fusion.at_ref, f32[16,96,384]{2,1,0:T(8,128)S(1)} %shard_map.53.acc_ref, bf16[4,96,256]{2,1,0:T(8,128)(2,1)S(1)} %collective-permute-done.1.t1_ref, bf16[4,96,256]{2,1,0:T(8,128)(2,1)S(1)} %collective-permute-done.3.t2_ref, ...), custom_call_target="tpu_custom_call" | custom-call | flops 301989888 | bytes 4194304 | tf_op jit(solution)/shard_map/pallas_call | solution.py:206
  70.6 11.7 %all-to-all-start = ((bf16[16,96,384]{2,1,0:T(8,128)(2,1)}), bf16[16,96,384]{2,1,0:T(8,128)(2,1)S(1)}, u32[]{:S(2)}, u32[]{:S(2)}) async-start(bf16[16,96,384]{2,1,0:T(8,128)(2,1)} %shard_map.55), calls=%async_computation | async-start | bytes 2359296 | tf_op jit(solution)/shard_map/all_to_all | solution.py:217
  82.4 3.2 %collective-permute-start.7 = (bf16[4,96,256]{2,1,0:T(8,128)(2,1)S(1)}, bf16[4,96,256]{2,1,0:T(8,128)(2,1)S(1)}, u32[]{:S(2)}, u32[]{:S(2)}) collective-permute-start(bf16[4,96,256]{2,1,0:T(8,128)(2,1)S(1)} %slice.66), channel_id=1, source_target_pairs={{0,8},{4,12},{8,0},{12,4},{16,24},{20,28},{24,16},{28,20},{1,9},{5... | collective-permute-start | bytes 589832 | tf_op jit(solution)/shard_map/ppermute | solution.py:127
  85.6 9.6 %collective-permute-done.7 = bf16[4,96,256]{2,1,0:T(8,128)(2,1)S(1)} collective-permute-done((bf16[4,96,256]{2,1,0:T(8,128)(2,1)S(1)}, bf16[4,96,256]{2,1,0:T(8,128)(2,1)S(1)}, u32[]{:S(2)}, u32[]{:S(2)}) %collective-permute-start.7) | collective-permute-done | bytes 196640 | tf_op jit(solution)/shard_map/ppermute | solution.py:127
  95.2 6.1 %collective-permute-start.8 = (bf16[2,96,256]{2,1,0:T(8,128)(2,1)S(1)}, bf16[2,96,256]{2,1,0:T(8,128)(2,1)S(1)}, u32[]{:S(2)}, u32[]{:S(2)}) collective-permute-start(bf16[2,96,256]{2,1,0:T(8,128)(2,1)S(1)} %slice.67), channel_id=1, source_target_pairs={{0,16},{4,20},{8,24},{12,28},{16,0},{20,4},{24,8},{28,12},{1,17},{... | collective-permute-start | bytes 294920 | tf_op jit(solution)/shard_map/ppermute | solution.py:127
  101.3 3.5 %collective-permute-done.8 = bf16[2,96,256]{2,1,0:T(8,128)(2,1)S(1)} collective-permute-done((bf16[2,96,256]{2,1,0:T(8,128)(2,1)S(1)}, bf16[2,96,256]{2,1,0:T(8,128)(2,1)S(1)}, u32[]{:S(2)}, u32[]{:S(2)}) %collective-permute-start.8) | collective-permute-done | bytes 98336 | tf_op jit(solution)/shard_map/ppermute | solution.py:127
  104.8 2.2 %collective-permute-start.9 = (bf16[1,96,256]{2,1,0:T(8,128)(2,1)S(1)}, bf16[1,96,256]{2,1,0:T(8,128)(2,1)S(1)}, u32[]{:S(2)}, u32[]{:S(2)}) collective-permute-start(bf16[1,96,256]{2,1,0:T(8,128)(2,1)S(1)} %slice.68), channel_id=1, source_target_pairs={{0,2},{2,0},{1,3},{3,1},{4,6},{6,4},{5,7},{7,5},{8,10},{10,8},{9,1... | collective-permute-start | bytes 147464 | tf_op jit(solution)/shard_map/ppermute | solution.py:127
  107.1 3.7 %collective-permute-done.9 = bf16[1,96,256]{2,1,0:T(8,128)(2,1)S(1)} collective-permute-done((bf16[1,96,256]{2,1,0:T(8,128)(2,1)S(1)}, bf16[1,96,256]{2,1,0:T(8,128)(2,1)S(1)}, u32[]{:S(2)}, u32[]{:S(2)}) %collective-permute-start.9) | collective-permute-done | bytes 49184 | tf_op jit(solution)/shard_map/ppermute | solution.py:127
  111.4 9.2 %all-to-all-done = bf16[16,96,384]{2,1,0:T(8,128)(2,1)S(1)} async-done(((bf16[16,96,384]{2,1,0:T(8,128)(2,1)}), bf16[16,96,384]{2,1,0:T(8,128)(2,1)S(1)}, u32[]{:S(2)}, u32[]{:S(2)}) %all-to-all-start) | async-done | bytes 1179680 | tf_op jit(solution)/shard_map/all_to_all | solution.py:217
  (26 shorter events, 4.1 us)
Async XLA Ops:
  31.8 12.5 %collective-permute-start = (bf16[8,96,256]{2,1,0:T(8,128)(2,1)S(1)}, bf16[8,96,256]{2,1,0:T(8,128)(2,1)S(1)}, u32[]{:S(2)}, u32[]{:S(2)}) collective-permute-start(bf16[8,96,256]{2,1,0:T(8,128)(2,1)S(1)} %dynamic-slice_bitcast_fusion), channel_id=1, source_target_pairs={{0,2},{2,0},{1,3},{3,1},{4,6},{6,4},{5,7},{7,5},{8,10},{10,8},{9,1... | collective-permute-start | bytes 1179656 | tf_op jit(solution)/shard_map/ppermute | solution.py:145
  33.7 8.2 %collective-permute-start.1 = (bf16[4,96,256]{2,1,0:T(8,128)(2,1)S(1)}, bf16[4,96,256]{2,1,0:T(8,128)(2,1)S(1)}, u32[]{:S(2)}, u32[]{:S(2)}) collective-permute-start(bf16[4,96,256]{2,1,0:T(8,128)(2,1)S(1)} %dynamic-slice_bitcast_fusion.2), channel_id=1, source_target_pairs={{0,128},{128,0},{1,129},{129,1},{2,130},{130,2},{3,131},{131,3},{4... | collective-permute-start | bytes 589832 | tf_op jit(solution)/shard_map/ppermute | solution.py:147
  35.8 1.7 %copy-start = (bf16[3072,384]{1,0:T(8,128)(2,1)S(1)}, bf16[3072,384]{1,0:T(8,128)(2,1)}, u32[]{:S(2)}) copy-start(bf16[3072,384]{1,0:T(8,128)(2,1)} %w_ref.5) | copy-start | bytes 7077892
  37.4 11.6 %copy-start.1 = (bf16[3072,384]{1,0:T(8,128)(2,1)S(1)}, bf16[3072,384]{1,0:T(8,128)(2,1)}, u32[]{:S(2)}) copy-start(bf16[3072,384]{1,0:T(8,128)(2,1)} %w_ref.5) | copy-start | bytes 7077892
  37.4 11.7 %copy-start.2 = (bf16[256,384]{1,0:T(8,128)(2,1)S(1)}, bf16[256,384]{1,0:T(8,128)(2,1)}, u32[]{:S(2)}) copy-start(bf16[256,384]{1,0:T(8,128)(2,1)} %g_ref.1) | copy-start | bytes 589828
  44.2 4.8 %collective-permute-start.2 = (bf16[8,96,256]{2,1,0:T(8,128)(2,1)S(1)}, bf16[8,96,256]{2,1,0:T(8,128)(2,1)S(1)}, u32[]{:S(2)}, u32[]{:S(2)}) collective-permute-start(bf16[8,96,256]{2,1,0:T(8,128)(2,1)S(1)} %collective-permute-done.mine_ref), channel_id=1, source_target_pairs={{0,1},{1,0},{2,3},{3,2},{4,5},{5,4},{6,7},{7,6},{8,9},{9,8},{10,11... | collective-permute-start | bytes 1179656 | tf_op jit(solution)/shard_map/ppermute | solution.py:160
  47.1 8.4 %collective-permute-start.3 = (bf16[4,96,256]{2,1,0:T(8,128)(2,1)S(1)}, bf16[4,96,256]{2,1,0:T(8,128)(2,1)S(1)}, u32[]{:S(2)}, u32[]{:S(2)}) collective-permute-start(bf16[4,96,256]{2,1,0:T(8,128)(2,1)S(1)} %dynamic-slice_bitcast_fusion.1), channel_id=1, source_target_pairs={{0,128},{128,0},{1,129},{129,1},{2,130},{130,2},{3,131},{131,3},{4... | collective-permute-start | bytes 589832 | tf_op jit(solution)/shard_map/ppermute | solution.py:161
  50.5 9.2 %collective-permute-start.4 = (bf16[256,384]{1,0:T(8,128)(2,1)S(1)}, bf16[256,384]{1,0:T(8,128)(2,1)S(1)}, u32[]{:S(2)}, u32[]{:S(2)}) collective-permute-start(bf16[256,384]{1,0:T(8,128)(2,1)S(1)} %get-tuple-element.16.pg_ref), channel_id=1, source_target_pairs={{0,128},{128,0},{1,129},{129,1},{2,130},{130,2},{3,131},{131,3},{4... | collective-permute-start | bytes 589832 | tf_op jit(solution)/shard_map/ppermute | solution.py:178
  59.8 5.2 %collective-permute-start.5 = (bf16[24,96,256]{2,1,0:T(8,128)(2,1)S(1)}, bf16[24,96,256]{2,1,0:T(8,128)(2,1)S(1)}, u32[]{:S(2)}, u32[]{:S(2)}) collective-permute-start(bf16[24,96,256]{2,1,0:T(8,128)(2,1)S(1)} %get-tuple-element.21), channel_id=1, source_target_pairs={{0,1},{1,0},{2,3},{3,2},{4,5},{5,4},{6,7},{7,6},{8,9},{9,8},{10,11... | collective-permute-start | bytes 3538952 | tf_op jit(solution)/shard_map/ppermute | solution.py:203
  65.2 17.1 %collective-permute-start.6 = (bf16[8,96,256]{2,1,0:T(8,128)(2,1)S(1)}, bf16[8,96,256]{2,1,0:T(8,128)(2,1)S(1)}, u32[]{:S(2)}, u32[]{:S(2)}) collective-permute-start(bf16[8,96,256]{2,1,0:T(8,128)(2,1)S(1)} %slice.65), channel_id=1, source_target_pairs={{0,4},{4,0},{8,12},{12,8},{16,20},{20,16},{24,28},{28,24},{1,5},{5... | collective-permute-start | bytes 1179656 | tf_op jit(solution)/shard_map/ppermute | solution.py:112
  70.6 50.0 %all-to-all-start = ((bf16[16,96,384]{2,1,0:T(8,128)(2,1)}), bf16[16,96,384]{2,1,0:T(8,128)(2,1)S(1)}, u32[]{:S(2)}, u32[]{:S(2)}) async-start(bf16[16,96,384]{2,1,0:T(8,128)(2,1)} %shard_map.55), calls=%async_computation | async-start | bytes 2359296 | tf_op jit(solution)/shard_map/all_to_all | solution.py:217
  82.4 12.8 %collective-permute-start.7 = (bf16[4,96,256]{2,1,0:T(8,128)(2,1)S(1)}, bf16[4,96,256]{2,1,0:T(8,128)(2,1)S(1)}, u32[]{:S(2)}, u32[]{:S(2)}) collective-permute-start(bf16[4,96,256]{2,1,0:T(8,128)(2,1)S(1)} %slice.66), channel_id=1, source_target_pairs={{0,8},{4,12},{8,0},{12,4},{16,24},{20,28},{24,16},{28,20},{1,9},{5... | collective-permute-start | bytes 589832 | tf_op jit(solution)/shard_map/ppermute | solution.py:127
  95.2 9.6 %collective-permute-start.8 = (bf16[2,96,256]{2,1,0:T(8,128)(2,1)S(1)}, bf16[2,96,256]{2,1,0:T(8,128)(2,1)S(1)}, u32[]{:S(2)}, u32[]{:S(2)}) collective-permute-start(bf16[2,96,256]{2,1,0:T(8,128)(2,1)S(1)} %slice.67), channel_id=1, source_target_pairs={{0,16},{4,20},{8,24},{12,28},{16,0},{20,4},{24,8},{28,12},{1,17},{... | collective-permute-start | bytes 294920 | tf_op jit(solution)/shard_map/ppermute | solution.py:127
  104.8 5.9 %collective-permute-start.9 = (bf16[1,96,256]{2,1,0:T(8,128)(2,1)S(1)}, bf16[1,96,256]{2,1,0:T(8,128)(2,1)S(1)}, u32[]{:S(2)}, u32[]{:S(2)}) collective-permute-start(bf16[1,96,256]{2,1,0:T(8,128)(2,1)S(1)} %slice.68), channel_id=1, source_target_pairs={{0,2},{2,0},{1,3},{3,1},{4,6},{6,4},{5,7},{7,5},{8,10},{10,8},{9,1... | collective-permute-start | bytes 147464 | tf_op jit(solution)/shard_map/ppermute | solution.py:127

commit v9 on v7

--- a/solution.py
+++ b/solution.py
@@ -59,14 +59,14 @@
     bits = ny.bit_length() - 1
     send_ref[2 * ny : 2 * ny + nh] = t1_ref[...]
     send_ref[2 * ny + nh :] = t2_ref[...]
-    pg = pg_ref[...]
+    pg_t = pg_ref[...].T
     for r in range(ny):
         at = sum((r >> k & 1) << (bits - 1 - k) for k in range(bits))
         start = lax.bitwise_xor(y_own, jnp.int32(r)) * (4 * feats)
         block = lax.dot_general(
             w_ref[pl.ds(pl.multiple_of(start, 4 * feats), 4 * feats), :],
-            pg,
-            (((1,), (1,)), ((), ())),
+            pg_t,
+            (((1,), (0,)), ((), ())),
             preferred_element_type=F32,
         )
         for c in range(2):

time: 121 us -> 121 us (level)
  no operation moved by 1% of the time
where the time goes in v9:
time: 121 us
  starting transfers between devices  50 us (41%)
  waiting for transfers between devices  35.1 us (29%)
  blocking collectives  21.3 us (18%)
  Pallas kernels  9.92 us (8%)
  local copies, waits for them, and re-layouts  1.93 us (2%)
  other arithmetic  1.76 us (1%)
    all_gather x1, blocking collectives, local(): lax.all_gather(tokens.T, ('y', 'c'), axis=0).reshape(ny, 2, feats, rows)  21.3 us
    all_to_all x1, starting transfers between devices, local(): pieces = lax.all_to_all(wpart, ('zh', 'xh'), 0, 0, tiled=True)  19.7 us
    ppermute x3, waiting for transfers between devices, halve(): arrived = lax.ppermute(total[half:].astype(BF16), axis, pairs)  15.4 us
    all_to_all x1, waiting for transfers between devices, local(): pieces = lax.all_to_all(wpart, ('zh', 'xh'), 0, 0, tiled=True)  13.7 us
    ppermute x3, starting transfers between devices, halve(): arrived = lax.ppermute(total[half:].astype(BF16), axis, pairs)  8.28 us
    ppermute x1, starting transfers between devices, local(): t1 = lax.ppermute(t1, 'zl', PAIR)  4.91 us
    ppermute x1, starting transfers between devices, local(): lax.ppermute(pick(mine.reshape(nh, 2, feats, rows), 1 - zl, 1), 'zl', PAIR)  4.91 us
    pallas_call x1, Pallas kernels, local(): pl.pallas_call(input_kernel, out_shape=(jax.ShapeDtypeStruct((2 * ny, fea...  3.83 us
  transfers between devices with their start and end apart: 11, of which 9 were waited for; matrix products, arithmetic and copies ran while one was open for 1% of the time, Pallas kernels for 8%

profile of v9, /device:TPU:7, one launch (start us, length us, event | category | flops | bytes accessed | tf_op | source)
XLA Modules:
  0.0 120.8 jit_solution(3356123135767106955)
XLA Ops:
  0.6 21.3 %all-gather = bf16[1536,256]{1,0:T(8,128)(2,1)S(1)} all-gather(bf16[96,256]{1,0:T(8,128)(2,1)} %bitcast.27), channel_id=2, replica_groups=mesh['zh'=4,'zl'=2,'xh'=4,'y'=8,'xl'=2,'c'=2] {'y','c'}, dimensions={0}, use_global_device_ids=true | all-gather | bytes 835584 | tf_op jit(solution)/shard_map/all_gather | solution.py:143
  22.0 2.2 %collective-permute-start = (bf16[8,96,256]{2,1,0:T(8,128)(2,1)S(1)}, bf16[8,96,256]{2,1,0:T(8,128)(2,1)S(1)}, u32[]{:S(2)}, u32[]{:S(2)}) collective-permute-start(bf16[8,96,256]{2,1,0:T(8,128)(2,1)S(1)} %dynamic-slice_bitcast_fusion), channel_id=1, source_target_pairs={{0,2},{2,0},{1,3},{3,1},{4,6},{6,4},{5,7},{7,5},{8,10},{10,8},{9,1... | collective-permute-start | bytes 1179656 | tf_op jit(solution)/shard_map/ppermute | solution.py:145
  24.2 4.9 %collective-permute-start.1 = (bf16[4,96,256]{2,1,0:T(8,128)(2,1)S(1)}, bf16[4,96,256]{2,1,0:T(8,128)(2,1)S(1)}, u32[]{:S(2)}, u32[]{:S(2)}) collective-permute-start(bf16[4,96,256]{2,1,0:T(8,128)(2,1)S(1)} %dynamic-slice_bitcast_fusion.2), channel_id=1, source_target_pairs={{0,128},{128,0},{1,129},{129,1},{2,130},{130,2},{3,131},{131,3},{4... | collective-permute-start | bytes 589832 | tf_op jit(solution)/shard_map/ppermute | solution.py:147
  29.2 1.7 %copy-done = bf16[3072,384]{1,0:T(8,128)(2,1)S(1)} copy-done((bf16[3072,384]{1,0:T(8,128)(2,1)S(1)}, bf16[3072,384]{1,0:T(8,128)(2,1)}, u32[]{:S(2)}) %copy-start) | copy-done | bytes 2359320
  30.9 1.2 shard_map.50.pre_ref
  32.0 2.0 %collective-permute-done.1.t1_ref = bf16[4,96,256]{2,1,0:T(8,128)(2,1)S(1)} collective-permute-done((bf16[4,96,256]{2,1,0:T(8,128)(2,1)S(1)}, bf16[4,96,256]{2,1,0:T(8,128)(2,1)S(1)}, u32[]{:S(2)}, u32[]{:S(2)}) %collective-permute-start.1) | collective-permute-done | bytes 196640 | tf_op jit(solution)/shard_map/ppermute | solution.py:147
  34.4 2.9 %collective-permute-start.2 = (bf16[8,96,256]{2,1,0:T(8,128)(2,1)S(1)}, bf16[8,96,256]{2,1,0:T(8,128)(2,1)S(1)}, u32[]{:S(2)}, u32[]{:S(2)}) collective-permute-start(bf16[8,96,256]{2,1,0:T(8,128)(2,1)S(1)} %collective-permute-done.mine_ref), channel_id=1, source_target_pairs={{0,1},{1,0},{2,3},{3,2},{4,5},{5,4},{6,7},{7,6},{8,9},{9,8},{10,11... | collective-permute-start | bytes 1179656 | tf_op jit(solution)/shard_map/ppermute | solution.py:160
  37.3 4.9 %collective-permute-start.3 = (bf16[4,96,256]{2,1,0:T(8,128)(2,1)S(1)}, bf16[4,96,256]{2,1,0:T(8,128)(2,1)S(1)}, u32[]{:S(2)}, u32[]{:S(2)}) collective-permute-start(bf16[4,96,256]{2,1,0:T(8,128)(2,1)S(1)} %dynamic-slice_bitcast_fusion.1), channel_id=1, source_target_pairs={{0,128},{128,0},{1,129},{129,1},{2,130},{130,2},{3,131},{131,3},{4... | collective-permute-start | bytes 589832 | tf_op jit(solution)/shard_map/ppermute | solution.py:161
  42.3 1.4 %shard_map.51 = (bf16[8,2,96,256]{3,2,1,0:T(8,128)(2,1)S(1)}, bf16[256,384]{1,0:T(8,128)(2,1)S(1)}) custom-call(s32[4]{0:T(128)S(1)} %pad_add_fusion.at_ref, bf16[8,96,256]{2,1,0:T(8,128)(2,1)S(1)} %collective-permute-done.mine_ref, bf16[8,96,256]{2,1,0:T(8,128)(2,1)S(1)} %collective-permute-done.2.other_ref, bf16[3072,384]{1,0:T(8,128)(2,1)S(1)} %copy-done.1, ...), custom_call_target="tpu_custom_call" | custom-call | flops 301989888 | bytes 5242880 | tf_op jit(solution)/shard_map/pallas_call | solution.py:162
  43.7 1.9 %collective-permute-start.4 = (bf16[256,384]{1,0:T(8,128)(2,1)S(1)}, bf16[256,384]{1,0:T(8,128)(2,1)S(1)}, u32[]{:S(2)}, u32[]{:S(2)}) collective-permute-start(bf16[256,384]{1,0:T(8,128)(2,1)S(1)} %get-tuple-element.16.pg_ref), channel_id=1, source_target_pairs={{0,128},{128,0},{1,129},{129,1},{2,130},{130,2},{3,131},{131,3},{4... | collective-permute-start | bytes 589832 | tf_op jit(solution)/shard_map/ppermute | solution.py:178
  45.7 1.2 shard_map.53.acc_ref
  47.5 3.8 %shard_map.52 = (f32[16,96,256]{2,1,0:T(8,128)S(1)}, bf16[24,96,256]{2,1,0:T(8,128)(2,1)S(1)}) custom-call(s32[4]{0:T(128)S(1)} %pad_add_fusion.at_ref, bf16[3072,384]{1,0:T(8,128)(2,1)S(1)} %copy-done.1, bf16[256,384]{1,0:T(8,128)(2,1)S(1)} %get-tuple-element.16.pg_ref, bf16[4,96,256]{2,1,0:T(8,128)(2,1)S(1)} %collective-permute-done.1.t1_ref, ...), custom_call_target="tpu_custom_call" | custom-call | flops 603979776 | bytes 5242880 | tf_op jit(solution)/shard_map/pallas_call | solution.py:179
  51.8 3.0 %collective-permute-start.5 = (bf16[24,96,256]{2,1,0:T(8,128)(2,1)S(1)}, bf16[24,96,256]{2,1,0:T(8,128)(2,1)S(1)}, u32[]{:S(2)}, u32[]{:S(2)}) collective-permute-start(bf16[24,96,256]{2,1,0:T(8,128)(2,1)S(1)} %get-tuple-element.21), channel_id=1, source_target_pairs={{0,1},{1,0},{2,3},{3,2},{4,5},{5,4},{6,7},{7,6},{8,9},{9,8},{10,11... | collective-permute-start | bytes 3538952 | tf_op jit(solution)/shard_map/ppermute | solution.py:203
  54.8 2.5 %collective-permute-done.5 = bf16[24,96,256]{2,1,0:T(8,128)(2,1)S(1)} collective-permute-done((bf16[24,96,256]{2,1,0:T(8,128)(2,1)S(1)}, bf16[24,96,256]{2,1,0:T(8,128)(2,1)S(1)}, u32[]{:S(2)}, u32[]{:S(2)}) %collective-permute-start.5) | collective-permute-done | bytes 1179680 | tf_op jit(solution)/shard_map/ppermute | solution.py:203
  57.6 2.2 %collective-permute-start.6 = (bf16[8,96,256]{2,1,0:T(8,128)(2,1)S(1)}, bf16[8,96,256]{2,1,0:T(8,128)(2,1)S(1)}, u32[]{:S(2)}, u32[]{:S(2)}) collective-permute-start(bf16[8,96,256]{2,1,0:T(8,128)(2,1)S(1)} %slice.65), channel_id=1, source_target_pairs={{0,2},{2,0},{1,3},{3,1},{4,6},{6,4},{5,7},{7,5},{8,10},{10,8},{9,1... | collective-permute-start | bytes 1179656 | tf_op jit(solution)/shard_map/ppermute | solution.py:112
  59.8 2.2 %shard_map.55 = bf16[16,96,384]{2,1,0:T(8,128)(2,1)} custom-call(s32[4]{0:T(128)S(1)} %pad_add_fusion.at_ref, f32[16,96,384]{2,1,0:T(8,128)S(1)} %shard_map.53.acc_ref, bf16[4,96,256]{2,1,0:T(8,128)(2,1)S(1)} %collective-permute-done.1.t1_ref, bf16[4,96,256]{2,1,0:T(8,128)(2,1)S(1)} %collective-permute-done.3.t2_ref, ...), custom_call_target="tpu_custom_call" | custom-call | flops 301989888 | bytes 4194304 | tf_op jit(solution)/shard_map/pallas_call | solution.py:206
  62.1 19.7 %all-to-all-start = ((bf16[16,96,384]{2,1,0:T(8,128)(2,1)}), bf16[16,96,384]{2,1,0:T(8,128)(2,1)S(1)}, u32[]{:S(2)}, u32[]{:S(2)}) async-start(bf16[16,96,384]{2,1,0:T(8,128)(2,1)} %shard_map.55), calls=%async_computation | async-start | bytes 2359296 | tf_op jit(solution)/shard_map/all_to_all | solution.py:217
  81.9 1.9 %collective-permute-start.7 = (bf16[4,96,256]{2,1,0:T(8,128)(2,1)S(1)}, bf16[4,96,256]{2,1,0:T(8,128)(2,1)S(1)}, u32[]{:S(2)}, u32[]{:S(2)}) collective-permute-start(bf16[4,96,256]{2,1,0:T(8,128)(2,1)S(1)} %slice.66), channel_id=1, source_target_pairs={{0,4},{4,0},{8,12},{12,8},{16,20},{20,16},{24,28},{28,24},{1,5},{5... | collective-permute-start | bytes 589832 | tf_op jit(solution)/shard_map/ppermute | solution.py:127
  83.8 5.1 %collective-permute-done.7 = bf16[4,96,256]{2,1,0:T(8,128)(2,1)S(1)} collective-permute-done((bf16[4,96,256]{2,1,0:T(8,128)(2,1)S(1)}, bf16[4,96,256]{2,1,0:T(8,128)(2,1)S(1)}, u32[]{:S(2)}, u32[]{:S(2)}) %collective-permute-start.7) | collective-permute-done | bytes 196640 | tf_op jit(solution)/shard_map/ppermute | solution.py:127
  89.1 1.9 %collective-permute-start.8 = (bf16[2,96,256]{2,1,0:T(8,128)(2,1)S(1)}, bf16[2,96,256]{2,1,0:T(8,128)(2,1)S(1)}, u32[]{:S(2)}, u32[]{:S(2)}) collective-permute-start(bf16[2,96,256]{2,1,0:T(8,128)(2,1)S(1)} %slice.67), channel_id=1, source_target_pairs={{0,8},{4,12},{8,0},{12,4},{16,24},{20,28},{24,16},{28,20},{1,9},{5... | collective-permute-start | bytes 294920 | tf_op jit(solution)/shard_map/ppermute | solution.py:127
  91.0 5.7 %collective-permute-done.8 = bf16[2,96,256]{2,1,0:T(8,128)(2,1)S(1)} collective-permute-done((bf16[2,96,256]{2,1,0:T(8,128)(2,1)S(1)}, bf16[2,96,256]{2,1,0:T(8,128)(2,1)S(1)}, u32[]{:S(2)}, u32[]{:S(2)}) %collective-permute-start.8) | collective-permute-done | bytes 98336 | tf_op jit(solution)/shard_map/ppermute | solution.py:127
  96.7 4.4 %collective-permute-start.9 = (bf16[1,96,256]{2,1,0:T(8,128)(2,1)S(1)}, bf16[1,96,256]{2,1,0:T(8,128)(2,1)S(1)}, u32[]{:S(2)}, u32[]{:S(2)}) collective-permute-start(bf16[1,96,256]{2,1,0:T(8,128)(2,1)S(1)} %slice.68), channel_id=1, source_target_pairs={{0,16},{4,20},{8,24},{12,28},{16,0},{20,4},{24,8},{28,12},{1,17},{... | collective-permute-start | bytes 147464 | tf_op jit(solution)/shard_map/ppermute | solution.py:127
  101.2 4.6 %collective-permute-done.9 = bf16[1,96,256]{2,1,0:T(8,128)(2,1)S(1)} collective-permute-done((bf16[1,96,256]{2,1,0:T(8,128)(2,1)S(1)}, bf16[1,96,256]{2,1,0:T(8,128)(2,1)S(1)}, u32[]{:S(2)}, u32[]{:S(2)}) %collective-permute-start.9) | collective-permute-done | bytes 49184 | tf_op jit(solution)/shard_map/ppermute | solution.py:127
  106.4 13.7 %all-to-all-done = bf16[16,96,384]{2,1,0:T(8,128)(2,1)S(1)} async-done(((bf16[16,96,384]{2,1,0:T(8,128)(2,1)}), bf16[16,96,384]{2,1,0:T(8,128)(2,1)S(1)}, u32[]{:S(2)}, u32[]{:S(2)}) %all-to-all-start) | async-done | bytes 1179680 | tf_op jit(solution)/shard_map/all_to_all | solution.py:217
  (26 shorter events, 3.7 us)
Async XLA Ops:
  22.0 12.5 %collective-permute-start = (bf16[8,96,256]{2,1,0:T(8,128)(2,1)S(1)}, bf16[8,96,256]{2,1,0:T(8,128)(2,1)S(1)}, u32[]{:S(2)}, u32[]{:S(2)}) collective-permute-start(bf16[8,96,256]{2,1,0:T(8,128)(2,1)S(1)} %dynamic-slice_bitcast_fusion), channel_id=1, source_target_pairs={{0,2},{2,0},{1,3},{3,1},{4,6},{6,4},{5,7},{7,5},{8,10},{10,8},{9,1... | collective-permute-start | bytes 1179656 | tf_op jit(solution)/shard_map/ppermute | solution.py:145
  24.2 9.8 %collective-permute-start.1 = (bf16[4,96,256]{2,1,0:T(8,128)(2,1)S(1)}, bf16[4,96,256]{2,1,0:T(8,128)(2,1)S(1)}, u32[]{:S(2)}, u32[]{:S(2)}) collective-permute-start(bf16[4,96,256]{2,1,0:T(8,128)(2,1)S(1)} %dynamic-slice_bitcast_fusion.2), channel_id=1, source_target_pairs={{0,128},{128,0},{1,129},{129,1},{2,130},{130,2},{3,131},{131,3},{4... | collective-permute-start | bytes 589832 | tf_op jit(solution)/shard_map/ppermute | solution.py:147
  29.2 1.7 %copy-start = (bf16[3072,384]{1,0:T(8,128)(2,1)S(1)}, bf16[3072,384]{1,0:T(8,128)(2,1)}, u32[]{:S(2)}) copy-start(bf16[3072,384]{1,0:T(8,128)(2,1)} %w_ref.5) | copy-start | bytes 7077892
  30.9 11.4 %copy-start.1 = (bf16[3072,384]{1,0:T(8,128)(2,1)S(1)}, bf16[3072,384]{1,0:T(8,128)(2,1)}, u32[]{:S(2)}) copy-start(bf16[3072,384]{1,0:T(8,128)(2,1)} %w_ref.5) | copy-start | bytes 7077892
  30.9 11.4 %copy-start.2 = (bf16[256,384]{1,0:T(8,128)(2,1)S(1)}, bf16[256,384]{1,0:T(8,128)(2,1)}, u32[]{:S(2)}) copy-start(bf16[256,384]{1,0:T(8,128)(2,1)} %g_ref.1) | copy-start | bytes 589828
  34.4 7.8 %collective-permute-start.2 = (bf16[8,96,256]{2,1,0:T(8,128)(2,1)S(1)}, bf16[8,96,256]{2,1,0:T(8,128)(2,1)S(1)}, u32[]{:S(2)}, u32[]{:S(2)}) collective-permute-start(bf16[8,96,256]{2,1,0:T(8,128)(2,1)S(1)} %collective-permute-done.mine_ref), channel_id=1, source_target_pairs={{0,1},{1,0},{2,3},{3,2},{4,5},{5,4},{6,7},{7,6},{8,9},{9,8},{10,11... | collective-permute-start | bytes 1179656 | tf_op jit(solution)/shard_map/ppermute | solution.py:160
  37.3 10.2 %collective-permute-start.3 = (bf16[4,96,256]{2,1,0:T(8,128)(2,1)S(1)}, bf16[4,96,256]{2,1,0:T(8,128)(2,1)S(1)}, u32[]{:S(2)}, u32[]{:S(2)}) collective-permute-start(bf16[4,96,256]{2,1,0:T(8,128)(2,1)S(1)} %dynamic-slice_bitcast_fusion.1), channel_id=1, source_target_pairs={{0,128},{128,0},{1,129},{129,1},{2,130},{130,2},{3,131},{131,3},{4... | collective-permute-start | bytes 589832 | tf_op jit(solution)/shard_map/ppermute | solution.py:161
  43.7 8.1 %collective-permute-start.4 = (bf16[256,384]{1,0:T(8,128)(2,1)S(1)}, bf16[256,384]{1,0:T(8,128)(2,1)S(1)}, u32[]{:S(2)}, u32[]{:S(2)}) collective-permute-start(bf16[256,384]{1,0:T(8,128)(2,1)S(1)} %get-tuple-element.16.pg_ref), channel_id=1, source_target_pairs={{0,128},{128,0},{1,129},{129,1},{2,130},{130,2},{3,131},{131,3},{4... | collective-permute-start | bytes 589832 | tf_op jit(solution)/shard_map/ppermute | solution.py:178
  51.8 5.5 %collective-permute-start.5 = (bf16[24,96,256]{2,1,0:T(8,128)(2,1)S(1)}, bf16[24,96,256]{2,1,0:T(8,128)(2,1)S(1)}, u32[]{:S(2)}, u32[]{:S(2)}) collective-permute-start(bf16[24,96,256]{2,1,0:T(8,128)(2,1)S(1)} %get-tuple-element.21), channel_id=1, source_target_pairs={{0,1},{1,0},{2,3},{3,2},{4,5},{5,4},{6,7},{7,6},{8,9},{9,8},{10,11... | collective-permute-start | bytes 3538952 | tf_op jit(solution)/shard_map/ppermute | solution.py:203
  57.6 24.2 %collective-permute-start.6 = (bf16[8,96,256]{2,1,0:T(8,128)(2,1)S(1)}, bf16[8,96,256]{2,1,0:T(8,128)(2,1)S(1)}, u32[]{:S(2)}, u32[]{:S(2)}) collective-permute-start(bf16[8,96,256]{2,1,0:T(8,128)(2,1)S(1)} %slice.65), channel_id=1, source_target_pairs={{0,2},{2,0},{1,3},{3,1},{4,6},{6,4},{5,7},{7,5},{8,10},{10,8},{9,1... | collective-permute-start | bytes 1179656 | tf_op jit(solution)/shard_map/ppermute | solution.py:112
  62.1 58.0 %all-to-all-start = ((bf16[16,96,384]{2,1,0:T(8,128)(2,1)}), bf16[16,96,384]{2,1,0:T(8,128)(2,1)S(1)}, u32[]{:S(2)}, u32[]{:S(2)}) async-start(bf16[16,96,384]{2,1,0:T(8,128)(2,1)} %shard_map.55), calls=%async_computation | async-start | bytes 2359296 | tf_op jit(solution)/shard_map/all_to_all | solution.py:217
  81.9 7.1 %collective-permute-start.7 = (bf16[4,96,256]{2,1,0:T(8,128)(2,1)S(1)}, bf16[4,96,256]{2,1,0:T(8,128)(2,1)S(1)}, u32[]{:S(2)}, u32[]{:S(2)}) collective-permute-start(bf16[4,96,256]{2,1,0:T(8,128)(2,1)S(1)} %slice.66), channel_id=1, source_target_pairs={{0,4},{4,0},{8,12},{12,8},{16,20},{20,16},{24,28},{28,24},{1,5},{5... | collective-permute-start | bytes 589832 | tf_op jit(solution)/shard_map/ppermute | solution.py:127
  89.1 7.6 %collective-permute-start.8 = (bf16[2,96,256]{2,1,0:T(8,128)(2,1)S(1)}, bf16[2,96,256]{2,1,0:T(8,128)(2,1)S(1)}, u32[]{:S(2)}, u32[]{:S(2)}) collective-permute-start(bf16[2,96,256]{2,1,0:T(8,128)(2,1)S(1)} %slice.67), channel_id=1, source_target_pairs={{0,8},{4,12},{8,0},{12,4},{16,24},{20,28},{24,16},{28,20},{1,9},{5... | collective-permute-start | bytes 294920 | tf_op jit(solution)/shard_map/ppermute | solution.py:127
  96.7 9.0 %collective-permute-start.9 = (bf16[1,96,256]{2,1,0:T(8,128)(2,1)S(1)}, bf16[1,96,256]{2,1,0:T(8,128)(2,1)S(1)}, u32[]{:S(2)}, u32[]{:S(2)}) collective-permute-start(bf16[1,96,256]{2,1,0:T(8,128)(2,1)S(1)} %slice.68), channel_id=1, source_target_pairs={{0,16},{4,20},{8,24},{12,28},{16,0},{20,4},{24,8},{28,12},{1,17},{... | collective-permute-start | bytes 147464 | tf_op jit(solution)/shard_map/ppermute | solution.py:127
